TPU v7x, 32 devices: a whole 2x2x4 slice. The times are simulated.
32 devices in a mesh: boxes: 8 (over y, x, core), grp: 4 (over z).
Axes of the slice: x: 2, y: 2, z: 4, core: 2. Of those that a mesh axis runs over, the one named last changes fastest.
Arguments:
- sources: float32 [22, 256, 1024], P(None, 'boxes', 'grp'), may hold values from -24 to 24
- absorption: float32 [256, 1024], P('boxes', 'grp'), may hold values from 0.5 to 5
- conductance: float32 [256, 1024], P('boxes', 'grp'), may hold values from 0.1 to 1
- diffusivity: float32 [22], replicated, may hold values from 0.3 to 3
- run_lengths: int32 [8], replicated, may hold values from 1 to 3, as said below
Outputs:
- correction: float32 [22, 384, 1024], P(None, 'boxes', 'grp')
Inputs may be any that keep to these rules, and one draw needn't show every extreme that they name: `run_lengths`: the lengths add up to 16, and first[b] lies between b * 2 and b * 2 + 1 for every b.
All inputs are finite; a program needn't handle non-finite values.
Results may differ from a plain program's by a relative error of at most 0.00002.
Values sent between devices are 32-bit elements; how exact they have to be, the bound alone decides.
No kernel may reach another device: no remote copies, remote signals or barrier semaphores. Data moves between devices by JAX's collectives and lax.ppermute only.
A program may use at most 64 MiB of HBM per device.

v0:
```python
import jax
import jax.numpy as jnp
from jax import lax
from jax.sharding import PartitionSpec as P

BOX_X = 16
PLANE_Y = 16
PLANE_Z = 16
OLD_DEV = 2
MOST = 3
SWEEPS = 4


def with_halo(shard, sides, width):
    for axis, dim in sides:
        peers, length = (lax.axis_size(axis), shard.shape[dim])
        up = [(i, (i + 1) % peers) for i in range(peers - 1)]
        down = [(j, i) for i, j in up]
        last = lax.slice_in_dim(shard, length - width, length, axis=dim)
        initial = lax.slice_in_dim(shard, 0, width, axis=dim)
        before = lax.ppermute(last, axis, up)
        after = lax.ppermute(initial, axis, down)
        shard = jnp.concatenate([before, shard, after], axis=dim)
    return shard


def passed_along(value, axis, steps):
    count = lax.axis_size(axis)
    initial, last = (max(0, -steps), min(count, count - steps))
    return lax.ppermute(value, axis, [(source, source + steps) for source in range(initial, last)])


def checker(row_count, plane_y, plane_z):
    x_index = lax.broadcasted_iota(jnp.int32, (row_count, plane_y * plane_z), 0)
    flat_index = lax.broadcasted_iota(jnp.int32, (row_count, plane_y * plane_z), 1)
    return (x_index + flat_index // plane_z + flat_index % plane_z) % 2


def exchange_faces(solution, conduct, live_rows, plane_z):
    first_plane = jnp.concatenate([solution[:, 0], conduct[:, 0]], 0)
    last_plane = jnp.concatenate(
        [
            lax.dynamic_index_in_dim(solution, live_rows - 1, 1, keepdims=False),
            lax.dynamic_index_in_dim(conduct, live_rows - 1, 1, keepdims=False),
        ],
        0,
    )
    extended = with_halo(jnp.stack([first_plane, last_plane], 1), (("boxes", 1),), 1)
    layers, row_count, plane_cells = (first_plane.shape[0], solution.shape[1], solution.shape[2])
    low_rim = jnp.concatenate([solution[:, :, :plane_z], conduct[:, :, :plane_z]], 0).reshape(
        layers, row_count * plane_z
    )
    high_rim = jnp.concatenate(
        [solution[:, :, plane_cells - plane_z :], conduct[:, :, plane_cells - plane_z :]], 0
    ).reshape(layers, row_count * plane_z)
    rimmed = with_halo(jnp.stack([low_rim, high_rim], 1), (("grp", 1),), 1)
    return (extended, rimmed)


def neighbours_of(field, below_plane, above_plane, low_row, high_row, live_rows, plane_z):
    layers, row_count, plane_cells = field.shape
    below_plane = below_plane.reshape(layers, 1, plane_cells)
    above_plane = above_plane.reshape(layers, 1, plane_cells)
    x_lower = jnp.concatenate([below_plane, field[:, :-1]], 1)
    x_next = jnp.concatenate([field[:, 1:], jnp.zeros_like(below_plane)], 1)
    at_end = lax.broadcasted_iota(jnp.int32, (row_count, 1), 0) == live_rows - 1
    x_upper = jnp.where(at_end, above_plane, x_next)
    y_lower = jnp.concatenate(
        [low_row.reshape(layers, row_count, plane_z), field[:, :, : plane_cells - plane_z]], 2
    )
    y_upper = jnp.concatenate(
        [field[:, :, plane_z:], high_row.reshape(layers, row_count, plane_z)], 2
    )
    z_place = lax.broadcasted_iota(jnp.int32, (1, 1, plane_cells), 2) % plane_z
    z_lower = jnp.where(z_place == 0, jnp.roll(field, -(plane_z - 1), 2), jnp.roll(field, 1, 2))
    z_upper = jnp.where(
        z_place == plane_z - 1, jnp.roll(field, plane_z - 1, 2), jnp.roll(field, -1, 2)
    )
    return [x_lower, x_upper, y_lower, y_upper, z_lower, z_upper]


def smooth_boxes(source, absorb, conduct, factor, live_rows):
    channels, row_count, plane_cells = source.shape
    parity = checker(row_count, PLANE_Y, PLANE_Z)
    active = lax.broadcasted_iota(jnp.int32, (row_count, 1), 0) < live_rows
    conduct = conduct[None]
    solution = jnp.zeros_like(source)
    for half_sweep in range(SWEEPS):
        extended, rimmed = exchange_faces(solution, conduct, live_rows, PLANE_Z)
        field_sides = neighbours_of(
            solution,
            extended[:channels, 0],
            extended[:channels, 3],
            rimmed[:channels, 0],
            rimmed[:channels, 3],
            live_rows,
            PLANE_Z,
        )
        conduct_sides = neighbours_of(
            conduct,
            extended[channels:, 0],
            extended[channels:, 3],
            rimmed[channels:, 0],
            rimmed[channels:, 3],
            live_rows,
            PLANE_Z,
        )
        weights = jnp.zeros_like(conduct)
        inflow = jnp.zeros_like(source)
        for beside, beside_conduct in zip(field_sides, conduct_sides):
            facing = 0.5 * (conduct + beside_conduct)
            weights = weights + facing
            inflow = inflow + facing * beside
        divisor = jnp.where(active, absorb[None] + factor * weights, 1.0)
        update = (source + factor * inflow) / divisor
        solution = jnp.where(active & (parity == half_sweep % 2), update, solution)
    return solution


def place_rows(own_rows, arrived_rows, pick_rows, keep_rows):
    joined = jnp.concatenate([own_rows, arrived_rows], 1)
    taken = jnp.take(joined, pick_rows, axis=1)
    return jnp.where(keep_rows.reshape(1, -1, 1), taken, jnp.zeros_like(taken))


def on_device(sources, absorption, conductance, diffusivity, run_lengths):
    channels, old_rows, plane_cells = sources.shape
    row_count = MOST * BOX_X
    position = lax.axis_index("boxes")
    device_order = lax.broadcasted_iota(jnp.int32, run_lengths.shape, 0)
    box_count = jnp.sum(jnp.where(device_order == position, run_lengths, 0))
    first_box = jnp.sum(jnp.where(device_order < position, run_lengths, 0))
    row_index = lax.broadcasted_iota(jnp.int32, (row_count,), 0)
    live_rows = box_count * BOX_X
    start_row = (first_box - position * OLD_DEV) * BOX_X
    pick_rows = jnp.clip(start_row + row_index, 0, 2 * old_rows - 1)
    keep_rows = row_index < live_rows
    factor = diffusivity.reshape(channels, 1, 1)
    bundle = jnp.concatenate([sources, absorption[None], conductance[None]], 0)
    arrived = passed_along(bundle, "boxes", -1)
    moved = place_rows(bundle, arrived, pick_rows, keep_rows)
    return smooth_boxes(moved[:channels], moved[channels], moved[channels + 1], factor, live_rows)


def solution(mesh):
    return jax.shard_map(
        on_device,
        mesh=mesh,
        in_specs=(P(None, "boxes", "grp"), P("boxes", "grp"), P("boxes", "grp"), P(), P()),
        out_specs=P(None, "boxes", "grp"),
        check_vma=False,
    )
```

profile of v0, /device:TPU:12, one launch (start us, length us, event | category | flops | bytes accessed | tf_op | source)
XLA Modules:
  0.0 179.3 jit_solution(12812707412407117102)
XLA Ops:
  3.2 2.8 %collective-permute-start = (f32[24,32,256]{2,0,1:T(8,128)S(1)}, f32[24,32,256]{2,0,1:T(8,128)S(1)}, u32[]{:S(2)}, u32[]{:S(2)}) collective-permute-start(f32[24,32,256]{2,0,1:T(8,128)S(1)} %pad_maximum_fusion.7), channel_id=1, source_target_pairs={{4,0},{8,4},{12,8},{16,12},{20,16},{24,20},{28,24},{5,1},{9,5},{13... | collective-permute-start | bytes 2359304 | tf_op jit(solution)/shard_map/ppermute | solution.py:30
  12.1 3.4 %collective-permute-done = f32[24,32,256]{2,0,1:T(8,128)S(1)} collective-permute-done((f32[24,32,256]{2,0,1:T(8,128)S(1)}, f32[24,32,256]{2,0,1:T(8,128)S(1)}, u32[]{:S(2)}, u32[]{:S(2)}) %collective-permute-start) | collective-permute-done | bytes 786464 | tf_op jit(solution)/shard_map/ppermute | solution.py:30
  19.9 4.7 %collective-permute-start.2 = (f32[23,1,256]{2,0,1:T(8,128)S(1)}, f32[23,1,256]{2,0,1:T(8,128)S(1)}, u32[]{:S(2)}, u32[]{:S(2)}) collective-permute-start(f32[23,1,256]{2,0,1:T(8,128)S(1)} %pad_bitcast_fusion), channel_id=1, source_target_pairs={{4,0},{8,4},{12,8},{16,12},{20,16},{24,20},{28,24},{5,1},{9,5},{13... | collective-permute-start | bytes 70664 | tf_op jit(solution)/shard_map/ppermute | solution.py:22
  24.7 1.9 %collective-permute-start.1 = (f32[23,1,256]{2,0,1:T(8,128)S(1)}, f32[23,1,256]{2,0,1:T(8,128)S(1)}, u32[]{:S(2)}, u32[]{:S(2)}) collective-permute-start(f32[23,1,256]{2,0,1:T(8,128)S(1)} %pad_bitcast_fusion.1), channel_id=1, source_target_pairs={{0,4},{4,8},{8,12},{12,16},{16,20},{20,24},{24,28},{1,5},{5,9},{9,... | collective-permute-start | bytes 70664 | tf_op jit(solution)/shard_map/ppermute | solution.py:21
  26.9 2.4 %collective-permute-start.4 = (f32[23,1,768]{2,0,1:T(8,128)S(1)}, f32[23,1,768]{2,0,1:T(8,128)S(1)}, u32[]{:S(2)}, u32[]{:S(2)}) collective-permute-start(f32[23,1,768]{2,0,1:T(8,128)S(1)} %stack_reshape.25), channel_id=1, source_target_pairs={{1,0},{2,1},{3,2},{5,4},{6,5},{7,6},{9,8},{10,9},{11,10},{13,12},{... | collective-permute-start | bytes 211976 | tf_op jit(solution)/shard_map/ppermute | solution.py:22
  29.6 3.5 %collective-permute-start.3 = (f32[23,1,768]{2,0,1:T(8,128)S(1)}, f32[23,1,768]{2,0,1:T(8,128)S(1)}, u32[]{:S(2)}, u32[]{:S(2)}) collective-permute-start(f32[23,1,768]{2,0,1:T(8,128)S(1)} %stack_reshape.24), channel_id=1, source_target_pairs={{0,1},{1,2},{2,3},{4,5},{5,6},{6,7},{8,9},{9,10},{10,11},{12,13},{... | collective-permute-start | bytes 211976 | tf_op jit(solution)/shard_map/ppermute | solution.py:21
  33.7 2.2 %collective-permute-done.3 = f32[23,1,768]{2,0,1:T(8,128)S(1)} collective-permute-done((f32[23,1,768]{2,0,1:T(8,128)S(1)}, f32[23,1,768]{2,0,1:T(8,128)S(1)}, u32[]{:S(2)}, u32[]{:S(2)}) %collective-permute-start.3) | collective-permute-done | bytes 70688 | tf_op jit(solution)/shard_map/ppermute | solution.py:21
  43.9 1.8 fusion.107
  47.5 1.8 %fusion.106 = (f32[22,48,241]{2,0,1:T(8,128)}, f32[22,48,241]{2,0,1:T(8,128)}) fusion(f32[22,48,256]{2,0,1:T(8,128)S(1)} %divide_select_fusion), kind=kLoop, calls=%fused_computation.208 | loop fusion | bytes 4071936 | tf_op jit(solution)/shard_map/jit(_roll_static)/slice | solution.py:77
  50.5 1.9 %collective-permute-start.5 = (f32[23,1,256]{2,0,1:T(8,128)}, f32[23,1,256]{2,0,1:T(8,128)}, u32[]{:S(2)}, u32[]{:S(2)}) collective-permute-start(f32[23,1,256]{2,0,1:T(8,128)} %fusion.61), channel_id=1, source_target_pairs={{0,4},{4,8},{8,12},{12,16},{16,20},{20,24},{24,28},{1,5},{5,9},{9,... | collective-permute-start | bytes 70664 | tf_op jit(solution)/shard_map/ppermute | solution.py:21
  52.4 4.5 %collective-permute-start.6 = (f32[23,1,256]{2,0,1:T(8,128)}, f32[23,1,256]{2,0,1:T(8,128)}, u32[]{:S(2)}, u32[]{:S(2)}) collective-permute-start(f32[23,1,256]{2,0,1:T(8,128)} %fusion.58), channel_id=1, source_target_pairs={{4,0},{8,4},{12,8},{16,12},{20,16},{24,20},{28,24},{5,1},{9,5},{13... | collective-permute-start | bytes 70664 | tf_op jit(solution)/shard_map/ppermute | solution.py:22
  58.1 1.9 %collective-permute-start.8 = (f32[23,1,768]{2,0,1:T(8,128)}, f32[23,1,768]{2,0,1:T(8,128)S(1)}, u32[]{:S(2)}, u32[]{:S(2)}) collective-permute-start(f32[23,1,768]{2,0,1:T(8,128)} %stack_reshape.27), channel_id=1, source_target_pairs={{1,0},{2,1},{3,2},{5,4},{6,5},{7,6},{9,8},{10,9},{11,10},{13,12},{... | collective-permute-start | bytes 211976 | tf_op jit(solution)/shard_map/ppermute | solution.py:22
  60.5 4.1 %collective-permute-start.7 = (f32[23,1,768]{2,0,1:T(8,128)S(1)}, f32[23,1,768]{2,0,1:T(8,128)S(1)}, u32[]{:S(2)}, u32[]{:S(2)}) collective-permute-start(f32[23,1,768]{2,0,1:T(8,128)S(1)} %stack_reshape.26), channel_id=1, source_target_pairs={{0,1},{1,2},{2,3},{4,5},{5,6},{6,7},{8,9},{9,10},{10,11},{12,13},{... | collective-permute-start | bytes 211976 | tf_op jit(solution)/shard_map/ppermute | solution.py:21
  73.5 6.0 %fusion.8 = f32[22,48,256]{2,0,1:T(8,128)S(1)} fusion(f32[22,48,256]{2,0,1:T(8,128)S(1)} %divide_select_fusion, f32[22,47,256]{2,0,1:T(8,128)} %get-tuple-element.64, f32[22,1,256]{2,0,1:T(8,128)} %bitcast.146, f32[22,48,240]{2,0,1:T(8,128)} %get-tuple-element.74, f32[22,48,16]{2,0,1:T(8,128)S(1)} %copy.85, f32[22,48,16]{2,0,1:T(8,128)} %copy.88, ...), kind=kLoop, calls=%fused_computation.11 | loop fusion | flops 7569408 | bytes 12300984 | tf_op jit(solution)/shard_map/jit(_where)/select_n | solution.py:116
  87.4 1.8 %fusion.99 = (f32[22,48,241]{2,0,1:T(8,128)}, f32[22,48,241]{2,0,1:T(8,128)}) fusion(f32[22,48,256]{2,0,1:T(8,128)S(1)} %fusion.8), kind=kLoop, calls=%fused_computation.201 | loop fusion | bytes 4071936 | tf_op jit(solution)/shard_map/jit(_roll_static)/slice | solution.py:77
  90.4 1.9 %collective-permute-start.9 = (f32[23,1,256]{2,0,1:T(8,128)}, f32[23,1,256]{2,0,1:T(8,128)}, u32[]{:S(2)}, u32[]{:S(2)}) collective-permute-start(f32[23,1,256]{2,0,1:T(8,128)} %fusion.62), channel_id=1, source_target_pairs={{0,4},{4,8},{8,12},{12,16},{16,20},{20,24},{24,28},{1,5},{5,9},{9,... | collective-permute-start | bytes 70664 | tf_op jit(solution)/shard_map/ppermute | solution.py:21
  92.4 4.5 %collective-permute-start.10 = (f32[23,1,256]{2,0,1:T(8,128)}, f32[23,1,256]{2,0,1:T(8,128)}, u32[]{:S(2)}, u32[]{:S(2)}) collective-permute-start(f32[23,1,256]{2,0,1:T(8,128)} %fusion.59), channel_id=1, source_target_pairs={{4,0},{8,4},{12,8},{16,12},{20,16},{24,20},{28,24},{5,1},{9,5},{13... | collective-permute-start | bytes 70664 | tf_op jit(solution)/shard_map/ppermute | solution.py:22
  98.0 1.9 %collective-permute-start.12 = (f32[23,1,768]{2,0,1:T(8,128)}, f32[23,1,768]{2,0,1:T(8,128)S(1)}, u32[]{:S(2)}, u32[]{:S(2)}) collective-permute-start(f32[23,1,768]{2,0,1:T(8,128)} %stack_reshape.29), channel_id=1, source_target_pairs={{1,0},{2,1},{3,2},{5,4},{6,5},{7,6},{9,8},{10,9},{11,10},{13,12},{... | collective-permute-start | bytes 211976 | tf_op jit(solution)/shard_map/ppermute | solution.py:22
  100.5 3.9 %collective-permute-start.11 = (f32[23,1,768]{2,0,1:T(8,128)S(1)}, f32[23,1,768]{2,0,1:T(8,128)S(1)}, u32[]{:S(2)}, u32[]{:S(2)}) collective-permute-start(f32[23,1,768]{2,0,1:T(8,128)S(1)} %stack_reshape.28), channel_id=1, source_target_pairs={{0,1},{1,2},{2,3},{4,5},{5,6},{6,7},{8,9},{9,10},{10,11},{12,13},{... | collective-permute-start | bytes 211976 | tf_op jit(solution)/shard_map/ppermute | solution.py:21
  114.7 6.0 %fusion.19 = f32[22,48,256]{2,0,1:T(8,128)S(1)} fusion(f32[22,48,256]{2,0,1:T(8,128)S(1)} %fusion.8, f32[22,47,256]{2,0,1:T(8,128)} %get-tuple-element.48, f32[22,1,256]{2,0,1:T(8,128)} %bitcast.149, f32[22,48,240]{2,0,1:T(8,128)} %get-tuple-element.58, f32[22,48,16]{2,0,1:T(8,128)S(1)} %copy.91, f32[22,48,16]{2,0,1:T(8,128)} %copy.94, ...), kind=kLoop, calls=%fused_computation.27 | loop fusion | flops 7569408 | bytes 12300984 | tf_op jit(solution)/shard_map/jit(_where)/select_n | solution.py:116
  127.2 1.8 %fusion.89 = (f32[22,48,255]{2,0,1:T(8,128)}, f32[22,48,255]{2,0,1:T(8,128)}) fusion(f32[22,48,256]{2,0,1:T(8,128)S(1)} %fusion.19), kind=kLoop, calls=%fused_computation.191 | loop fusion | bytes 4308480 | tf_op jit(solution)/shard_map/jit(_roll_static)/slice | solution.py:77
  129.0 1.8 %fusion.92 = (f32[22,48,241]{2,0,1:T(8,128)}, f32[22,48,241]{2,0,1:T(8,128)}) fusion(f32[22,48,256]{2,0,1:T(8,128)S(1)} %fusion.19), kind=kLoop, calls=%fused_computation.194 | loop fusion | bytes 4071936 | tf_op jit(solution)/shard_map/jit(_roll_static)/slice | solution.py:77
  132.0 1.9 %collective-permute-start.13 = (f32[23,1,256]{2,0,1:T(8,128)}, f32[23,1,256]{2,0,1:T(8,128)}, u32[]{:S(2)}, u32[]{:S(2)}) collective-permute-start(f32[23,1,256]{2,0,1:T(8,128)} %fusion.63), channel_id=1, source_target_pairs={{0,4},{4,8},{8,12},{12,16},{16,20},{20,24},{24,28},{1,5},{5,9},{9,... | collective-permute-start | bytes 70664 | tf_op jit(solution)/shard_map/ppermute | solution.py:21
  133.9 4.5 %collective-permute-start.14 = (f32[23,1,256]{2,0,1:T(8,128)}, f32[23,1,256]{2,0,1:T(8,128)}, u32[]{:S(2)}, u32[]{:S(2)}) collective-permute-start(f32[23,1,256]{2,0,1:T(8,128)} %fusion.60), channel_id=1, source_target_pairs={{4,0},{8,4},{12,8},{16,12},{20,16},{24,20},{28,24},{5,1},{9,5},{13... | collective-permute-start | bytes 70664 | tf_op jit(solution)/shard_map/ppermute | solution.py:22
  139.5 1.9 %stack_reshape.31 = f32[23,1,768]{2,0,1:T(8,128)} reshape(f32[23,48,16]{2,1,0:T(8,128)} %copy.98) | data formatting | bytes 141312 | tf_op jit(solution)/shard_map/stack;reshape | solution.py:56
  141.4 1.9 %collective-permute-start.16 = (f32[23,1,768]{2,0,1:T(8,128)}, f32[23,1,768]{2,0,1:T(8,128)}, u32[]{:S(2)}, u32[]{:S(2)}) collective-permute-start(f32[23,1,768]{2,0,1:T(8,128)} %stack_reshape.31), channel_id=1, source_target_pairs={{1,0},{2,1},{3,2},{5,4},{6,5},{7,6},{9,8},{10,9},{11,10},{13,12},{... | collective-permute-start | bytes 211976 | tf_op jit(solution)/shard_map/ppermute | solution.py:22
  145.4 1.9 %stack_reshape.30 = f32[23,1,768]{2,0,1:T(8,128)} reshape(f32[23,48,16]{2,1,0:T(8,128)} %copy.95) | data formatting | bytes 141312 | tf_op jit(solution)/shard_map/stack;reshape | solution.py:56
  147.3 4.1 %collective-permute-start.15 = (f32[23,1,768]{2,0,1:T(8,128)}, f32[23,1,768]{2,0,1:T(8,128)}, u32[]{:S(2)}, u32[]{:S(2)}) collective-permute-start(f32[23,1,768]{2,0,1:T(8,128)} %stack_reshape.30), channel_id=1, source_target_pairs={{0,1},{1,2},{2,3},{4,5},{5,6},{6,7},{8,9},{9,10},{10,11},{12,13},{... | collective-permute-start | bytes 211976 | tf_op jit(solution)/shard_map/ppermute | solution.py:21
  158.1 1.9 %reshape_squeeze.63 = f32[22,48,16]{2,1,0:T(8,128)} reshape(f32[22,1,768]{2,0,1:T(8,128)} %bitcast.154) | data formatting | bytes 135168 | tf_op jit(solution)/shard_map/reshape;squeeze | solution.py:72
  160.0 2.0 %copy.100 = f32[22,48,16]{2,0,1:T(8,128)} copy(f32[22,48,16]{2,1,0:T(8,128)} %reshape_squeeze.63) | data formatting | bytes 135168 | tf_op jit(solution)/shard_map/reshape;squeeze | solution.py:72
  169.2 1.9 %reshape_squeeze.61 = f32[22,48,16]{2,1,0:T(8,128)} reshape(f32[22,1,768]{2,0,1:T(8,128)} %bitcast.153) | data formatting | bytes 135168 | tf_op jit(solution)/shard_map/reshape;squeeze | solution.py:69
  172.5 5.4 %fusion.30 = f32[22,48,256]{2,0,1:T(8,128)S(1)} fusion(f32[22,48,256]{2,0,1:T(8,128)S(1)} %fusion.19, f32[22,47,256]{2,0,1:T(8,128)} %get-tuple-element.32, f32[22,1,256]{2,0,1:T(8,128)} %bitcast.152, f32[22,48,240]{2,0,1:T(8,128)} %get-tuple-element.42, f32[22,48,16]{2,0,1:T(8,128)S(1)} %copy.97, f32[22,48,16]{2,0,1:T(8,128)} %copy.100, ...), kind=kLoop, calls=%fused_computation.43 | loop fusion | flops 7569408 | bytes 12300984 | tf_op jit(solution)/shard_map/jit(_where)/select_n | solution.py:116
  (291 shorter events, 82.4 us)
Async XLA Ops:
  3.2 12.3 %collective-permute-start = (f32[24,32,256]{2,0,1:T(8,128)S(1)}, f32[24,32,256]{2,0,1:T(8,128)S(1)}, u32[]{:S(2)}, u32[]{:S(2)}) collective-permute-start(f32[24,32,256]{2,0,1:T(8,128)S(1)} %pad_maximum_fusion.7), channel_id=1, source_target_pairs={{4,0},{8,4},{12,8},{16,12},{20,16},{24,20},{28,24},{5,1},{9,5},{13... | collective-permute-start | bytes 2359304 | tf_op jit(solution)/shard_map/ppermute | solution.py:30
  19.2 37.8 %copy-start.24 = (f32[1,48,16]{2,0,1:T(1,128)}, f32[1,48,16]{2,0,1:T(1,128)S(1)}, u32[]{:S(2)}) copy-start(f32[1,48,16]{2,0,1:T(1,128)S(1)} %get-tuple-element.92) | copy-start | bytes 9220
  19.2 40.8 %copy-start.22 = (f32[1,48,16]{2,0,1:T(1,128)}, f32[1,48,16]{2,0,1:T(1,128)S(1)}, u32[]{:S(2)}) copy-start(f32[1,48,16]{2,0,1:T(1,128)S(1)} %get-tuple-element.91) | copy-start | bytes 9220
  19.2 16.7 %copy-start.16 = (f32[1,47,256]{2,0,1:T(1,128)}, f32[1,47,256]{2,0,1:T(1,128)S(1)}, u32[]{:S(2)}) copy-start(f32[1,47,256]{2,0,1:T(1,128)S(1)} %get-tuple-element.89) | copy-start | bytes 144388
  19.3 16.7 %copy-start.19 = (f32[1,47,256]{2,0,1:T(1,128)}, f32[1,47,256]{2,0,1:T(1,128)S(1)}, u32[]{:S(2)}) copy-start(f32[1,47,256]{2,0,1:T(1,128)S(1)} %get-tuple-element.90) | copy-start | bytes 144388
  19.8 16.2 %copy-start.7 = (f32[1,48,240]{2,0,1:T(1,128)}, f32[1,48,240]{2,0,1:T(1,128)S(1)}, u32[]{:S(2)}) copy-start(f32[1,48,240]{2,0,1:T(1,128)S(1)} %get-tuple-element.87) | copy-start | bytes 138244
  19.8 16.2 %copy-start.10 = (f32[1,48,240]{2,0,1:T(1,128)}, f32[1,48,240]{2,0,1:T(1,128)S(1)}, u32[]{:S(2)}) copy-start(f32[1,48,240]{2,0,1:T(1,128)S(1)} %get-tuple-element.88) | copy-start | bytes 138244
  19.9 13.2 %collective-permute-start.2 = (f32[23,1,256]{2,0,1:T(8,128)S(1)}, f32[23,1,256]{2,0,1:T(8,128)S(1)}, u32[]{:S(2)}, u32[]{:S(2)}) collective-permute-start(f32[23,1,256]{2,0,1:T(8,128)S(1)} %pad_bitcast_fusion), channel_id=1, source_target_pairs={{4,0},{8,4},{12,8},{16,12},{20,16},{24,20},{28,24},{5,1},{9,5},{13... | collective-permute-start | bytes 70664 | tf_op jit(solution)/shard_map/ppermute | solution.py:22
  24.7 13.2 %copy-start.13 = (f32[1,48,256]{2,1,0:T(8,128)}, f32[1,48,256]{2,1,0:T(8,128)S(1)}, u32[]{:S(2)}) copy-start(f32[1,48,256]{2,1,0:T(8,128)S(1)} %copy.166) | copy-start | bytes 147460
  24.7 8.5 %collective-permute-start.1 = (f32[23,1,256]{2,0,1:T(8,128)S(1)}, f32[23,1,256]{2,0,1:T(8,128)S(1)}, u32[]{:S(2)}, u32[]{:S(2)}) collective-permute-start(f32[23,1,256]{2,0,1:T(8,128)S(1)} %pad_bitcast_fusion.1), channel_id=1, source_target_pairs={{0,4},{4,8},{8,12},{12,16},{16,20},{20,24},{24,28},{1,5},{5,9},{9,... | collective-permute-start | bytes 70664 | tf_op jit(solution)/shard_map/ppermute | solution.py:21
  26.9 6.3 %collective-permute-start.4 = (f32[23,1,768]{2,0,1:T(8,128)S(1)}, f32[23,1,768]{2,0,1:T(8,128)S(1)}, u32[]{:S(2)}, u32[]{:S(2)}) collective-permute-start(f32[23,1,768]{2,0,1:T(8,128)S(1)} %stack_reshape.25), channel_id=1, source_target_pairs={{1,0},{2,1},{3,2},{5,4},{6,5},{7,6},{9,8},{10,9},{11,10},{13,12},{... | collective-permute-start | bytes 211976 | tf_op jit(solution)/shard_map/ppermute | solution.py:22
  29.6 6.2 %collective-permute-start.3 = (f32[23,1,768]{2,0,1:T(8,128)S(1)}, f32[23,1,768]{2,0,1:T(8,128)S(1)}, u32[]{:S(2)}, u32[]{:S(2)}) collective-permute-start(f32[23,1,768]{2,0,1:T(8,128)S(1)} %stack_reshape.24), channel_id=1, source_target_pairs={{0,1},{1,2},{2,3},{4,5},{5,6},{6,7},{8,9},{9,10},{10,11},{12,13},{... | collective-permute-start | bytes 211976 | tf_op jit(solution)/shard_map/ppermute | solution.py:21
  50.5 16.2 %collective-permute-start.5 = (f32[23,1,256]{2,0,1:T(8,128)}, f32[23,1,256]{2,0,1:T(8,128)}, u32[]{:S(2)}, u32[]{:S(2)}) collective-permute-start(f32[23,1,256]{2,0,1:T(8,128)} %fusion.61), channel_id=1, source_target_pairs={{0,4},{4,8},{8,12},{12,16},{16,20},{20,24},{24,28},{1,5},{5,9},{9,... | collective-permute-start | bytes 70664 | tf_op jit(solution)/shard_map/ppermute | solution.py:21
  52.4 12.2 %collective-permute-start.6 = (f32[23,1,256]{2,0,1:T(8,128)}, f32[23,1,256]{2,0,1:T(8,128)}, u32[]{:S(2)}, u32[]{:S(2)}) collective-permute-start(f32[23,1,256]{2,0,1:T(8,128)} %fusion.58), channel_id=1, source_target_pairs={{4,0},{8,4},{12,8},{16,12},{20,16},{24,20},{28,24},{5,1},{9,5},{13... | collective-permute-start | bytes 70664 | tf_op jit(solution)/shard_map/ppermute | solution.py:22
  58.1 9.3 %collective-permute-start.8 = (f32[23,1,768]{2,0,1:T(8,128)}, f32[23,1,768]{2,0,1:T(8,128)S(1)}, u32[]{:S(2)}, u32[]{:S(2)}) collective-permute-start(f32[23,1,768]{2,0,1:T(8,128)} %stack_reshape.27), channel_id=1, source_target_pairs={{1,0},{2,1},{3,2},{5,4},{6,5},{7,6},{9,8},{10,9},{11,10},{13,12},{... | collective-permute-start | bytes 211976 | tf_op jit(solution)/shard_map/ppermute | solution.py:22
  60.5 8.2 %collective-permute-start.7 = (f32[23,1,768]{2,0,1:T(8,128)S(1)}, f32[23,1,768]{2,0,1:T(8,128)S(1)}, u32[]{:S(2)}, u32[]{:S(2)}) collective-permute-start(f32[23,1,768]{2,0,1:T(8,128)S(1)} %stack_reshape.26), channel_id=1, source_target_pairs={{0,1},{1,2},{2,3},{4,5},{5,6},{6,7},{8,9},{9,10},{10,11},{12,13},{... | collective-permute-start | bytes 211976 | tf_op jit(solution)/shard_map/ppermute | solution.py:21
  87.4 9.5 %copy-start.25 = (f32[1,48,16]{2,0,1:T(1,128)S(1)}, f32[1,48,16]{2,0,1:T(1,128)}, u32[]{:S(2)}) copy-start(f32[1,48,16]{2,0,1:T(1,128)} %copy-done.24) | copy-start | bytes 9220
  90.4 16.0 %collective-permute-start.9 = (f32[23,1,256]{2,0,1:T(8,128)}, f32[23,1,256]{2,0,1:T(8,128)}, u32[]{:S(2)}, u32[]{:S(2)}) collective-permute-start(f32[23,1,256]{2,0,1:T(8,128)} %fusion.62), channel_id=1, source_target_pairs={{0,4},{4,8},{8,12},{12,16},{16,20},{20,24},{24,28},{1,5},{5,9},{9,... | collective-permute-start | bytes 70664 | tf_op jit(solution)/shard_map/ppermute | solution.py:21
  92.4 12.0 %collective-permute-start.10 = (f32[23,1,256]{2,0,1:T(8,128)}, f32[23,1,256]{2,0,1:T(8,128)}, u32[]{:S(2)}, u32[]{:S(2)}) collective-permute-start(f32[23,1,256]{2,0,1:T(8,128)} %fusion.59), channel_id=1, source_target_pairs={{4,0},{8,4},{12,8},{16,12},{20,16},{24,20},{28,24},{5,1},{9,5},{13... | collective-permute-start | bytes 70664 | tf_op jit(solution)/shard_map/ppermute | solution.py:22
  98.0 9.1 %collective-permute-start.12 = (f32[23,1,768]{2,0,1:T(8,128)}, f32[23,1,768]{2,0,1:T(8,128)S(1)}, u32[]{:S(2)}, u32[]{:S(2)}) collective-permute-start(f32[23,1,768]{2,0,1:T(8,128)} %stack_reshape.29), channel_id=1, source_target_pairs={{1,0},{2,1},{3,2},{5,4},{6,5},{7,6},{9,8},{10,9},{11,10},{13,12},{... | collective-permute-start | bytes 211976 | tf_op jit(solution)/shard_map/ppermute | solution.py:22
  100.2 8.9 %copy-start.3 = (f32[1,48,256]{2,0,1:T(1,128)S(1)}, f32[1,48,256]{2,0,1:T(1,128)}, u32[]{:S(2)}) copy-start(f32[1,48,256]{2,0,1:T(1,128)} %copy-done.1) | copy-start | bytes 147460
  100.2 8.9 %copy-start.6 = (f32[1,48,256]{2,0,1:T(1,128)S(1)}, f32[1,48,256]{2,0,1:T(1,128)}, u32[]{:S(2)}) copy-start(f32[1,48,256]{2,0,1:T(1,128)} %copy-done.4) | copy-start | bytes 147460
  100.2 8.9 %copy-start.9 = (f32[1,48,240]{2,0,1:T(1,128)S(1)}, f32[1,48,240]{2,0,1:T(1,128)}, u32[]{:S(2)}) copy-start(f32[1,48,240]{2,0,1:T(1,128)} %copy-done.7) | copy-start | bytes 138244
  100.2 8.9 %copy-start.12 = (f32[1,48,240]{2,0,1:T(1,128)S(1)}, f32[1,48,240]{2,0,1:T(1,128)}, u32[]{:S(2)}) copy-start(f32[1,48,240]{2,0,1:T(1,128)} %copy-done.10) | copy-start | bytes 138244
  100.2 8.9 %copy-start.18 = (f32[1,47,256]{2,0,1:T(1,128)S(1)}, f32[1,47,256]{2,0,1:T(1,128)}, u32[]{:S(2)}) copy-start(f32[1,47,256]{2,0,1:T(1,128)} %copy-done.16) | copy-start | bytes 144388
  100.2 8.9 %copy-start.21 = (f32[1,47,256]{2,0,1:T(1,128)S(1)}, f32[1,47,256]{2,0,1:T(1,128)}, u32[]{:S(2)}) copy-start(f32[1,47,256]{2,0,1:T(1,128)} %copy-done.19) | copy-start | bytes 144388
  100.5 8.0 %collective-permute-start.11 = (f32[23,1,768]{2,0,1:T(8,128)S(1)}, f32[23,1,768]{2,0,1:T(8,128)S(1)}, u32[]{:S(2)}, u32[]{:S(2)}) collective-permute-start(f32[23,1,768]{2,0,1:T(8,128)S(1)} %stack_reshape.28), channel_id=1, source_target_pairs={{0,1},{1,2},{2,3},{4,5},{5,6},{6,7},{8,9},{9,10},{10,11},{12,13},{... | collective-permute-start | bytes 211976 | tf_op jit(solution)/shard_map/ppermute | solution.py:21
  129.0 9.5 %copy-start.26 = (f32[1,48,16]{2,0,1:T(1,128)S(1)}, f32[1,48,16]{2,0,1:T(1,128)}, u32[]{:S(2)}) copy-start(f32[1,48,16]{2,0,1:T(1,128)} %copy-done.24) | copy-start | bytes 9220
  132.0 22.1 %collective-permute-start.13 = (f32[23,1,256]{2,0,1:T(8,128)}, f32[23,1,256]{2,0,1:T(8,128)}, u32[]{:S(2)}, u32[]{:S(2)}) collective-permute-start(f32[23,1,256]{2,0,1:T(8,128)} %fusion.63), channel_id=1, source_target_pairs={{0,4},{4,8},{8,12},{12,16},{16,20},{20,24},{24,28},{1,5},{5,9},{9,... | collective-permute-start | bytes 70664 | tf_op jit(solution)/shard_map/ppermute | solution.py:21
  133.9 17.5 %collective-permute-start.14 = (f32[23,1,256]{2,0,1:T(8,128)}, f32[23,1,256]{2,0,1:T(8,128)}, u32[]{:S(2)}, u32[]{:S(2)}) collective-permute-start(f32[23,1,256]{2,0,1:T(8,128)} %fusion.60), channel_id=1, source_target_pairs={{4,0},{8,4},{12,8},{16,12},{20,16},{24,20},{28,24},{5,1},{9,5},{13... | collective-permute-start | bytes 70664 | tf_op jit(solution)/shard_map/ppermute | solution.py:22
  141.4 14.0 %collective-permute-start.16 = (f32[23,1,768]{2,0,1:T(8,128)}, f32[23,1,768]{2,0,1:T(8,128)}, u32[]{:S(2)}, u32[]{:S(2)}) collective-permute-start(f32[23,1,768]{2,0,1:T(8,128)} %stack_reshape.31), channel_id=1, source_target_pairs={{1,0},{2,1},{3,2},{5,4},{6,5},{7,6},{9,8},{10,9},{11,10},{13,12},{... | collective-permute-start | bytes 211976 | tf_op jit(solution)/shard_map/ppermute | solution.py:22
  147.3 14.7 %collective-permute-start.15 = (f32[23,1,768]{2,0,1:T(8,128)}, f32[23,1,768]{2,0,1:T(8,128)}, u32[]{:S(2)}, u32[]{:S(2)}) collective-permute-start(f32[23,1,768]{2,0,1:T(8,128)} %stack_reshape.30), channel_id=1, source_target_pairs={{0,1},{1,2},{2,3},{4,5},{5,6},{6,7},{8,9},{9,10},{10,11},{12,13},{... | collective-permute-start | bytes 211976 | tf_op jit(solution)/shard_map/ppermute | solution.py:21
  (47 other events, 135.0 us)
where the time goes:
time: 182 us; the launch traced here: 179 us
  local copies, waits for them, and re-layouts  87 us (48%)
  starting transfers between devices  52.5 us (29%)
  other arithmetic  31.5 us (17%)
  waiting for transfers between devices  5.6 us (3%)
  between operations  2.67 us (1%)
    ppermute x8, starting transfers between devices, with_halo(): after = lax.ppermute(initial, axis, down)  26.4 us
    ppermute x8, starting transfers between devices, with_halo(): before = lax.ppermute(last, axis, up)  23.3 us
    select_n x4, other arithmetic, smooth_boxes(): solution = jnp.where(active & (parity == half_sweep % 2), update, solution)  19.1 us
    unnamed x148, local copies, waits for them, and re-layouts  13.5 us
    slice x9, local copies, waits for them, and re-layouts, neighbours_of(): jnp.roll(field, -1, 2)  9.31 us
    slice x9, local copies, waits for them, and re-layouts, neighbours_of(): jnp.roll(field, plane_z - 1, 2)  9.3 us
    another operation x12, local copies, waits for them, and re-layouts, neighbours_of(): high_row.reshape(layers, row_count, plane_z)  8.29 us
    another operation x12, local copies, waits for them, and re-layouts, neighbours_of(): low_row.reshape(layers, row_count, plane_z)  6.83 us
  transfers between devices with their start and end apart: 17, of which 2 were waited for; matrix products, arithmetic and copies ran while one was open for 19% of the time, Pallas kernels for 0%

commit v1 on v0

v1 whole, which is shorter than its diff:
```python
import jax
import jax.numpy as jnp
from jax import lax
from jax.experimental import pallas as pl
from jax.experimental.pallas import tpu as pltpu
from jax.sharding import PartitionSpec as P

BOX_X = 16
PLANE_Z = 16
OLD_DEV = 2
MOST = 3
LANES = 128
PAIRS = 32
RIM = 64
VMEM_LIMIT = 48 * 1024 * 1024


def swap_pairs(count, first):
    lower = range(first, count - 1, 2)
    return [(i, i + 1) for i in lower] + [(i + 1, i) for i in lower]


def lane_places(rows):
    lane = lax.broadcasted_iota(jnp.int32, (rows, LANES), 1)
    even = (lane + lane // PLANE_Z) % 2 == 0
    return lane, even


def fold(ref, layer, tile, even):
    low = ref[tile, layer, pl.ds(0, 16, stride=2)]
    high = ref[tile, layer, pl.ds(1, 16, stride=2)]
    return jnp.where(even, low, high), jnp.where(even, high, low)


def pack_rims(
    src_ref, absorb_ref, conduct_ref, own_ref, first_ref, second_ref, box_ref, tiles_ref, sems
):
    channels = src_ref.shape[0]
    copies = []
    for tile in range(2):
        lanes = pl.ds(tile * LANES, LANES)
        for i, (source, place) in enumerate(
            [
                (src_ref.at[:, :, lanes], tiles_ref.at[tile, 0:channels]),
                (absorb_ref.at[:, lanes], tiles_ref.at[tile, channels]),
                (conduct_ref.at[:, lanes], tiles_ref.at[tile, channels + 1]),
            ]
        ):
            copies.append(pltpu.make_async_copy(source, place, sems.at[tile, i]))
    for copy in copies:
        copy.start()
    for copy in copies:
        copy.wait()
    lane, even = lane_places(16)
    low_half = lane < RIM
    even_group = lax.axis_index("grp") % 2 == 0

    def step(place, carry):
        red, black = zip(*[fold(tiles_ref, place, tile, even) for tile in range(2)])
        for tile in range(2):
            lanes = pl.ds(tile * LANES, LANES)
            own_ref[place, 0:16, lanes] = red[tile]
            own_ref[place, 16:32, lanes] = black[tile]
            box_ref[place, 0:8, lanes] = red[tile][:8]
            box_ref[place, 8:16, lanes] = black[tile][:8]
        low_rim = jnp.where(low_half, red[0], pltpu.roll(black[0], RIM, 1))
        high_rim = jnp.where(low_half, pltpu.roll(red[1], RIM, 1), black[1])
        first_ref[place] = jnp.where(even_group, high_rim, low_rim)
        second_ref[place] = jnp.where(even_group, low_rim, high_rim)
        return carry

    lax.fori_loop(0, channels + 2, step, 0)


def halo_tile(first_ref, second_ref, layer, low_half, even_group):
    first, second = first_ref[layer], second_ref[layer]
    above = jnp.where(even_group, first, second)
    below = jnp.where(even_group, second, first)
    red = jnp.where(low_half, above, pltpu.roll(below, RIM, 1))
    black = jnp.where(low_half, pltpu.roll(above, RIM, 1), below)
    return red, black


def pack_faces(own_ref, first_ref, second_ref, chip_ref, far_ref):
    layers = own_ref.shape[0]
    lane, _ = lane_places(16)
    low_half = lane < RIM
    even_group = lax.axis_index("grp") % 2 == 0
    even_box = lax.axis_index("boxes") % 2 == 0

    def layer_of(layer, conduct=False):
        halo_red, halo_black = halo_tile(first_ref, second_ref, layer, low_half, even_group)
        chip_ref[layer, 0:8] = halo_red[:8]
        far_ref[layer, 0:8] = halo_red[:8]
        chip_ref[layer, 8:16] = halo_black[:8]
        far_ref[layer, 8:16] = halo_black[:8]

        def rows(near, next_one):
            def row(colour, pair, tile):
                if tile < 2:
                    return own_ref[layer, pl.ds(16 * colour + pair, 1), pl.ds(tile * LANES, LANES)]
                return (halo_red, halo_black)[colour][pair : pair + 1]

            kept = [(0, near, 0), (0, near, 1), (0, near, 2), (0, next_one, 0), (0, next_one, 1)]
            kept += [(1, near, 0), (1, near, 1), (1, near, 2)]
            extra = [(0, next_one, 2), (1, next_one, 0), (1, next_one, 1), (1, next_one, 2)]
            return [row(*place) for place in kept], [row(*place) for place in extra]

        down, down_extra = rows(8, 9)
        up, up_extra = rows(15, 14)
        for i, (to_before, to_after) in enumerate(zip(down, up)):
            chip_ref[layer, 16 + i : 17 + i] = jnp.where(even_box, to_after, to_before)
            far_ref[layer, 16 + i : 17 + i] = jnp.where(even_box, to_before, to_after)
        if conduct:
            chip_ref[layers, 4:24] = jnp.zeros((20, LANES), jnp.float32)
            far_ref[layers, 4:24] = jnp.zeros((20, LANES), jnp.float32)
            for i, (to_before, to_after) in enumerate(zip(down_extra, up_extra)):
                chip_ref[layers, i : i + 1] = jnp.where(even_box, to_after, to_before)
                far_ref[layers, i : i + 1] = jnp.where(even_box, to_before, to_after)

    def step(layer, carry):
        layer_of(layer)
        return carry

    lax.fori_loop(0, layers - 1, step, 0)
    layer_of(layers - 1, True)


def z_up(x, z):
    return jnp.where(z == PLANE_Z - 1, pltpu.roll(x, PLANE_Z - 1, 1), pltpu.roll(x, LANES - 1, 1))


def z_down(x, z):
    return jnp.where(z == 0, pltpu.roll(x, LANES - PLANE_Z + 1, 1), pltpu.roll(x, 1, 1))


def around(tiles, lane, even, red, wanted=(0, 1, 2)):
    z = lane % PLANE_Z
    up = [pltpu.roll(x, LANES - PLANE_Z, 1) for x in tiles]
    down = [pltpu.roll(x, PLANE_Z, 1) for x in tiles]
    result = []
    for j in wanted:
        x = tiles[j]
        after = pltpu.roll(x, PAIRS - 1, 0)
        before = pltpu.roll(x, 1, 0)
        result.append(
            [
                x,
                jnp.where(even, before, after) if red else jnp.where(even, after, before),
                z_up(x, z),
                z_down(x, z),
                jnp.where(lane < LANES - PLANE_Z, up[j], up[(j + 1) % 3]),
                jnp.where(lane < PLANE_Z, down[(j + 2) % 3], down[j]),
            ]
        )
    return result


def smooth(
    lengths_ref, factor_ref, own_ref, first_ref, second_ref, box_ref, chip_ref, far_ref, out_ref,
    weight_ref, red_face, black_face, red_ref, black_ref, placed_ref, sems,
):
    layers = own_ref.shape[0]
    channels = layers - 2
    position = lax.axis_index("boxes")
    group = lax.axis_index("grp")
    even_box = position % 2 == 0
    even_group = group % 2 == 0
    last_box = position == lax.axis_size("boxes") - 1
    lane, even = lane_places(PAIRS)
    low_half = lane[:16] < RIM
    sub = lax.broadcasted_iota(jnp.int32, (8, LANES), 0)

    def assemble(layer, conduct=False):
        halo = halo_tile(first_ref, second_ref, layer, low_half, even_group)
        chip, far = chip_ref[layer], far_ref[layer]
        down = jnp.where(even_box, chip, far)
        up = jnp.where(even_box, far[16:], chip[16:])
        rows = lambda x: {(0, 0, 0): x[0:1], (0, 0, 1): x[1:2], (0, 0, 2): x[2:3], (0, 1, 0): x[3:4],
                          (0, 1, 1): x[4:5], (1, 0, 0): x[5:6], (1, 0, 1): x[6:7], (1, 0, 2): x[7:8]}
        down_rows, up_rows = rows(down[16:]), rows(up)
        if conduct:
            chip, far = chip_ref[layers, 0:8], far_ref[layers, 0:8]
            down_more = jnp.where(even_box, chip, far)
            up_more = jnp.where(even_box, far, chip)
            for i, key in enumerate([(0, 1, 2), (1, 1, 0), (1, 1, 1), (1, 1, 2)]):
                down_rows[key], up_rows[key] = down_more[i : i + 1], up_more[i : i + 1]
        colours = []
        for colour in range(2):
            tiles = []
            for j in range(3):
                if j < 2:
                    lanes = pl.ds(j * LANES, LANES)
                    own = own_ref[layer, 16 * colour : 16 * colour + 16, lanes]
                    box = box_ref[layer, 8 * colour : 8 * colour + 8, lanes]
                else:
                    own, box = halo[colour], down[8 * colour : 8 * colour + 8]
                spread = lambda x: jnp.broadcast_to(x, (8, LANES))
                edge = jnp.where(sub == 0, spread(down_rows[colour, 0, j]), 0.0)
                edge = jnp.where(sub == 7, spread(up_rows[colour, 0, j]), edge)
                if (colour, 1, j) in down_rows:
                    edge = jnp.where(sub == 1, spread(down_rows[colour, 1, j]), edge)
                    edge = jnp.where(sub == 6, spread(up_rows[colour, 1, j]), edge)
                tiles.append(jnp.concatenate([own, box, edge], 0))
            colours.append(tiles)
        return colours

    absorb = assemble(channels)
    conduct = assemble(channels + 1, True)
    for colour, face_ref in ((0, red_face), (1, black_face)):
        beside = around(conduct[1 - colour], lane, even, colour == 0)
        for j in range(3):
            total = jnp.zeros((PAIRS, LANES), jnp.float32)
            for i, other in enumerate(beside[j]):
                face = conduct[colour][j] + other
                face_ref[i, j] = face
                total = total + face
            weight_ref[colour, 0, j] = absorb[colour][j]
            weight_ref[colour, 1, j] = total

    pair = lax.broadcasted_iota(jnp.int32, (PAIRS, LANES), 0)
    no_after = jnp.where(last_box, 16, 26)
    no_before = jnp.where(position == 0, 32, 30)
    in_x = (pair < no_after) | (pair >= no_before)
    has_above = jnp.where(group == lax.axis_size("grp") - 1, 0, RIM)
    has_below = jnp.where(group == 0, LANES, RIM)
    in_y = (lane < has_above) | (lane >= has_below)
    inside = [in_x, in_x, in_x & in_y]

    box_count = lengths_ref[position]
    first_box = lax.fori_loop(0, position, lambda i, total: total + lengths_ref[i], jnp.int32(0))
    start = pl.multiple_of((first_box - position * OLD_DEV) * (BOX_X // 2), 8)

    def component(c, carry):
        source = assemble(c)
        factor = 0.5 * factor_ref[c]
        inverse = [
            [
                jnp.where(inside[j], 1.0 / (weight_ref[k, 0, j] + factor * weight_ref[k, 1, j]), 0.0)
                for j in range(3)
            ]
            for k in range(2)
        ]

        def update(colour, others, face_ref, wanted=(0, 1, 2)):
            result = []
            for j, beside in zip(wanted, around(others, lane, even, colour == 0, wanted)):
                inflow = face_ref[0, j] * beside[0]
                for i in range(1, 6):
                    inflow = inflow + face_ref[i, j] * beside[i]
                result.append((source[colour][j] + factor * inflow) * inverse[colour][j])
            return result

        red = [source[0][j] * inverse[0][j] for j in range(3)]
        black = update(1, red, black_face)
        red = update(0, black, red_face)
        black = update(1, red, black_face, (0, 1))
        for j in range(2):
            red_ref[j], black_ref[j] = red[j], black[j]
        for k in range(MOST):
            live = k < box_count
            for j in range(2):
                reds = red_ref[j, pl.ds(start + 8 * k, 8)]
                blacks = black_ref[j, pl.ds(start + 8 * k, 8)]
                low = jnp.where(live, jnp.where(even[:8], reds, blacks), 0.0)
                high = jnp.where(live, jnp.where(even[:8], blacks, reds), 0.0)
                placed_ref[j, c, pl.ds(BOX_X * k, 8, stride=2)] = low
                placed_ref[j, c, pl.ds(BOX_X * k + 1, 8, stride=2)] = high
        return carry

    copies = []
    half = channels // 2
    for part, (begin, end) in enumerate([(0, half), (half, channels)]):
        lax.fori_loop(begin, end, component, 0)
        for j in range(2):
            copy = pltpu.make_async_copy(
                placed_ref.at[j, begin:end],
                out_ref.at[begin:end, :, pl.ds(j * LANES, LANES)],
                sems.at[part, j],
            )
            copy.start()
            copies.append(copy)
    for copy in copies:
        copy.wait()


def in_vmem(count):
    return [pl.BlockSpec(memory_space=pltpu.VMEM)] * count


def on_device(sources, absorption, conductance, diffusivity, run_lengths):
    channels, planes, cells = sources.shape
    boxes, groups = lax.axis_size("boxes"), lax.axis_size("grp")
    layers = channels + 2
    real = lambda *shape: jax.ShapeDtypeStruct(shape, jnp.float32)
    params = pltpu.CompilerParams(vmem_limit_bytes=VMEM_LIMIT)
    own, first, second, box = pl.pallas_call(
        pack_rims,
        out_shape=(real(layers, planes, cells), real(layers, 16, LANES), real(layers, 16, LANES),
                   real(layers, 16, cells)),
        in_specs=[pl.BlockSpec(memory_space=pl.ANY)] * 3,
        out_specs=tuple(in_vmem(4)),
        scratch_shapes=[
            pltpu.VMEM((2, layers, planes, LANES), jnp.float32),
            pltpu.SemaphoreType.DMA((2, 3)),
        ],
        compiler_params=params,
    )(sources, absorption, conductance)
    first = lax.ppermute(first, "grp", swap_pairs(groups, 0))
    second = lax.ppermute(second, "grp", swap_pairs(groups, 1))
    box = lax.ppermute(box, "boxes", [(i + 1, i) for i in range(boxes - 1)])
    chip, far = pl.pallas_call(
        pack_faces,
        out_shape=(real(layers + 1, 24, LANES),) * 2,
        in_specs=in_vmem(3),
        out_specs=tuple(in_vmem(2)),
        compiler_params=params,
    )(own, first, second)
    chip = lax.ppermute(chip, "boxes", swap_pairs(boxes, 0))
    far = lax.ppermute(far, "boxes", swap_pairs(boxes, 1))
    smem = pl.BlockSpec(memory_space=pltpu.SMEM)
    return pl.pallas_call(
        smooth,
        out_shape=real(channels, MOST * BOX_X, cells),
        in_specs=[smem, smem] + in_vmem(6),
        out_specs=pl.BlockSpec(memory_space=pl.ANY),
        scratch_shapes=[
            pltpu.VMEM((2, 2, 3, PAIRS, LANES), jnp.float32),
            pltpu.VMEM((6, 3, PAIRS, LANES), jnp.float32),
            pltpu.VMEM((6, 3, PAIRS, LANES), jnp.float32),
            pltpu.VMEM((2, PAIRS, LANES), jnp.float32),
            pltpu.VMEM((2, PAIRS, LANES), jnp.float32),
            pltpu.VMEM((2, channels, MOST * BOX_X, LANES), jnp.float32),
            pltpu.SemaphoreType.DMA((2, 2)),
        ],
        compiler_params=params,
    )(run_lengths, diffusivity, own, first, second, box, chip, far)


def solution(mesh):
    return jax.shard_map(
        on_device,
        mesh=mesh,
        in_specs=(P(None, "boxes", "grp"), P("boxes", "grp"), P("boxes", "grp"), P(), P()),
        out_specs=P(None, "boxes", "grp"),
        check_vma=False,
    )
```

time: 182 us -> 40.1 us (0.22); the launches traced: 179 us -> 39.3 us
  local copies, waits for them, and re-layouts: 87 us -> 2.63 us
  starting transfers between devices: 52.5 us -> 10.8 us
  other arithmetic: 31.5 us -> 0 us
  Pallas kernels: 0 us -> 14.8 us
  waiting for transfers between devices: 5.6 us -> 11 us
  between operations: 2.67 us -> 0.07 us
    ppermute x17 -> x5, starting transfers between devices: 52.5 us -> 10.8 us  [the longest x1 4.6 us: on_device(): second = lax.ppermute(second, 'grp', swap_pairs(groups, 1))]
    slice x48 -> x0, local copies, waits for them, and re-layouts: 38.5 us -> none  [the longest x9 9.31 us: neighbours_of(): jnp.roll(field, -1, 2)]
    another operation x35 -> x0, local copies, waits for them, and re-layouts: 21.8 us -> none  [the longest x12 8.29 us: neighbours_of(): high_row.reshape(layers, row_count, plane_z)]
    select_n x6 -> x0, other arithmetic: 20.5 us -> none  [the longest x4 19.1 us: smooth_boxes(): solution = jnp.where(active & (parity == half_sweep % 2), update, solution)]
    pallas_call x0 -> x3, Pallas kernels: none -> 14.8 us  [the longest x1 11.2 us: on_device(): pl.pallas_call(smooth, out_shape=real(channels, MOST * BOX_X, cells), in_...]
    unnamed x148 -> x10, local copies, waits for them, and re-layouts: 13.5 us -> 2.63 us
    broadcast_in_dim x6 -> x0, local copies, waits for them, and re-layouts: 5.6 us -> none  [the longest x4 4.04 us: neighbours_of(): x_upper = jnp.where(at_end, above_plane, x_next)]
    ppermute x17 -> x5, waiting for transfers between devices: 5.6 us -> 11 us  [the longest x1 8.61 us: on_device(): far = lax.ppermute(far, 'boxes', swap_pairs(boxes, 1))]
  transfers between devices with their start and end apart: 17 -> 5, of which waited for: 2 -> 2; matrix products, arithmetic and copies ran while one was open for 19% -> 0% of each run, Pallas kernels for 0% -> 4%
where the time goes in v1:
time: 40.1 us; the launch traced here: 39.3 us
  Pallas kernels  14.8 us (37%)
  waiting for transfers between devices  11 us (27%)
  starting transfers between devices  10.8 us (27%)
  local copies, waits for them, and re-layouts  2.63 us (7%)
    pallas_call x1, Pallas kernels, on_device(): pl.pallas_call(smooth, out_shape=real(channels, MOST * BOX_X, cells), in_...  11.2 us
    ppermute x1, waiting for transfers between devices, on_device(): far = lax.ppermute(far, 'boxes', swap_pairs(boxes, 1))  8.61 us
    ppermute x1, starting transfers between devices, on_device(): second = lax.ppermute(second, 'grp', swap_pairs(groups, 1))  4.6 us
    ppermute x1, starting transfers between devices, on_device(): far = lax.ppermute(far, 'boxes', swap_pairs(boxes, 1))  3.43 us
    unnamed x10, local copies, waits for them, and re-layouts  2.63 us
    ppermute x1, waiting for transfers between devices, on_device(): second = lax.ppermute(second, 'grp', swap_pairs(groups, 1))  2.37 us
    ppermute x1, starting transfers between devices, on_device(): box = lax.ppermute(box, 'boxes', [(i + 1, i) for i in range(boxes - 1)])  2.22 us
    pallas_call x1, Pallas kernels, on_device(): pl.pallas_call(pack_rims, out_shape=(real(layers, planes, cells), real(la...  1.9 us
  transfers between devices with their start and end apart: 5, of which 2 were waited for; matrix products, arithmetic and copies ran while one was open for 0% of the time, Pallas kernels for 4%

profile of v1, /device:TPU:12, one launch (start us, length us, event | category | flops | bytes accessed | tf_op | source)
XLA Modules:
  0.0 39.3 jit_solution(5912270580325888082)
XLA Ops:
  0.0 0.0 copy-start
  0.0 1.1 %copy-done = f32[22,32,256]{2,1,0:T(8,128)S(1)} copy-done((f32[22,32,256]{2,1,0:T(8,128)S(1)}, f32[22,32,256]{2,1,0:T(8,128)}, u32[]{:S(2)}) %copy-start) | copy-done | bytes 720920
  1.1 0.0 copy-start.1
  1.1 0.8 %copy-done.1 = f32[32,256]{1,0:T(8,128)S(1)} copy-done((f32[32,256]{1,0:T(8,128)S(1)}, f32[32,256]{1,0:T(8,128)}, u32[]{:S(2)}) %copy-start.1) | copy-done | bytes 32792
  1.9 0.0 copy-start.2
  1.9 0.8 %copy-done.2 = f32[32,256]{1,0:T(8,128)S(1)} copy-done((f32[32,256]{1,0:T(8,128)S(1)}, f32[32,256]{1,0:T(8,128)}, u32[]{:S(2)}) %copy-start.2) | copy-done | bytes 32792
  2.6 0.0 copy-start.3
  2.6 0.0 copy-start.4
  2.6 1.9 %shard_map.55 = (f32[24,32,256]{2,1,0:T(8,128)S(1)}, f32[24,16,128]{2,1,0:T(8,128)S(1)}, f32[24,16,128]{2,1,0:T(8,128)S(1)}, f32[24,16,256]{2,1,0:T(8,128)S(1)}) custom-call(f32[22,32,256]{2,1,0:T(8,128)S(1)} %copy-done, f32[32,256]{1,0:T(8,128)S(1)} %copy-done.1, f32[32,256]{1,0:T(8,128)S(1)} %copy-done.2), custom_call_target="tpu_custom_call" | custom-call | tf_op jit(solution)/shard_map/pallas_call | solution.py:297
  4.5 0.5 %collective-permute-start = (f32[24,16,128]{2,1,0:T(8,128)S(1)}, f32[24,16,128]{2,1,0:T(8,128)S(1)}, u32[]{:S(2)}, u32[]{:S(2)}) collective-permute-start(f32[24,16,128]{2,1,0:T(8,128)S(1)} %get-tuple-element.12), channel_id=1, source_target_pairs={{0,1},{2,3},{1,0},{3,2},{4,5},{6,7},{5,4},{7,6},{8,9},{10,11},{9,8... | collective-permute-start | bytes 589832 | tf_op jit(solution)/shard_map/ppermute | solution.py:309
  5.1 4.6 %collective-permute-start.1 = (f32[24,16,128]{2,1,0:T(8,128)S(1)}, f32[24,16,128]{2,1,0:T(8,128)S(1)}, u32[]{:S(2)}, u32[]{:S(2)}) collective-permute-start(f32[24,16,128]{2,1,0:T(8,128)S(1)} %get-tuple-element.13), channel_id=1, source_target_pairs={{1,2},{2,1},{5,6},{6,5},{9,10},{10,9},{13,14},{14,13},{17,18},{18,... | collective-permute-start | bytes 589832 | tf_op jit(solution)/shard_map/ppermute | solution.py:310
  9.7 2.2 %collective-permute-start.2 = (f32[24,16,256]{2,1,0:T(8,128)S(1)}, f32[24,16,256]{2,1,0:T(8,128)S(1)}, u32[]{:S(2)}, u32[]{:S(2)}) collective-permute-start(f32[24,16,256]{2,1,0:T(8,128)S(1)} %get-tuple-element.14), channel_id=1, source_target_pairs={{4,0},{8,4},{12,8},{16,12},{20,16},{24,20},{28,24},{5,1},{9,5},{13... | collective-permute-start | bytes 1179656 | tf_op jit(solution)/shard_map/ppermute | solution.py:311
  11.9 0.0 collective-permute-done.first_ref
  11.9 2.4 %collective-permute-done.1.second_ref = f32[24,16,128]{2,1,0:T(8,128)S(1)} collective-permute-done((f32[24,16,128]{2,1,0:T(8,128)S(1)}, f32[24,16,128]{2,1,0:T(8,128)S(1)}, u32[]{:S(2)}, u32[]{:S(2)}) %collective-permute-start.1) | collective-permute-done | bytes 196640 | tf_op jit(solution)/shard_map/ppermute | solution.py:310
  14.3 1.7 %shard_map.56 = (f32[25,24,128]{2,1,0:T(8,128)S(1)}, f32[25,24,128]{2,1,0:T(8,128)S(1)}) custom-call(f32[24,32,256]{2,1,0:T(8,128)S(1)} %get-tuple-element.11.own_ref, f32[24,16,128]{2,1,0:T(8,128)S(1)} %collective-permute-done.first_ref, f32[24,16,128]{2,1,0:T(8,128)S(1)} %collective-permute-done.1.second_ref), custom_call_target="tpu_custom_call" | custom-call | tf_op jit(solution)/shard_map/pallas_call | solution.py:312
  16.0 0.1 collective-permute-start.3
  16.1 3.4 %collective-permute-start.4 = (f32[25,24,128]{2,1,0:T(8,128)S(1)}, f32[25,24,128]{2,1,0:T(8,128)S(1)}, u32[]{:S(2)}, u32[]{:S(2)}) collective-permute-start(f32[25,24,128]{2,1,0:T(8,128)S(1)} %get-tuple-element.16), channel_id=1, source_target_pairs={{4,8},{12,16},{20,24},{8,4},{16,12},{24,20},{5,9},{13,17},{21,25},... | collective-permute-start | bytes 921608 | tf_op jit(solution)/shard_map/ppermute | solution.py:320
  19.5 0.0 collective-permute-done.2.box_ref
  19.5 0.0 collective-permute-done.3.chip_ref
  19.5 8.6 %collective-permute-done.4.far_ref = f32[25,24,128]{2,1,0:T(8,128)S(1)} collective-permute-done((f32[25,24,128]{2,1,0:T(8,128)S(1)}, f32[25,24,128]{2,1,0:T(8,128)S(1)}, u32[]{:S(2)}, u32[]{:S(2)}) %collective-permute-start.4) | collective-permute-done | bytes 307232 | tf_op jit(solution)/shard_map/ppermute | solution.py:320
  28.2 0.0 copy-done.3
  28.2 0.0 copy-done.4
  28.2 11.2 %shard_map.57 = f32[22,48,256]{2,1,0:T(8,128)} custom-call(s32[8]{0:T(128)S(1)} %copy-done.3, f32[22]{0:T(128)S(1)} %copy-done.4, f32[24,32,256]{2,1,0:T(8,128)S(1)} %get-tuple-element.11.own_ref, f32[24,16,128]{2,1,0:T(8,128)S(1)} %collective-permute-done.first_ref, f32[24,16,128]{2,1,0:T(8,128)S(1)} %collective-permute-done.1.second_ref, ...), custom_call_target="tpu_custom_call" | custom-call | tf_op jit(solution)/shard_map/pallas_call | solution.py:322
Async XLA Ops:
  0.0 1.1 %copy-start = (f32[22,32,256]{2,1,0:T(8,128)S(1)}, f32[22,32,256]{2,1,0:T(8,128)}, u32[]{:S(2)}) copy-start(f32[22,32,256]{2,1,0:T(8,128)} %src_ref.1) | copy-start | bytes 2162692
  1.1 0.8 %copy-start.1 = (f32[32,256]{1,0:T(8,128)S(1)}, f32[32,256]{1,0:T(8,128)}, u32[]{:S(2)}) copy-start(f32[32,256]{1,0:T(8,128)} %absorb_ref.1) | copy-start | bytes 98308
  1.9 0.8 %copy-start.2 = (f32[32,256]{1,0:T(8,128)S(1)}, f32[32,256]{1,0:T(8,128)}, u32[]{:S(2)}) copy-start(f32[32,256]{1,0:T(8,128)} %conduct_ref.1) | copy-start | bytes 98308
  2.6 25.5 %copy-start.3 = (s32[8]{0:T(128)S(1)}, s32[8]{0:T(128)}, u32[]{:S(2)}) copy-start(s32[8]{0:T(128)} %lengths_ref.1) | copy-start | bytes 100
  2.6 25.5 %copy-start.4 = (f32[22]{0:T(128)S(1)}, f32[22]{0:T(128)}, u32[]{:S(2)}) copy-start(f32[22]{0:T(128)} %factor_ref.1) | copy-start | bytes 268
  4.5 7.4 %collective-permute-start = (f32[24,16,128]{2,1,0:T(8,128)S(1)}, f32[24,16,128]{2,1,0:T(8,128)S(1)}, u32[]{:S(2)}, u32[]{:S(2)}) collective-permute-start(f32[24,16,128]{2,1,0:T(8,128)S(1)} %get-tuple-element.12), channel_id=1, source_target_pairs={{0,1},{2,3},{1,0},{3,2},{4,5},{6,7},{5,4},{7,6},{8,9},{10,11},{9,8... | collective-permute-start | bytes 589832 | tf_op jit(solution)/shard_map/ppermute | solution.py:309
  5.1 9.2 %collective-permute-start.1 = (f32[24,16,128]{2,1,0:T(8,128)S(1)}, f32[24,16,128]{2,1,0:T(8,128)S(1)}, u32[]{:S(2)}, u32[]{:S(2)}) collective-permute-start(f32[24,16,128]{2,1,0:T(8,128)S(1)} %get-tuple-element.13), channel_id=1, source_target_pairs={{1,2},{2,1},{5,6},{6,5},{9,10},{10,9},{13,14},{14,13},{17,18},{18,... | collective-permute-start | bytes 589832 | tf_op jit(solution)/shard_map/ppermute | solution.py:310
  9.7 9.9 %collective-permute-start.2 = (f32[24,16,256]{2,1,0:T(8,128)S(1)}, f32[24,16,256]{2,1,0:T(8,128)S(1)}, u32[]{:S(2)}, u32[]{:S(2)}) collective-permute-start(f32[24,16,256]{2,1,0:T(8,128)S(1)} %get-tuple-element.14), channel_id=1, source_target_pairs={{4,0},{8,4},{12,8},{16,12},{20,16},{24,20},{28,24},{5,1},{9,5},{13... | collective-permute-start | bytes 1179656 | tf_op jit(solution)/shard_map/ppermute | solution.py:311
  16.0 3.5 %collective-permute-start.3 = (f32[25,24,128]{2,1,0:T(8,128)S(1)}, f32[25,24,128]{2,1,0:T(8,128)S(1)}, u32[]{:S(2)}, u32[]{:S(2)}) collective-permute-start(f32[25,24,128]{2,1,0:T(8,128)S(1)} %get-tuple-element.15), channel_id=1, source_target_pairs={{0,4},{8,12},{16,20},{24,28},{4,0},{12,8},{20,16},{28,24},{1,5},{9... | collective-permute-start | bytes 921608 | tf_op jit(solution)/shard_map/ppermute | solution.py:319
  16.1 12.1 %collective-permute-start.4 = (f32[25,24,128]{2,1,0:T(8,128)S(1)}, f32[25,24,128]{2,1,0:T(8,128)S(1)}, u32[]{:S(2)}, u32[]{:S(2)}) collective-permute-start(f32[25,24,128]{2,1,0:T(8,128)S(1)} %get-tuple-element.16), channel_id=1, source_target_pairs={{4,8},{12,16},{20,24},{8,4},{16,12},{24,20},{5,9},{13,17},{21,25},... | collective-permute-start | bytes 921608 | tf_op jit(solution)/shard_map/ppermute | solution.py:320

commit v2 on v0

v2 whole, which is shorter than its diff:
```python
import jax
import jax.numpy as jnp
from jax import lax
from jax.experimental import pallas as pl
from jax.experimental.pallas import tpu as pltpu
from jax.sharding import PartitionSpec as P

BOX_X = 16
PLANE_Z = 16
OLD_DEV = 2
MOST = 3
LANES = 128
SUBS = 8
RING = 32
RIM = 64
VMEM_LIMIT = 40 * 1024 * 1024
F32 = jnp.float32


def swap_pairs(count, first):
    lower = range(first, count - 1, 2)
    return [(i, i + 1) for i in lower] + [(i + 1, i) for i in lower]


def lane_places(rows):
    lane = lax.broadcasted_iota(jnp.int32, (rows, LANES), 1)
    even = (lane + lane // PLANE_Z) % 2 == 0
    return lane, even


def roll(x, shift):
    return pltpu.roll(x, shift % LANES, 1)


def pack_rim(red, black, lane):
    first = jnp.where(lane < 64, red[0], roll(red[1], 64))
    first = jnp.where((lane >= 48) & (lane < 64), roll(black[2], 48), first)
    first = jnp.where(lane >= 112, roll(black[2], 96), first)
    second = jnp.where(lane < 32, black[0], jnp.where(lane < 64, roll(black[1], 32), roll(red[2], 64)))
    return first, second


def unpack_rim(first, second, lane):
    black = jnp.where(lane < 16, roll(first, -48), roll(first, -96))
    return [first, roll(first, -64), roll(second, -64)], [second, roll(second, -32), black]


def pack_halo(red, black, lane):
    gap = (lane >= 48) & (lane < 80)
    wide = (lane >= 32) & (lane < 96)
    return [
        jnp.where(gap, roll(black[2], 48), red[0]),
        jnp.where(gap, roll(black[2], -48), red[1]),
        red[2],
        jnp.where(wide, roll(black[1], 64), black[0]),
    ]


def unpack_halo(parts, lane):
    black = jnp.where(lane < 64, roll(parts[0], -48), roll(parts[1], 48))
    return parts[:3], [parts[3], roll(parts[3], 64), black]


def pack_rims(
    src_ref, absorb_ref, conduct_ref,
    own_ref, plane_ref, first_ref, second_ref, box_ref,
    tiles_ref, sems,
):
    channels, planes, _ = src_ref.shape
    layers = channels + 2
    half = planes // 2
    copies = []
    for tile in range(2):
        lanes = pl.ds(tile * LANES, LANES)
        for i, (source, place, count) in enumerate(
            [
                (src_ref.at[:, :, lanes], 0, channels),
                (absorb_ref.at[:, lanes], channels, None),
                (conduct_ref.at[:, lanes], channels + 1, None),
            ]
        ):
            into = tiles_ref.at[tile, place] if count is None else tiles_ref.at[tile, pl.ds(0, count)]
            copies.append(pltpu.make_async_copy(source, into, sems.at[tile, i]))
    for copy in copies:
        copy.start()
    for copy in copies:
        copy.wait()

    lane, even = lane_places(SUBS)
    even_group = lax.axis_index("grp") % 2 == 0
    flat = tiles_ref.reshape(2 * layers * planes, LANES)

    def step(p, carry):
        reds, blacks = [], []
        for j in range(2):
            red, black = [], []
            for ct in range(3):
                row = (j * layers + ct * SUBS) * planes + 2 * p
                low = flat[pl.ds(row, SUBS, stride=planes)]
                high = flat[pl.ds(row + 1, SUBS, stride=planes)]
                red.append(jnp.where(even, low, high))
                black.append(jnp.where(even, high, low))
                own_ref[0, ct, p, j] = red[ct]
                own_ref[1, ct, p, j] = black[ct]
            reds.append(red)
            blacks.append(black)
        low_rim = pack_rim(reds[0], blacks[0], lane)
        high_rim = pack_rim([roll(x, 48) for x in reds[1]], [roll(x, 32) for x in blacks[1]], lane)
        for i in range(2):
            first_ref[2 * p + i] = jnp.where(even_group, high_rim[i], low_rim[i])
            second_ref[2 * p + i] = jnp.where(even_group, low_rim[i], high_rim[i])
        return carry

    lax.fori_loop(0, half, step, 0)

    for q in range(2):
        compact = []
        for j in range(2):
            row = (j * layers + channels + 1) * planes + 16 * q
            low = flat[pl.ds(row, SUBS, stride=2)]
            high = flat[pl.ds(row + 1, SUBS, stride=2)]
            compact.append((jnp.where(even, low, high), jnp.where(even, high, low)))
            for colour in range(2):
                plane_ref[colour, j, q] = compact[j][colour]
                if q == 0:
                    box_ref[96 + 2 * colour + j] = compact[j][colour]
        low_rim = jnp.where(lane < RIM, compact[0][0], roll(compact[0][1], RIM))
        high_rim = jnp.where(lane < RIM, roll(compact[1][0], RIM), compact[1][1])
        first_ref[2 * half + q] = jnp.where(even_group, high_rim, low_rim)
        second_ref[2 * half + q] = jnp.where(even_group, low_rim, high_rim)

    def copy_box(p, carry):
        for colour in range(2):
            for ct in range(3):
                for j in range(2):
                    box_ref[((colour * 3 + ct) * 8 + p) * 2 + j] = own_ref[colour, ct, p, j]
        return carry

    lax.fori_loop(0, 8, copy_box, 0)


def pack_faces(own_ref, plane_ref, first_ref, second_ref, rim_ref, rim_plane_ref, chip_ref, far_ref):
    pairs = own_ref.shape[2]
    lane, _ = lane_places(SUBS)
    low_half = lane < RIM
    even_group = lax.axis_index("grp") % 2 == 0
    even_box = lax.axis_index("boxes") % 2 == 0

    def sides(i):
        first, second = first_ref[i], second_ref[i]
        return jnp.where(even_group, first, second), jnp.where(even_group, second, first)

    def step(p, carry):
        above, below = zip(*[sides(2 * p + i) for i in range(2)])
        above, below = unpack_rim(*above, lane), unpack_rim(*below, lane)
        reds, blacks = [], []
        for ct in range(3):
            reds.append(jnp.where(low_half, above[0][ct], roll(below[0][ct], -48)))
            blacks.append(jnp.where(low_half, above[1][ct], roll(below[1][ct], -32)))
            rim_ref[0, ct, p] = reds[ct]
            rim_ref[1, ct, p] = blacks[ct]
        return reds, blacks

    def with_halo(p, carry):
        reds, blacks = step(p, carry)
        for i, part in enumerate(pack_halo(reds, blacks, lane)):
            chip_ref[4 * p + i] = part
            far_ref[4 * p + i] = part
        return carry

    def without_halo(p, carry):
        step(p, carry)
        return carry

    lax.fori_loop(0, 8, with_halo, 0)
    lax.fori_loop(8, pairs, without_halo, 0)
    for q in range(2):
        above, below = sides(2 * pairs + q)
        rim_plane_ref[0, q] = jnp.where(low_half, above, roll(below, RIM))
        rim_plane_ref[1, q] = jnp.where(low_half, roll(above, RIM), below)

    def put(i, to_before, to_after):
        chip_ref[i] = jnp.where(even_box, to_after, to_before)
        far_ref[i] = jnp.where(even_box, to_before, to_after)

    def piece(colour, ct, p, j):
        return own_ref[colour, ct, p, j] if j < 2 else rim_ref[colour, ct, p]

    for ct in range(3):
        for i, (colour, near, j) in enumerate(EDGE):
            down, up = (8, 15) if near else (9, 14)
            put(32 + ct * 8 + i, piece(colour, ct, down, j), piece(colour, ct, up, j))
    for colour in range(2):
        chip_ref[56 + colour] = rim_plane_ref[colour, 0]
        far_ref[56 + colour] = rim_plane_ref[colour, 0]
    for colour in range(2):
        for near in range(2):
            for j in range(3):
                down, up = (0, 7) if near else (1, 6)
                rows = [
                    (plane_ref[colour, j, 1] if j < 2 else rim_plane_ref[colour, 1])[k : k + 1]
                    for k in (down, up)
                ]
                k = colour * 6 + near * 3 + j
                chip_ref[58 + k // 8, k % 8 : k % 8 + 1] = jnp.where(even_box, rows[1], rows[0])
                far_ref[58 + k // 8, k % 8 : k % 8 + 1] = jnp.where(even_box, rows[0], rows[1])
    chip_ref[59, 4:8] = jnp.zeros((4, LANES), F32)
    far_ref[59, 4:8] = jnp.zeros((4, LANES), F32)


EDGE = [(0, 1, 0), (0, 1, 1), (0, 1, 2), (0, 0, 0), (0, 0, 1), (1, 1, 0), (1, 1, 1), (1, 1, 2)]


def z_up(x, z):
    return jnp.where(z == PLANE_Z - 1, roll(x, PLANE_Z - 1), roll(x, -1))


def z_down(x, z):
    return jnp.where(z == 0, roll(x, 1 - PLANE_Z), roll(x, 1))


def lane_neighbours(tiles, lane, wanted=(0, 1, 2)):
    z = lane % PLANE_Z
    up = [roll(x, -PLANE_Z) for x in tiles]
    down = [roll(x, PLANE_Z) for x in tiles]
    return [
        [
            z_up(tiles[j], z),
            z_down(tiles[j], z),
            jnp.where(lane < LANES - PLANE_Z, up[j], up[(j + 1) % 3]),
            jnp.where(lane < PLANE_Z, down[(j + 2) % 3], down[j]),
        ]
        for j in wanted
    ]


def smooth(
    lengths_ref, factor_ref, own_ref, plane_ref, rim_ref, rim_plane_ref, box_ref, chip_ref, far_ref,
    out_ref,
    face_ref, weight_ref, box_rim_ref, edge_ref, inverse_ref, value_ref, placed_ref, sems,
):
    channels, rows, _ = out_ref.shape
    position = lax.axis_index("boxes")
    group = lax.axis_index("grp")
    even_box = position % 2 == 0
    last_box = position == lax.axis_size("boxes") - 1
    lane, even = lane_places(SUBS)
    sub = lax.broadcasted_iota(jnp.int32, (SUBS, LANES), 0)
    tiles = range(3)

    def from_after(i):
        return jnp.where(even_box, chip_ref[i], far_ref[i])

    def from_before(i):
        return jnp.where(even_box, far_ref[i], chip_ref[i])

    edges = [[jnp.concatenate([get(58), get(59)], 0) for get in (from_after, from_before)]][0]
    conduct = []
    for colour in range(2):
        planes = []
        for j in tiles:
            own = [plane_ref[colour, j, q] if j < 2 else rim_plane_ref[colour, q] for q in range(2)]
            box = box_ref[96 + 2 * colour + j] if j < 2 else from_after(56 + colour)
            edge = jnp.zeros((SUBS, LANES), F32)
            for place, side, near in ((0, 0, 1), (1, 0, 0), (6, 1, 0), (7, 1, 1)):
                k = colour * 6 + near * 3 + j
                edge = jnp.where(sub == place, jnp.broadcast_to(edges[side][k : k + 1], sub.shape), edge)
            planes.append(jnp.concatenate(own + [box, edge], 0))
        conduct.append(planes)
    wide_lane, wide_even = lane_places(RING)
    for colour in range(2):
        others = conduct[1 - colour]
        beside = lane_neighbours(others, wide_lane)
        for j in tiles:
            after, before = pltpu.roll(others[j], RING - 1, 0), pltpu.roll(others[j], 1, 0)
            across = jnp.where(wide_even, *((before, after) if colour == 0 else (after, before)))
            total = jnp.zeros((RING, LANES), F32)
            for i, other in enumerate([others[j], across] + beside[j]):
                face = conduct[colour][j] + other
                face_ref[colour, i, j] = face
                total = total + face
            weight_ref[colour, j] = total

    def open_box(p, carry):
        reds, blacks = unpack_halo([from_after(4 * p + i) for i in range(4)], lane)
        for ct in range(3):
            box_rim_ref[0, ct, p], box_rim_ref[1, ct, p] = reds[ct], blacks[ct]
        return carry

    lax.fori_loop(0, 8, open_box, 0)
    for ct in range(3):
        for i in range(8):
            edge_ref[0, ct, i] = from_before(32 + ct * 8 + i)
            edge_ref[1, ct, i] = from_after(32 + ct * 8 + i)

    def own_source(q):
        p = q - 2
        return lambda colour, ct, j: own_ref[colour, ct, p, j] if j < 2 else rim_ref[colour, ct, p]

    def box_source(q):
        p = q - 18
        return lambda colour, ct, j: (
            box_ref[((colour * 3 + ct) * 8 + p) * 2 + j] if j < 2 else box_rim_ref[colour, ct, p]
        )

    def edge_source(q):
        near, side = (q in (1, 26)), int(q > 20)
        return lambda colour, ct, j: edge_ref[side, ct, EDGE.index((colour, int(near), j))]

    lane_limit = [
        None,
        None,
        (lane < jnp.where(group == lax.axis_size("grp") - 1, 0, RIM))
        | (lane >= jnp.where(group == 0, LANES, RIM)),
    ]
    factors = []
    for ct in range(3):
        factor = jnp.zeros((SUBS, LANES), F32)
        for i in range(min(SUBS, channels - ct * SUBS)):
            factor = jnp.where(sub == i, 0.5 * factor_ref[ct * SUBS + i], factor)
        factors.append(factor)

    def spread(ref, index, row):
        return jnp.broadcast_to(ref[index + (pl.ds(row, 1),)], (SUBS, LANES))

    def invert(q, colour, source, exists, wanted=(0, 1, 2)):
        row = (q + RING - 2) % RING
        for j in wanted:
            absorb = jnp.broadcast_to(source(colour, 2, j)[6:7], (SUBS, LANES))
            weight = spread(weight_ref, (colour, j), row)
            for ct in range(3):
                inverse = 1.0 / (absorb + factors[ct] * weight)
                keep = lane_limit[j]
                if exists is not None:
                    keep = exists if keep is None else keep & exists
                if keep is not None:
                    inverse = jnp.where(keep, inverse, 0.0)
                inverse_ref[colour, ct, q, j] = inverse

    def start_red(q, source, exists, wanted=(0, 1, 2)):
        invert(q, 0, source, exists, wanted)
        for j in wanted:
            for ct in range(3):
                value_ref[0, ct, q, j] = source(0, ct, j) * inverse_ref[0, ct, q, j]

    def update(q, colour, source, wanted=(0, 1, 2)):
        row = (q + RING - 2) % RING
        faces = [[spread(face_ref, (colour, i, j), row) for i in range(6)] for j in wanted]
        result = []
        for ct in range(3):
            others = [value_ref[1 - colour, ct, q, j] for j in tiles]
            beside = lane_neighbours(others, lane, wanted)
            results = []
            for j, face, near in zip(wanted, faces, beside):
                before, after = value_ref[1 - colour, ct, q - 1, j], value_ref[1 - colour, ct, q + 1, j]
                across = jnp.where(even, *((before, after) if colour == 0 else (after, before)))
                inflow = face[0] * others[j]
                for one, other in zip(face[1:], [across] + near):
                    inflow = inflow + one * other
                value = (source(colour, ct, j) + factors[ct] * inflow) * inverse_ref[colour, ct, q, j]
                results.append(value)
            result.append(results)
        return result

    def keep(q, colour, result):
        for ct in range(3):
            for j in tiles:
                value_ref[colour, ct, q, j] = result[ct][j]

    has_before, has_after = position > 0, jnp.logical_not(last_box)
    regions = [
        (2, 18, own_source, None),
        (18, 26, box_source, jnp.broadcast_to(has_after, (SUBS, LANES))),
    ]
    before_exists = jnp.broadcast_to(has_before, (SUBS, LANES))
    after_exists = regions[1][3]
    sides = [(1, 0, before_exists), (26, 27, after_exists)]

    for begin, end, source_of, exists in regions:
        def first_red(q, carry, source_of=source_of, exists=exists):
            start_red(q, source_of(q), exists)
            return carry

        lax.fori_loop(begin, end, first_red, 0)
    for near, far, exists in sides:
        start_red(near, edge_source(near), exists)

    for near, far, exists in sides:
        start_red(far, edge_source(far), exists, (0, 1))
        for ct in range(3):
            value_ref[0, ct, far, 2] = jnp.zeros((SUBS, LANES), F32)

    for near, far, exists in sides:
        invert(near, 1, edge_source(near), exists)
        keep(near, 1, update(near, 1, edge_source(near)))
    for begin, end, source_of, exists in regions:
        def first_black(q, carry, source_of=source_of, exists=exists):
            invert(q, 1, source_of(q), exists)
            keep(q, 1, update(q, 1, source_of(q)))
            return carry

        lax.fori_loop(begin, end, first_black, 0)

    for near, far, exists in sides:
        for ct in range(3):
            for j in tiles:
                value_ref[1, ct, far, j] = jnp.zeros((SUBS, LANES), F32)
        keep(near, 0, update(near, 0, edge_source(near)))
    for begin, end, source_of, exists in regions:
        def second_red(q, carry, source_of=source_of):
            keep(q, 0, update(q, 0, source_of(q)))
            return carry

        lax.fori_loop(begin, end, second_red, 0)

    box_count = lengths_ref[position]
    first_box = lax.fori_loop(0, position, lambda i, total: total + lengths_ref[i], jnp.int32(0))
    start = (first_box - position * OLD_DEV) * (BOX_X // 2)
    flat = placed_ref.reshape(2 * 3 * SUBS * rows, LANES)
    for begin, end, source_of, exists in regions:
        def second_black(q, carry, source_of=source_of):
            p = q - 2
            result = update(q, 1, source_of(q), (0, 1))
            for ct in range(3):
                for j in range(2):
                    red, black = value_ref[0, ct, q, j], result[ct][j]
                    row = (j * 3 + ct) * SUBS * rows + 2 * (p - start)
                    flat[pl.ds(row, SUBS, stride=rows)] = jnp.where(even, red, black)
                    flat[pl.ds(row + 1, SUBS, stride=rows)] = jnp.where(even, black, red)
            return carry

        lax.fori_loop(
            jnp.maximum(begin, start + 2),
            jnp.minimum(end, start + 2 + box_count * (BOX_X // 2)),
            second_black,
            0,
        )

    def clear_channel(c, carry):
        def clear_box(k, carry):
            for j in range(2):
                placed_ref[j, c, pl.ds(pl.multiple_of(k * BOX_X, BOX_X), BOX_X)] = jnp.zeros((BOX_X, LANES), F32)
            return carry

        return lax.fori_loop(box_count, MOST, clear_box, carry)

    lax.fori_loop(0, channels, clear_channel, 0)
    copies = []
    for j in range(2):
        copies.append(
            pltpu.make_async_copy(
                placed_ref.at[j, pl.ds(0, channels)], out_ref.at[:, :, pl.ds(j * LANES, LANES)], sems.at[j]
            )
        )
        copies[-1].start()
    for copy in copies:
        copy.wait()


def in_vmem(count):
    return [pl.BlockSpec(memory_space=pltpu.VMEM)] * count


def on_device(sources, absorption, conductance, diffusivity, run_lengths):
    channels, planes, cells = sources.shape
    boxes, groups = lax.axis_size("boxes"), lax.axis_size("grp")
    pairs = planes // 2
    real = lambda *shape: jax.ShapeDtypeStruct(shape + (SUBS, LANES), F32)
    vmem = lambda *shape: pltpu.VMEM(shape + (SUBS, LANES), F32)
    params = pltpu.CompilerParams(vmem_limit_bytes=VMEM_LIMIT)
    own, plane, first, second, box = pl.pallas_call(
        pack_rims,
        out_shape=(
            real(2, 3, pairs, 2),
            real(2, 2, 2),
            real(2 * pairs + 2),
            real(2 * pairs + 2),
            real(100),
        ),
        in_specs=[pl.BlockSpec(memory_space=pltpu.HBM)] * 3,
        out_specs=tuple(in_vmem(5)),
        scratch_shapes=[
            pltpu.VMEM((2, channels + 2, planes, LANES), F32),
            pltpu.SemaphoreType.DMA((2, 3)),
        ],
        compiler_params=params,
    )(sources, absorption, conductance)
    second = lax.ppermute(second, "grp", swap_pairs(groups, 1))
    first = lax.ppermute(first, "grp", swap_pairs(groups, 0))
    box = lax.ppermute(box, "boxes", [(i + 1, i) for i in range(boxes - 1)])
    rim, rim_plane, chip, far = pl.pallas_call(
        pack_faces,
        out_shape=(real(2, 3, pairs), real(2, 2), real(60), real(60)),
        in_specs=in_vmem(4),
        out_specs=tuple(in_vmem(4)),
        compiler_params=params,
    )(own, plane, first, second)
    chip = lax.ppermute(chip, "boxes", swap_pairs(boxes, 0))
    far = lax.ppermute(far, "boxes", swap_pairs(boxes, 1))
    smem = pl.BlockSpec(memory_space=pltpu.SMEM)
    return pl.pallas_call(
        smooth,
        out_shape=jax.ShapeDtypeStruct((channels, MOST * BOX_X, cells), F32),
        in_specs=[smem, smem] + in_vmem(7),
        out_specs=pl.BlockSpec(memory_space=pltpu.HBM),
        scratch_shapes=[
            pltpu.VMEM((2, 6, 3, RING, LANES), F32),
            pltpu.VMEM((2, 3, RING, LANES), F32),
            vmem(2, 3, 8),
            vmem(2, 3, 8),
            vmem(2, 3, 28, 3),
            vmem(2, 3, 28, 3),
            pltpu.VMEM((2, 3 * SUBS, MOST * BOX_X, LANES), F32),
            pltpu.SemaphoreType.DMA((2,)),
        ],
        compiler_params=params,
    )(run_lengths, diffusivity, own, plane, rim, rim_plane, box, chip, far)


def solution(mesh):
    return jax.shard_map(
        on_device,
        mesh=mesh,
        in_specs=(P(None, "boxes", "grp"), P("boxes", "grp"), P("boxes", "grp"), P(), P()),
        out_specs=P(None, "boxes", "grp"),
        check_vma=False,
    )
```

time: 182 us -> 43.4 us (0.24); the launches traced: 179 us -> 42.6 us
  local copies, waits for them, and re-layouts: 87 us -> 2.63 us
  starting transfers between devices: 52.5 us -> 11.4 us
  other arithmetic: 31.5 us -> 0 us
  Pallas kernels: 0 us -> 18.3 us
  waiting for transfers between devices: 5.6 us -> 10.2 us
  between operations: 2.67 us -> 0.07 us
    ppermute x17 -> x5, starting transfers between devices: 52.5 us -> 11.4 us  [the longest x1 4.6 us: on_device(): second = lax.ppermute(second, 'grp', swap_pairs(groups, 1))]
    slice x48 -> x0, local copies, waits for them, and re-layouts: 38.5 us -> none  [the longest x9 9.31 us: neighbours_of(): jnp.roll(field, -1, 2)]
    another operation x35 -> x0, local copies, waits for them, and re-layouts: 21.8 us -> none  [the longest x12 8.29 us: neighbours_of(): high_row.reshape(layers, row_count, plane_z)]
    select_n x6 -> x0, other arithmetic: 20.5 us -> none  [the longest x4 19.1 us: smooth_boxes(): solution = jnp.where(active & (parity == half_sweep % 2), update, solution)]
    pallas_call x0 -> x3, Pallas kernels: none -> 18.3 us  [the longest x1 12.8 us: on_device(): pl.pallas_call(smooth, out_shape=jax.ShapeDtypeStruct((channels, MOST * B...]
    unnamed x148 -> x10, local copies, waits for them, and re-layouts: 13.5 us -> 2.63 us
    broadcast_in_dim x6 -> x0, local copies, waits for them, and re-layouts: 5.6 us -> none  [the longest x4 4.04 us: neighbours_of(): x_upper = jnp.where(at_end, above_plane, x_next)]
    concatenate x12 -> x0, local copies, waits for them, and re-layouts: 4.59 us -> none  [the longest x4 1.17 us: exchange_faces(): jnp.concatenate([solution[:, :, plane_cells - plane_z:], conduct[:, :, pl...]
  transfers between devices with their start and end apart: 17 -> 5, of which waited for: 2 -> 3; matrix products, arithmetic and copies ran while one was open for 19% -> 0% of each run, Pallas kernels for 0% -> 7%
where the time goes in v2:
time: 43.4 us; the launch traced here: 42.6 us
  Pallas kernels  18.3 us (42%)
  starting transfers between devices  11.4 us (26%)
  waiting for transfers between devices  10.2 us (24%)
  local copies, waits for them, and re-layouts  2.63 us (6%)
    pallas_call x1, Pallas kernels, on_device(): pl.pallas_call(smooth, out_shape=jax.ShapeDtypeStruct((channels, MOST * B...  12.8 us
    ppermute x1, waiting for transfers between devices, on_device(): far = lax.ppermute(far, 'boxes', swap_pairs(boxes, 1))  6.99 us
    ppermute x1, starting transfers between devices, on_device(): second = lax.ppermute(second, 'grp', swap_pairs(groups, 1))  4.6 us
    ppermute x1, starting transfers between devices, on_device(): far = lax.ppermute(far, 'boxes', swap_pairs(boxes, 1))  3.43 us
    ppermute x1, waiting for transfers between devices, on_device(): second = lax.ppermute(second, 'grp', swap_pairs(groups, 1))  3.02 us
    pallas_call x1, Pallas kernels, on_device(): pl.pallas_call(pack_faces, out_shape=(real(2, 3, pairs), real(2, 2), real...  2.86 us
    ppermute x1, starting transfers between devices, on_device(): box = lax.ppermute(box, 'boxes', [(i + 1, i) for i in range(boxes - 1)])  2.78 us
    pallas_call x1, Pallas kernels, on_device(): pl.pallas_call(pack_rims, out_shape=(real(2, 3, pairs, 2), real(2, 2, 2),...  2.66 us
  transfers between devices with their start and end apart: 5, of which 3 were waited for; matrix products, arithmetic and copies ran while one was open for 0% of the time, Pallas kernels for 7%

profile of v2, /device:TPU:12, one launch (start us, length us, event | category | flops | bytes accessed | tf_op | source)
XLA Modules:
  0.0 42.6 jit_solution(15884996966718171301)
XLA Ops:
  0.0 0.0 copy-start
  0.0 1.1 %copy-done = f32[22,32,256]{2,1,0:T(8,128)S(1)} copy-done((f32[22,32,256]{2,1,0:T(8,128)S(1)}, f32[22,32,256]{2,1,0:T(8,128)}, u32[]{:S(2)}) %copy-start) | copy-done | bytes 720920
  1.1 0.0 copy-start.1
  1.1 0.8 %copy-done.1 = f32[32,256]{1,0:T(8,128)S(1)} copy-done((f32[32,256]{1,0:T(8,128)S(1)}, f32[32,256]{1,0:T(8,128)}, u32[]{:S(2)}) %copy-start.1) | copy-done | bytes 32792
  1.9 0.0 copy-start.2
  1.9 0.8 %copy-done.2 = f32[32,256]{1,0:T(8,128)S(1)} copy-done((f32[32,256]{1,0:T(8,128)S(1)}, f32[32,256]{1,0:T(8,128)}, u32[]{:S(2)}) %copy-start.2) | copy-done | bytes 32792
  2.6 0.0 copy-start.3
  2.6 0.0 copy-start.4
  2.6 2.7 %shard_map.55 = (f32[2,3,16,2,8,128]{5,4,3,2,1,0:T(8,128)S(1)}, f32[2,2,2,8,128]{4,3,2,1,0:T(8,128)S(1)}, f32[34,8,128]{2,1,0:T(8,128)S(1)}, f32[34,8,128]{2,1,0:T(8,128)S(1)}, f32[100,8,128]{2,1,0:T(8,128)S(1)}) custom-call(f32[22,32,256]{2,1,0:T(8,128)S(1)} %copy-done, f32[32,256]{1,0:T(8,128)S(1)} %copy-done.1, f32[32,256]{1,0:T(8,128)S(1)} %copy-done.2), custom_call_target="tpu_custom_call" | custom-call | tf_op jit(solution)/shard_map/pallas_call | solution.py:471
  5.3 2.8 %collective-permute-start.2 = (f32[100,8,128]{2,1,0:T(8,128)S(1)}, f32[100,8,128]{2,1,0:T(8,128)S(1)}, u32[]{:S(2)}, u32[]{:S(2)}) collective-permute-start(f32[100,8,128]{2,1,0:T(8,128)S(1)} %get-tuple-element.20), channel_id=1, source_target_pairs={{4,0},{8,4},{12,8},{16,12},{20,16},{24,20},{28,24},{5,1},{9,5},{13... | collective-permute-start | bytes 1228808 | tf_op jit(solution)/shard_map/ppermute | solution.py:490
  8.1 0.5 %collective-permute-start = (f32[34,8,128]{2,1,0:T(8,128)S(1)}, f32[34,8,128]{2,1,0:T(8,128)S(1)}, u32[]{:S(2)}, u32[]{:S(2)}) collective-permute-start(f32[34,8,128]{2,1,0:T(8,128)S(1)} %get-tuple-element.16), channel_id=1, source_target_pairs={{0,1},{2,3},{1,0},{3,2},{4,5},{6,7},{5,4},{7,6},{8,9},{10,11},{9,8... | collective-permute-start | bytes 417800 | tf_op jit(solution)/shard_map/ppermute | solution.py:489
  8.6 4.6 %collective-permute-start.1 = (f32[34,8,128]{2,1,0:T(8,128)S(1)}, f32[34,8,128]{2,1,0:T(8,128)S(1)}, u32[]{:S(2)}, u32[]{:S(2)}) collective-permute-start(f32[34,8,128]{2,1,0:T(8,128)S(1)} %get-tuple-element.17), channel_id=1, source_target_pairs={{1,2},{2,1},{5,6},{6,5},{9,10},{10,9},{13,14},{14,13},{17,18},{18,... | collective-permute-start | bytes 417800 | tf_op jit(solution)/shard_map/ppermute | solution.py:488
  13.2 0.2 collective-permute-done.first_ref
  13.4 3.0 %collective-permute-done.1.second_ref = f32[34,8,128]{2,1,0:T(8,128)S(1)} collective-permute-done((f32[34,8,128]{2,1,0:T(8,128)S(1)}, f32[34,8,128]{2,1,0:T(8,128)S(1)}, u32[]{:S(2)}, u32[]{:S(2)}) %collective-permute-start.1) | collective-permute-done | bytes 139296 | tf_op jit(solution)/shard_map/ppermute | solution.py:488
  16.4 2.9 %shard_map.56 = (f32[2,3,16,8,128]{4,3,2,1,0:T(8,128)S(1)}, f32[2,2,8,128]{3,2,1,0:T(8,128)S(1)}, f32[60,8,128]{2,1,0:T(8,128)S(1)}, f32[60,8,128]{2,1,0:T(8,128)S(1)}) custom-call(f32[2,3,16,2,8,128]{5,4,3,2,1,0:T(8,128)S(1)} %get-tuple-element.14.own_ref, f32[2,2,2,8,128]{4,3,2,1,0:T(8,128)S(1)} %get-tuple-element.15.plane_ref, ...), custom_call_target="tpu_custom_call" | custom-call | tf_op jit(solution)/shard_map/pallas_call | solution.py:491
  19.3 0.1 collective-permute-start.3
  19.3 3.4 %collective-permute-start.4 = (f32[60,8,128]{2,1,0:T(8,128)S(1)}, f32[60,8,128]{2,1,0:T(8,128)S(1)}, u32[]{:S(2)}, u32[]{:S(2)}) collective-permute-start(f32[60,8,128]{2,1,0:T(8,128)S(1)} %get-tuple-element.22), channel_id=1, source_target_pairs={{4,8},{12,16},{20,24},{8,4},{16,12},{24,20},{5,9},{13,17},{21,25},... | collective-permute-start | bytes 737288 | tf_op jit(solution)/shard_map/ppermute | solution.py:499
  22.8 0.0 collective-permute-done.3.chip_ref
  22.8 7.0 %collective-permute-done.4.far_ref = f32[60,8,128]{2,1,0:T(8,128)S(1)} collective-permute-done((f32[60,8,128]{2,1,0:T(8,128)S(1)}, f32[60,8,128]{2,1,0:T(8,128)S(1)}, u32[]{:S(2)}, u32[]{:S(2)}) %collective-permute-start.4) | collective-permute-done | bytes 245792 | tf_op jit(solution)/shard_map/ppermute | solution.py:499
  29.8 0.0 collective-permute-done.2.box_ref
  29.8 0.0 copy-done.3
  29.8 0.0 copy-done.4
  29.8 12.8 %shard_map.57 = f32[22,48,256]{2,1,0:T(8,128)} custom-call(s32[8]{0:T(128)S(1)} %copy-done.3, f32[22]{0:T(128)S(1)} %copy-done.4, f32[2,3,16,2,8,128]{5,4,3,2,1,0:T(8,128)S(1)} %get-tuple-element.14.own_ref, f32[2,2,2,8,128]{4,3,2,1,0:T(8,128)S(1)} %get-tuple-element.15.plane_ref, f32[2,3,16,8,128]{4,3,2,1,0:T(8,128)S(1)} %get-tuple-element.18.rim_ref, ...), custom_call_target="tpu_custom_call" | custom-call | tf_op jit(solution)/shard_map/pallas_call | solution.py:501
Async XLA Ops:
  0.0 1.1 %copy-start = (f32[22,32,256]{2,1,0:T(8,128)S(1)}, f32[22,32,256]{2,1,0:T(8,128)}, u32[]{:S(2)}) copy-start(f32[22,32,256]{2,1,0:T(8,128)} %src_ref.1) | copy-start | bytes 2162692
  1.1 0.8 %copy-start.1 = (f32[32,256]{1,0:T(8,128)S(1)}, f32[32,256]{1,0:T(8,128)}, u32[]{:S(2)}) copy-start(f32[32,256]{1,0:T(8,128)} %absorb_ref.1) | copy-start | bytes 98308
  1.9 0.8 %copy-start.2 = (f32[32,256]{1,0:T(8,128)S(1)}, f32[32,256]{1,0:T(8,128)}, u32[]{:S(2)}) copy-start(f32[32,256]{1,0:T(8,128)} %conduct_ref.1) | copy-start | bytes 98308
  2.6 27.2 %copy-start.3 = (s32[8]{0:T(128)S(1)}, s32[8]{0:T(128)}, u32[]{:S(2)}) copy-start(s32[8]{0:T(128)} %lengths_ref.1) | copy-start | bytes 100
  2.6 27.2 %copy-start.4 = (f32[22]{0:T(128)S(1)}, f32[22]{0:T(128)}, u32[]{:S(2)}) copy-start(f32[22]{0:T(128)} %factor_ref.1) | copy-start | bytes 268
  5.3 24.5 %collective-permute-start.2 = (f32[100,8,128]{2,1,0:T(8,128)S(1)}, f32[100,8,128]{2,1,0:T(8,128)S(1)}, u32[]{:S(2)}, u32[]{:S(2)}) collective-permute-start(f32[100,8,128]{2,1,0:T(8,128)S(1)} %get-tuple-element.20), channel_id=1, source_target_pairs={{4,0},{8,4},{12,8},{16,12},{20,16},{24,20},{28,24},{5,1},{9,5},{13... | collective-permute-start | bytes 1228808 | tf_op jit(solution)/shard_map/ppermute | solution.py:490
  8.1 5.3 %collective-permute-start = (f32[34,8,128]{2,1,0:T(8,128)S(1)}, f32[34,8,128]{2,1,0:T(8,128)S(1)}, u32[]{:S(2)}, u32[]{:S(2)}) collective-permute-start(f32[34,8,128]{2,1,0:T(8,128)S(1)} %get-tuple-element.16), channel_id=1, source_target_pairs={{0,1},{2,3},{1,0},{3,2},{4,5},{6,7},{5,4},{7,6},{8,9},{10,11},{9,8... | collective-permute-start | bytes 417800 | tf_op jit(solution)/shard_map/ppermute | solution.py:489
  8.6 7.8 %collective-permute-start.1 = (f32[34,8,128]{2,1,0:T(8,128)S(1)}, f32[34,8,128]{2,1,0:T(8,128)S(1)}, u32[]{:S(2)}, u32[]{:S(2)}) collective-permute-start(f32[34,8,128]{2,1,0:T(8,128)S(1)} %get-tuple-element.17), channel_id=1, source_target_pairs={{1,2},{2,1},{5,6},{6,5},{9,10},{10,9},{13,14},{14,13},{17,18},{18,... | collective-permute-start | bytes 417800 | tf_op jit(solution)/shard_map/ppermute | solution.py:488
  19.3 3.5 %collective-permute-start.3 = (f32[60,8,128]{2,1,0:T(8,128)S(1)}, f32[60,8,128]{2,1,0:T(8,128)S(1)}, u32[]{:S(2)}, u32[]{:S(2)}) collective-permute-start(f32[60,8,128]{2,1,0:T(8,128)S(1)} %get-tuple-element.21), channel_id=1, source_target_pairs={{0,4},{8,12},{16,20},{24,28},{4,0},{12,8},{20,16},{28,24},{1,5},{9... | collective-permute-start | bytes 737288 | tf_op jit(solution)/shard_map/ppermute | solution.py:498
  19.3 10.4 %collective-permute-start.4 = (f32[60,8,128]{2,1,0:T(8,128)S(1)}, f32[60,8,128]{2,1,0:T(8,128)S(1)}, u32[]{:S(2)}, u32[]{:S(2)}) collective-permute-start(f32[60,8,128]{2,1,0:T(8,128)S(1)} %get-tuple-element.22), channel_id=1, source_target_pairs={{4,8},{12,16},{20,24},{8,4},{16,12},{24,20},{5,9},{13,17},{21,25},... | collective-permute-start | bytes 737288 | tf_op jit(solution)/shard_map/ppermute | solution.py:499

commit v3 on v2

--- a/solution.py
+++ b/solution.py
@@ -62,35 +62,26 @@
 
 
 def pack_rims(
-    src_ref, absorb_ref, conduct_ref,
+    src_ref, plain_ref,
     own_ref, plane_ref, first_ref, second_ref, box_ref,
-    tiles_ref, sems,
+    tiles_ref,
 ):
     channels, planes, _ = src_ref.shape
     layers = channels + 2
     half = planes // 2
-    copies = []
-    for tile in range(2):
-        lanes = pl.ds(tile * LANES, LANES)
-        for i, (source, place, count) in enumerate(
-            [
-                (src_ref.at[:, :, lanes], 0, channels),
-                (absorb_ref.at[:, lanes], channels, None),
-                (conduct_ref.at[:, lanes], channels + 1, None),
-            ]
-        ):
-            into = tiles_ref.at[tile, place] if count is None else tiles_ref.at[tile, pl.ds(0, count)]
-            copies.append(pltpu.make_async_copy(source, into, sems.at[tile, i]))
-    for copy in copies:
-        copy.start()
-    for copy in copies:
-        copy.wait()
+    for layer in range(layers):
+        for j in range(2):
+            lanes = pl.ds(j * LANES, LANES)
+            if layer < channels:
+                tiles_ref[j, layer] = src_ref[layer, :, lanes]
+            else:
+                tiles_ref[j, layer] = plain_ref[layer - channels, :, lanes]
 
     lane, even = lane_places(SUBS)
     even_group = lax.axis_index("grp") % 2 == 0
     flat = tiles_ref.reshape(2 * layers * planes, LANES)
 
-    def step(p, carry):
+    for p in range(half):
         reds, blacks = [], []
         for j in range(2):
             red, black = [], []
@@ -102,6 +93,9 @@
                 black.append(jnp.where(even, high, low))
                 own_ref[0, ct, p, j] = red[ct]
                 own_ref[1, ct, p, j] = black[ct]
+                if p < 8:
+                    box_ref[(ct * 8 + p) * 2 + j] = red[ct]
+                    box_ref[((3 + ct) * 8 + p) * 2 + j] = black[ct]
             reds.append(red)
             blacks.append(black)
         low_rim = pack_rim(reds[0], blacks[0], lane)
@@ -109,9 +103,6 @@
         for i in range(2):
             first_ref[2 * p + i] = jnp.where(even_group, high_rim[i], low_rim[i])
             second_ref[2 * p + i] = jnp.where(even_group, low_rim[i], high_rim[i])
-        return carry
-
-    lax.fori_loop(0, half, step, 0)
 
     for q in range(2):
         compact = []
@@ -129,15 +120,6 @@
         first_ref[2 * half + q] = jnp.where(even_group, high_rim, low_rim)
         second_ref[2 * half + q] = jnp.where(even_group, low_rim, high_rim)
 
-    def copy_box(p, carry):
-        for colour in range(2):
-            for ct in range(3):
-                for j in range(2):
-                    box_ref[((colour * 3 + ct) * 8 + p) * 2 + j] = own_ref[colour, ct, p, j]
-        return carry
-
-    lax.fori_loop(0, 8, copy_box, 0)
-
 
 def pack_faces(own_ref, plane_ref, first_ref, second_ref, rim_ref, rim_plane_ref, chip_ref, far_ref):
     pairs = own_ref.shape[2]
@@ -150,7 +132,7 @@
         first, second = first_ref[i], second_ref[i]
         return jnp.where(even_group, first, second), jnp.where(even_group, second, first)
 
-    def step(p, carry):
+    for p in range(pairs):
         above, below = zip(*[sides(2 * p + i) for i in range(2)])
         above, below = unpack_rim(*above, lane), unpack_rim(*below, lane)
         reds, blacks = [], []
@@ -159,21 +141,10 @@
             blacks.append(jnp.where(low_half, above[1][ct], roll(below[1][ct], -32)))
             rim_ref[0, ct, p] = reds[ct]
             rim_ref[1, ct, p] = blacks[ct]
-        return reds, blacks
-
-    def with_halo(p, carry):
-        reds, blacks = step(p, carry)
-        for i, part in enumerate(pack_halo(reds, blacks, lane)):
-            chip_ref[4 * p + i] = part
-            far_ref[4 * p + i] = part
-        return carry
-
-    def without_halo(p, carry):
-        step(p, carry)
-        return carry
-
-    lax.fori_loop(0, 8, with_halo, 0)
-    lax.fori_loop(8, pairs, without_halo, 0)
+        if p < 8:
+            for i, part in enumerate(pack_halo(reds, blacks, lane)):
+                chip_ref[4 * p + i] = part
+                far_ref[4 * p + i] = part
     for q in range(2):
         above, below = sides(2 * pairs + q)
         rim_plane_ref[0, q] = jnp.where(low_half, above, roll(below, RIM))
@@ -211,6 +182,16 @@
 EDGE = [(0, 1, 0), (0, 1, 1), (0, 1, 2), (0, 0, 0), (0, 0, 1), (1, 1, 0), (1, 1, 1), (1, 1, 2)]
 
 
+def shift_matrices():
+    row = lax.broadcasted_iota(jnp.int32, (2 * LANES, LANES), 0) % LANES
+    col = lax.broadcasted_iota(jnp.int32, (2 * LANES, LANES), 1)
+    z = col % PLANE_Z
+    pick = lambda source: jnp.where(row == source, 1.0, 0.0)
+    along_z = [pick(col - z + (z + step) % PLANE_Z) for step in (1, PLANE_Z - 1)]
+    along_y = [pick((col + step) % LANES) for step in (PLANE_Z, LANES - PLANE_Z)]
+    return [jnp.concatenate(pair, 1).astype(jnp.bfloat16) for pair in (along_z, along_y)]
+
+
 def z_up(x, z):
     return jnp.where(z == PLANE_Z - 1, roll(x, PLANE_Z - 1), roll(x, -1))
 
@@ -237,7 +218,7 @@
 def smooth(
     lengths_ref, factor_ref, own_ref, plane_ref, rim_ref, rim_plane_ref, box_ref, chip_ref, far_ref,
     out_ref,
-    face_ref, weight_ref, box_rim_ref, edge_ref, inverse_ref, value_ref, placed_ref, sems,
+    face_ref, weight_ref, box_rim_ref, edge_ref, inverse_ref, value_ref, placed_ref, shift_ref, sems,
 ):
     channels, rows, _ = out_ref.shape
     position = lax.axis_index("boxes")
@@ -281,13 +262,10 @@
                 total = total + face
             weight_ref[colour, j] = total
 
-    def open_box(p, carry):
+    for p in range(8):
         reds, blacks = unpack_halo([from_after(4 * p + i) for i in range(4)], lane)
         for ct in range(3):
             box_rim_ref[0, ct, p], box_rim_ref[1, ct, p] = reds[ct], blacks[ct]
-        return carry
-
-    lax.fori_loop(0, 8, open_box, 0)
     for ct in range(3):
         for i in range(8):
             edge_ref[0, ct, i] = from_before(32 + ct * 8 + i)
@@ -343,118 +321,110 @@
             for ct in range(3):
                 value_ref[0, ct, q, j] = source(0, ct, j) * inverse_ref[0, ct, q, j]
 
-    def update(q, colour, source, wanted=(0, 1, 2)):
-        row = (q + RING - 2) % RING
-        faces = [[spread(face_ref, (colour, i, j), row) for i in range(6)] for j in wanted]
-        result = []
+    for i, matrix in enumerate(shift_matrices()):
+        shift_ref[i] = matrix
+
+    def shifted(places, colour):
+        index = [(ct, q, j) for q in places for ct in range(3) for j in tiles]
+        x = jnp.concatenate([value_ref[colour, ct, q, j] for ct, q, j in index], 0)
+        high = x.astype(jnp.bfloat16)
+        both = jnp.concatenate([high, (x - high.astype(F32)).astype(jnp.bfloat16)], 1)
+        moved = [jnp.dot(both, shift_ref[i], preferred_element_type=F32) for i in range(2)]
+        result = {}
+        for k, key in enumerate(index):
+            rows = slice(k * SUBS, (k + 1) * SUBS)
+            result[key] = [m[rows, i * LANES : (i + 1) * LANES] for m in moved for i in range(2)]
+        return result
+
+    def update(places, colour, wanted=(0, 1, 2)):
+        moved = shifted(places, 1 - colour)
+        for q in places:
+            row = (q + RING - 2) % RING
+            source = source_of(q)
+            faces = [[spread(face_ref, (colour, i, j), row) for i in range(6)] for j in wanted]
+            for ct in range(3):
+                near = [moved[ct, q, j] for j in tiles]
+                for j, face in zip(wanted, faces):
+                    same = value_ref[1 - colour, ct, q, j]
+                    before, after = value_ref[1 - colour, ct, q - 1, j], value_ref[1 - colour, ct, q + 1, j]
+                    across = jnp.where(even, *((before, after) if colour == 0 else (after, before)))
+                    up = jnp.where(lane < LANES - PLANE_Z, near[j][2], near[(j + 1) % 3][2])
+                    down = jnp.where(lane < PLANE_Z, near[(j + 2) % 3][3], near[j][3])
+                    inflow = face[0] * same
+                    for one, other in zip(face[1:], [across, near[j][0], near[j][1], up, down]):
+                        inflow = inflow + one * other
+                    value = (source(colour, ct, j) + factors[ct] * inflow) * inverse_ref[colour, ct, q, j]
+                    value_ref[colour, ct, q, j] = value
+
+    after_exists = jnp.broadcast_to(jnp.logical_not(last_box), (SUBS, LANES))
+    before_exists = jnp.broadcast_to(position > 0, (SUBS, LANES))
+
+    def source_of(q):
+        return own_source(q) if 2 <= q < 18 else box_source(q) if 18 <= q < 26 else edge_source(q)
+
+    def exists(q):
+        return before_exists if q < 2 else None if q < 18 else after_exists
+
+    for q in range(28):
+        start_red(q, source_of(q), exists(q), (0, 1) if q in (0, 27) else (0, 1, 2))
+    zero = jnp.zeros((SUBS, LANES), F32)
+    for q in (0, 27):
         for ct in range(3):
-            others = [value_ref[1 - colour, ct, q, j] for j in tiles]
-            beside = lane_neighbours(others, lane, wanted)
-            results = []
-            for j, face, near in zip(wanted, faces, beside):
-                before, after = value_ref[1 - colour, ct, q - 1, j], value_ref[1 - colour, ct, q + 1, j]
-                across = jnp.where(even, *((before, after) if colour == 0 else (after, before)))
-                inflow = face[0] * others[j]
-                for one, other in zip(face[1:], [across] + near):
-                    inflow = inflow + one * other
-                value = (source(colour, ct, j) + factors[ct] * inflow) * inverse_ref[colour, ct, q, j]
-                results.append(value)
-            result.append(results)
-        return result
-
-    def keep(q, colour, result):
-        for ct in range(3):
+            value_ref[0, ct, q, 2] = zero
             for j in tiles:
-                value_ref[colour, ct, q, j] = result[ct][j]
-
-    has_before, has_after = position > 0, jnp.logical_not(last_box)
-    regions = [
-        (2, 18, own_source, None),
-        (18, 26, box_source, jnp.broadcast_to(has_after, (SUBS, LANES))),
-    ]
-    before_exists = jnp.broadcast_to(has_before, (SUBS, LANES))
-    after_exists = regions[1][3]
-    sides = [(1, 0, before_exists), (26, 27, after_exists)]
-
-    for begin, end, source_of, exists in regions:
-        def first_red(q, carry, source_of=source_of, exists=exists):
-            start_red(q, source_of(q), exists)
-            return carry
-
-        lax.fori_loop(begin, end, first_red, 0)
-    for near, far, exists in sides:
-        start_red(near, edge_source(near), exists)
-
-    for near, far, exists in sides:
-        start_red(far, edge_source(far), exists, (0, 1))
-        for ct in range(3):
-            value_ref[0, ct, far, 2] = jnp.zeros((SUBS, LANES), F32)
-
-    for near, far, exists in sides:
-        invert(near, 1, edge_source(near), exists)
-        keep(near, 1, update(near, 1, edge_source(near)))
-    for begin, end, source_of, exists in regions:
-        def first_black(q, carry, source_of=source_of, exists=exists):
-            invert(q, 1, source_of(q), exists)
-            keep(q, 1, update(q, 1, source_of(q)))
-            return carry
-
-        lax.fori_loop(begin, end, first_black, 0)
-
-    for near, far, exists in sides:
-        for ct in range(3):
-            for j in tiles:
-                value_ref[1, ct, far, j] = jnp.zeros((SUBS, LANES), F32)
-        keep(near, 0, update(near, 0, edge_source(near)))
-    for begin, end, source_of, exists in regions:
-        def second_red(q, carry, source_of=source_of):
-            keep(q, 0, update(q, 0, source_of(q)))
-            return carry
-
-        lax.fori_loop(begin, end, second_red, 0)
+                value_ref[1, ct, q, j] = zero
+
+    blocks = [range(1, 11), range(11, 19), range(19, 27)]
+    for places in blocks:
+        for q in places:
+            invert(q, 1, source_of(q), exists(q))
+        update(places, 1)
+    for places in blocks:
+        update(places, 0)
 
     box_count = lengths_ref[position]
     first_box = lax.fori_loop(0, position, lambda i, total: total + lengths_ref[i], jnp.int32(0))
-    start = (first_box - position * OLD_DEV) * (BOX_X // 2)
+    start = first_box - position * OLD_DEV
+
+    def send(k):
+        rows = pl.ds(pl.multiple_of(k * BOX_X, BOX_X), BOX_X)
+        return [
+            pltpu.make_async_copy(
+                placed_ref.at[j, pl.ds(0, channels), rows],
+                out_ref.at[:, rows, pl.ds(j * LANES, LANES)],
+                sems.at[k, j],
+            )
+            for j in range(2)
+        ]
+
     flat = placed_ref.reshape(2 * 3 * SUBS * rows, LANES)
-    for begin, end, source_of, exists in regions:
-        def second_black(q, carry, source_of=source_of):
-            p = q - 2
-            result = update(q, 1, source_of(q), (0, 1))
-            for ct in range(3):
-                for j in range(2):
-                    red, black = value_ref[0, ct, q, j], result[ct][j]
-                    row = (j * 3 + ct) * SUBS * rows + 2 * (p - start)
-                    flat[pl.ds(row, SUBS, stride=rows)] = jnp.where(even, red, black)
-                    flat[pl.ds(row + 1, SUBS, stride=rows)] = jnp.where(even, black, red)
-            return carry
-
-        lax.fori_loop(
-            jnp.maximum(begin, start + 2),
-            jnp.minimum(end, start + 2 + box_count * (BOX_X // 2)),
-            second_black,
-            0,
-        )
-
-    def clear_channel(c, carry):
-        def clear_box(k, carry):
+    for box in range(MOST):
+        @pl.when((box >= start) & (box < start + box_count))
+        def _():
+            places = range(2 + box * 8, 10 + box * 8)
+            update(places, 1, (0, 1))
+            for q in places:
+                for ct in range(3):
+                    for j in range(2):
+                        red, black = value_ref[0, ct, q, j], value_ref[1, ct, q, j]
+                        row = (j * 3 + ct) * SUBS * rows + 2 * (q - 2 - 8 * start)
+                        flat[pl.ds(row, SUBS, stride=rows)] = jnp.where(even, red, black)
+                        flat[pl.ds(row + 1, SUBS, stride=rows)] = jnp.where(even, black, red)
+            for copy in send(box - start):
+                copy.start()
+
+    for k in range(1, MOST):
+        @pl.when(k >= box_count)
+        def _():
             for j in range(2):
-                placed_ref[j, c, pl.ds(pl.multiple_of(k * BOX_X, BOX_X), BOX_X)] = jnp.zeros((BOX_X, LANES), F32)
-            return carry
-
-        return lax.fori_loop(box_count, MOST, clear_box, carry)
-
-    lax.fori_loop(0, channels, clear_channel, 0)
-    copies = []
-    for j in range(2):
-        copies.append(
-            pltpu.make_async_copy(
-                placed_ref.at[j, pl.ds(0, channels)], out_ref.at[:, :, pl.ds(j * LANES, LANES)], sems.at[j]
-            )
-        )
-        copies[-1].start()
-    for copy in copies:
-        copy.wait()
+                for c in range(channels):
+                    placed_ref[j, c, k * BOX_X : (k + 1) * BOX_X] = jnp.zeros((BOX_X, LANES), F32)
+            for copy in send(k):
+                copy.start()
+
+    for k in range(MOST):
+        for copy in send(k):
+            copy.wait()
 
 
 def in_vmem(count):
@@ -477,14 +447,11 @@
             real(2 * pairs + 2),
             real(100),
         ),
-        in_specs=[pl.BlockSpec(memory_space=pltpu.HBM)] * 3,
+        in_specs=in_vmem(2),
         out_specs=tuple(in_vmem(5)),
-        scratch_shapes=[
-            pltpu.VMEM((2, channels + 2, planes, LANES), F32),
-            pltpu.SemaphoreType.DMA((2, 3)),
-        ],
+        scratch_shapes=[pltpu.VMEM((2, channels + 2, planes, LANES), F32)],
         compiler_params=params,
-    )(sources, absorption, conductance)
+    )(sources, jnp.stack([absorption, conductance]))
     second = lax.ppermute(second, "grp", swap_pairs(groups, 1))
     first = lax.ppermute(first, "grp", swap_pairs(groups, 0))
     box = lax.ppermute(box, "boxes", [(i + 1, i) for i in range(boxes - 1)])
@@ -511,7 +478,8 @@
             vmem(2, 3, 28, 3),
             vmem(2, 3, 28, 3),
             pltpu.VMEM((2, 3 * SUBS, MOST * BOX_X, LANES), F32),
-            pltpu.SemaphoreType.DMA((2,)),
+            pltpu.VMEM((2, 2 * LANES, 2 * LANES), jnp.bfloat16),
+            pltpu.SemaphoreType.DMA((MOST, 2)),
         ],
         compiler_params=params,
     )(run_lengths, diffusivity, own, plane, rim, rim_plane, box, chip, far)

time: 43.4 us -> 31.1 us (0.72)
  the two profiles are of different devices: /device:TPU:12 before, /device:TPU:19 now
where the time goes in v3:
time: 31.1 us; the launch traced here: 30.7 us
  waiting for transfers between devices  12.2 us (39%)
  starting transfers between devices  10.2 us (33%)
  Pallas kernels  6.36 us (20%)
  local copies, waits for them, and re-layouts  1.12 us (4%)
  other arithmetic  0.81 us (3%)
    ppermute x1, waiting for transfers between devices, on_device(): far = lax.ppermute(far, 'boxes', swap_pairs(boxes, 1))  7.29 us
    pallas_call x1, Pallas kernels, on_device(): pl.pallas_call(smooth, out_shape=jax.ShapeDtypeStruct((channels, MOST * B...  4.6 us
    ppermute x1, starting transfers between devices, on_device(): far = lax.ppermute(far, 'boxes', swap_pairs(boxes, 1))  3.14 us
    ppermute x1, waiting for transfers between devices, on_device(): second = lax.ppermute(second, 'grp', swap_pairs(groups, 1))  2.86 us
    ppermute x1, starting transfers between devices, on_device(): box = lax.ppermute(box, 'boxes', [(i + 1, i) for i in range(boxes - 1)])  2.58 us
    ppermute x1, waiting for transfers between devices, on_device(): first = lax.ppermute(first, 'grp', swap_pairs(groups, 0))  2.08 us
    ppermute x1, starting transfers between devices, on_device(): second = lax.ppermute(second, 'grp', swap_pairs(groups, 1))  1.91 us
    ppermute x1, starting transfers between devices, on_device(): first = lax.ppermute(first, 'grp', swap_pairs(groups, 0))  1.36 us
  transfers between devices with their start and end apart: 5, of which 3 were waited for; matrix products, arithmetic and copies ran while one was open for 0% of the time, Pallas kernels for 2%

profile of v3, /device:TPU:19, one launch (start us, length us, event | category | flops | bytes accessed | tf_op | source)
XLA Modules:
  0.0 30.7 jit_solution(12783939118572341419)
XLA Ops:
  0.0 0.0 copy-start.1
  0.0 0.0 copy-start.2
  0.0 0.8 %pad_maximum_fusion.plain_ref = f32[2,32,256]{2,1,0:T(8,128)S(1)} fusion(f32[1,32,256]{2,1,0:T(8,128)} %bitcast.2, f32[1,32,256]{2,1,0:T(8,128)} %bitcast.3), kind=kLoop, calls=%fused_computation | loop fusion | flops 16384 | bytes 131072 | tf_op jit(solution)/shard_map/stack | solution.py:454
  0.8 0.0 copy-start
  0.8 1.1 %copy-done = f32[22,32,256]{2,1,0:T(8,128)S(1)} copy-done((f32[22,32,256]{2,1,0:T(8,128)S(1)}, f32[22,32,256]{2,1,0:T(8,128)}, u32[]{:S(2)}) %copy-start) | copy-done | bytes 720920
  1.9 1.0 %shard_map.55 = (f32[2,3,16,2,8,128]{5,4,3,2,1,0:T(8,128)S(1)}, f32[2,2,2,8,128]{4,3,2,1,0:T(8,128)S(1)}, f32[34,8,128]{2,1,0:T(8,128)S(1)}, f32[34,8,128]{2,1,0:T(8,128)S(1)}, f32[100,8,128]{2,1,0:T(8,128)S(1)}) custom-call(f32[22,32,256]{2,1,0:T(8,128)S(1)} %copy-done, f32[2,32,256]{2,1,0:T(8,128)S(1)} %pad_maximum_fusion.plain_ref), custom_call_target="tpu_custom_call" | custom-call | tf_op jit(solution)/shard_map/pallas_call | solution.py:441
  2.9 2.6 %collective-permute-start.2 = (f32[100,8,128]{2,1,0:T(8,128)S(1)}, f32[100,8,128]{2,1,0:T(8,128)S(1)}, u32[]{:S(2)}, u32[]{:S(2)}) collective-permute-start(f32[100,8,128]{2,1,0:T(8,128)S(1)} %get-tuple-element.20), channel_id=1, source_target_pairs={{4,0},{8,4},{12,8},{16,12},{20,16},{24,20},{28,24},{5,1},{9,5},{13... | collective-permute-start | bytes 1228808 | tf_op jit(solution)/shard_map/ppermute | solution.py:457
  5.5 1.4 %collective-permute-start = (f32[34,8,128]{2,1,0:T(8,128)S(1)}, f32[34,8,128]{2,1,0:T(8,128)S(1)}, u32[]{:S(2)}, u32[]{:S(2)}) collective-permute-start(f32[34,8,128]{2,1,0:T(8,128)S(1)} %get-tuple-element.16), channel_id=1, source_target_pairs={{0,1},{2,3},{1,0},{3,2},{4,5},{6,7},{5,4},{7,6},{8,9},{10,11},{9,8... | collective-permute-start | bytes 417800 | tf_op jit(solution)/shard_map/ppermute | solution.py:456
  6.9 1.9 %collective-permute-start.1 = (f32[34,8,128]{2,1,0:T(8,128)S(1)}, f32[34,8,128]{2,1,0:T(8,128)S(1)}, u32[]{:S(2)}, u32[]{:S(2)}) collective-permute-start(f32[34,8,128]{2,1,0:T(8,128)S(1)} %get-tuple-element.17), channel_id=1, source_target_pairs={{1,2},{2,1},{5,6},{6,5},{9,10},{10,9},{13,14},{14,13},{17,18},{18,... | collective-permute-start | bytes 417800 | tf_op jit(solution)/shard_map/ppermute | solution.py:455
  8.8 2.1 %collective-permute-done.first_ref = f32[34,8,128]{2,1,0:T(8,128)S(1)} collective-permute-done((f32[34,8,128]{2,1,0:T(8,128)S(1)}, f32[34,8,128]{2,1,0:T(8,128)S(1)}, u32[]{:S(2)}, u32[]{:S(2)}) %collective-permute-start) | collective-permute-done | bytes 139296 | tf_op jit(solution)/shard_map/ppermute | solution.py:456
  10.9 2.9 %collective-permute-done.1.second_ref = f32[34,8,128]{2,1,0:T(8,128)S(1)} collective-permute-done((f32[34,8,128]{2,1,0:T(8,128)S(1)}, f32[34,8,128]{2,1,0:T(8,128)S(1)}, u32[]{:S(2)}, u32[]{:S(2)}) %collective-permute-start.1) | collective-permute-done | bytes 139296 | tf_op jit(solution)/shard_map/ppermute | solution.py:455
  13.8 0.7 %shard_map.56 = (f32[2,3,16,8,128]{4,3,2,1,0:T(8,128)S(1)}, f32[2,2,8,128]{3,2,1,0:T(8,128)S(1)}, f32[60,8,128]{2,1,0:T(8,128)S(1)}, f32[60,8,128]{2,1,0:T(8,128)S(1)}) custom-call(f32[2,3,16,2,8,128]{5,4,3,2,1,0:T(8,128)S(1)} %get-tuple-element.14.own_ref, f32[2,2,2,8,128]{4,3,2,1,0:T(8,128)S(1)} %get-tuple-element.15.plane_ref, ...), custom_call_target="tpu_custom_call" | custom-call | tf_op jit(solution)/shard_map/pallas_call | solution.py:458
  14.5 1.2 %collective-permute-start.3 = (f32[60,8,128]{2,1,0:T(8,128)S(1)}, f32[60,8,128]{2,1,0:T(8,128)S(1)}, u32[]{:S(2)}, u32[]{:S(2)}) collective-permute-start(f32[60,8,128]{2,1,0:T(8,128)S(1)} %get-tuple-element.21), channel_id=1, source_target_pairs={{0,4},{8,12},{16,20},{24,28},{4,0},{12,8},{20,16},{28,24},{1,5},{9... | collective-permute-start | bytes 737288 | tf_op jit(solution)/shard_map/ppermute | solution.py:465
  15.7 3.1 %collective-permute-start.4 = (f32[60,8,128]{2,1,0:T(8,128)S(1)}, f32[60,8,128]{2,1,0:T(8,128)S(1)}, u32[]{:S(2)}, u32[]{:S(2)}) collective-permute-start(f32[60,8,128]{2,1,0:T(8,128)S(1)} %get-tuple-element.22), channel_id=1, source_target_pairs={{4,8},{12,16},{20,24},{8,4},{16,12},{24,20},{5,9},{13,17},{21,25},... | collective-permute-start | bytes 737288 | tf_op jit(solution)/shard_map/ppermute | solution.py:466
  18.8 0.0 collective-permute-done.3.chip_ref
  18.8 7.3 %collective-permute-done.4.far_ref = f32[60,8,128]{2,1,0:T(8,128)S(1)} collective-permute-done((f32[60,8,128]{2,1,0:T(8,128)S(1)}, f32[60,8,128]{2,1,0:T(8,128)S(1)}, u32[]{:S(2)}, u32[]{:S(2)}) %collective-permute-start.4) | collective-permute-done | bytes 245792 | tf_op jit(solution)/shard_map/ppermute | solution.py:466
  26.1 0.0 collective-permute-done.2.box_ref
  26.1 0.0 copy-done.1
  26.1 0.0 copy-done.2
  26.1 4.6 %shard_map.57 = f32[22,48,256]{2,1,0:T(8,128)} custom-call(s32[8]{0:T(128)S(1)} %copy-done.1, f32[22]{0:T(128)S(1)} %copy-done.2, f32[2,3,16,2,8,128]{5,4,3,2,1,0:T(8,128)S(1)} %get-tuple-element.14.own_ref, f32[2,2,2,8,128]{4,3,2,1,0:T(8,128)S(1)} %get-tuple-element.15.plane_ref, f32[2,3,16,8,128]{4,3,2,1,0:T(8,128)S(1)} %get-tuple-element.18.rim_ref, ...), custom_call_target="tpu_custom_call" | custom-call | tf_op jit(solution)/shard_map/pallas_call | solution.py:468
Async XLA Ops:
  0.0 26.1 %copy-start.1 = (s32[8]{0:T(128)S(1)}, s32[8]{0:T(128)}, u32[]{:S(2)}) copy-start(s32[8]{0:T(128)} %lengths_ref.1) | copy-start | bytes 100
  0.0 26.1 %copy-start.2 = (f32[22]{0:T(128)S(1)}, f32[22]{0:T(128)}, u32[]{:S(2)}) copy-start(f32[22]{0:T(128)} %factor_ref.1) | copy-start | bytes 268
  0.8 1.1 %copy-start = (f32[22,32,256]{2,1,0:T(8,128)S(1)}, f32[22,32,256]{2,1,0:T(8,128)}, u32[]{:S(2)}) copy-start(f32[22,32,256]{2,1,0:T(8,128)} %src_ref.1) | copy-start | bytes 2162692
  2.9 23.2 %collective-permute-start.2 = (f32[100,8,128]{2,1,0:T(8,128)S(1)}, f32[100,8,128]{2,1,0:T(8,128)S(1)}, u32[]{:S(2)}, u32[]{:S(2)}) collective-permute-start(f32[100,8,128]{2,1,0:T(8,128)S(1)} %get-tuple-element.20), channel_id=1, source_target_pairs={{4,0},{8,4},{12,8},{16,12},{20,16},{24,20},{28,24},{5,1},{9,5},{13... | collective-permute-start | bytes 1228808 | tf_op jit(solution)/shard_map/ppermute | solution.py:457
  5.5 5.4 %collective-permute-start = (f32[34,8,128]{2,1,0:T(8,128)S(1)}, f32[34,8,128]{2,1,0:T(8,128)S(1)}, u32[]{:S(2)}, u32[]{:S(2)}) collective-permute-start(f32[34,8,128]{2,1,0:T(8,128)S(1)} %get-tuple-element.16), channel_id=1, source_target_pairs={{0,1},{2,3},{1,0},{3,2},{4,5},{6,7},{5,4},{7,6},{8,9},{10,11},{9,8... | collective-permute-start | bytes 417800 | tf_op jit(solution)/shard_map/ppermute | solution.py:456
  6.9 6.9 %collective-permute-start.1 = (f32[34,8,128]{2,1,0:T(8,128)S(1)}, f32[34,8,128]{2,1,0:T(8,128)S(1)}, u32[]{:S(2)}, u32[]{:S(2)}) collective-permute-start(f32[34,8,128]{2,1,0:T(8,128)S(1)} %get-tuple-element.17), channel_id=1, source_target_pairs={{1,2},{2,1},{5,6},{6,5},{9,10},{10,9},{13,14},{14,13},{17,18},{18,... | collective-permute-start | bytes 417800 | tf_op jit(solution)/shard_map/ppermute | solution.py:455
  14.5 4.3 %collective-permute-start.3 = (f32[60,8,128]{2,1,0:T(8,128)S(1)}, f32[60,8,128]{2,1,0:T(8,128)S(1)}, u32[]{:S(2)}, u32[]{:S(2)}) collective-permute-start(f32[60,8,128]{2,1,0:T(8,128)S(1)} %get-tuple-element.21), channel_id=1, source_target_pairs={{0,4},{8,12},{16,20},{24,28},{4,0},{12,8},{20,16},{28,24},{1,5},{9... | collective-permute-start | bytes 737288 | tf_op jit(solution)/shard_map/ppermute | solution.py:465
  15.7 10.4 %collective-permute-start.4 = (f32[60,8,128]{2,1,0:T(8,128)S(1)}, f32[60,8,128]{2,1,0:T(8,128)S(1)}, u32[]{:S(2)}, u32[]{:S(2)}) collective-permute-start(f32[60,8,128]{2,1,0:T(8,128)S(1)} %get-tuple-element.22), channel_id=1, source_target_pairs={{4,8},{12,16},{20,24},{8,4},{16,12},{24,20},{5,9},{13,17},{21,25},... | collective-permute-start | bytes 737288 | tf_op jit(solution)/shard_map/ppermute | solution.py:466

commit v4 on v3

--- a/solution.py
+++ b/solution.py
@@ -62,20 +62,17 @@
 
 
 def pack_rims(
-    src_ref, plain_ref,
+    src_ref,
     own_ref, plane_ref, first_ref, second_ref, box_ref,
     tiles_ref,
 ):
-    channels, planes, _ = src_ref.shape
-    layers = channels + 2
+    layers, planes, _ = src_ref.shape
+    channels = layers - 2
     half = planes // 2
     for layer in range(layers):
         for j in range(2):
             lanes = pl.ds(j * LANES, LANES)
-            if layer < channels:
-                tiles_ref[j, layer] = src_ref[layer, :, lanes]
-            else:
-                tiles_ref[j, layer] = plain_ref[layer - channels, :, lanes]
+            tiles_ref[j, layer] = src_ref[layer, :, lanes]
 
     lane, even = lane_places(SUBS)
     even_group = lax.axis_index("grp") % 2 == 0
@@ -113,15 +110,13 @@
             compact.append((jnp.where(even, low, high), jnp.where(even, high, low)))
             for colour in range(2):
                 plane_ref[colour, j, q] = compact[j][colour]
-                if q == 0:
-                    box_ref[96 + 2 * colour + j] = compact[j][colour]
         low_rim = jnp.where(lane < RIM, compact[0][0], roll(compact[0][1], RIM))
         high_rim = jnp.where(lane < RIM, roll(compact[1][0], RIM), compact[1][1])
         first_ref[2 * half + q] = jnp.where(even_group, high_rim, low_rim)
         second_ref[2 * half + q] = jnp.where(even_group, low_rim, high_rim)
 
 
-def pack_faces(own_ref, plane_ref, first_ref, second_ref, rim_ref, rim_plane_ref, chip_ref, far_ref):
+def pack_faces(own_ref, plane_ref, second_ref, first_ref, rim_ref, rim_plane_ref, chip_ref, far_ref):
     pairs = own_ref.shape[2]
     lane, _ = lane_places(SUBS)
     low_half = lane < RIM
@@ -216,7 +211,7 @@
 
 
 def smooth(
-    lengths_ref, factor_ref, own_ref, plane_ref, rim_ref, rim_plane_ref, box_ref, chip_ref, far_ref,
+    lengths_ref, factor_ref, own_ref, plane_ref, rim_ref, rim_plane_ref, box_ref, far_ref, chip_ref,
     out_ref,
     face_ref, weight_ref, box_rim_ref, edge_ref, inverse_ref, value_ref, placed_ref, shift_ref, sems,
 ):
@@ -236,12 +231,13 @@
         return jnp.where(even_box, far_ref[i], chip_ref[i])
 
     edges = [[jnp.concatenate([get(58), get(59)], 0) for get in (from_after, from_before)]][0]
+    flat_box = box_ref.reshape(96 * SUBS, LANES)
     conduct = []
     for colour in range(2):
         planes = []
         for j in tiles:
             own = [plane_ref[colour, j, q] if j < 2 else rim_plane_ref[colour, q] for q in range(2)]
-            box = box_ref[96 + 2 * colour + j] if j < 2 else from_after(56 + colour)
+            box = flat_box[pl.ds((((3 * colour + 2) * 8) * 2 + j) * SUBS + 7, SUBS, stride=2 * SUBS)] if j < 2 else from_after(56 + colour)
             edge = jnp.zeros((SUBS, LANES), F32)
             for place, side, near in ((0, 0, 1), (1, 0, 0), (6, 1, 0), (7, 1, 1)):
                 k = colour * 6 + near * 3 + j
@@ -445,13 +441,13 @@
             real(2, 2, 2),
             real(2 * pairs + 2),
             real(2 * pairs + 2),
-            real(100),
+            real(96),
         ),
-        in_specs=in_vmem(2),
+        in_specs=in_vmem(1),
         out_specs=tuple(in_vmem(5)),
         scratch_shapes=[pltpu.VMEM((2, channels + 2, planes, LANES), F32)],
         compiler_params=params,
-    )(sources, jnp.stack([absorption, conductance]))
+    )(jnp.concatenate([sources, absorption[None], conductance[None]]))
     second = lax.ppermute(second, "grp", swap_pairs(groups, 1))
     first = lax.ppermute(first, "grp", swap_pairs(groups, 0))
     box = lax.ppermute(box, "boxes", [(i + 1, i) for i in range(boxes - 1)])
@@ -460,8 +456,9 @@
         out_shape=(real(2, 3, pairs), real(2, 2), real(60), real(60)),
         in_specs=in_vmem(4),
         out_specs=tuple(in_vmem(4)),
+        cost_estimate=pl.CostEstimate(flops=5_000_000_000, bytes_accessed=0, transcendentals=0),
         compiler_params=params,
-    )(own, plane, first, second)
+    )(own, plane, second, first)
     chip = lax.ppermute(chip, "boxes", swap_pairs(boxes, 0))
     far = lax.ppermute(far, "boxes", swap_pairs(boxes, 1))
     smem = pl.BlockSpec(memory_space=pltpu.SMEM)
@@ -482,7 +479,7 @@
             pltpu.SemaphoreType.DMA((MOST, 2)),
         ],
         compiler_params=params,
-    )(run_lengths, diffusivity, own, plane, rim, rim_plane, box, chip, far)
+    )(run_lengths, diffusivity, own, plane, rim, rim_plane, box, far, chip)
 
 
 def solution(mesh):

time: 31.1 us -> 26.7 us (0.86)
  the two profiles are of different devices: /device:TPU:19 before, /device:TPU:12 now
where the time goes in v4:
time: 26.7 us
  starting transfers between devices  9.64 us (36%)
  waiting for transfers between devices  9.17 us (34%)
  Pallas kernels  6.63 us (25%)
  other arithmetic  1.21 us (5%)
    ppermute x1, waiting for transfers between devices, on_device(): far = lax.ppermute(far, 'boxes', swap_pairs(boxes, 1))  6.56 us
    pallas_call x1, Pallas kernels, on_device(): pl.pallas_call(smooth, out_shape=jax.ShapeDtypeStruct((channels, MOST * B...  4.87 us
    ppermute x1, starting transfers between devices, on_device(): second = lax.ppermute(second, 'grp', swap_pairs(groups, 1))  3.48 us
    ppermute x1, starting transfers between devices, on_device(): box = lax.ppermute(box, 'boxes', [(i + 1, i) for i in range(boxes - 1)])  2.5 us
    ppermute x1, starting transfers between devices, on_device(): far = lax.ppermute(far, 'boxes', swap_pairs(boxes, 1))  1.92 us
    ppermute x1, starting transfers between devices, on_device(): chip = lax.ppermute(chip, 'boxes', swap_pairs(boxes, 0))  1.66 us
    ppermute x1, waiting for transfers between devices, on_device(): first = lax.ppermute(first, 'grp', swap_pairs(groups, 0))  1.38 us
    ppermute x1, waiting for transfers between devices, on_device(): second = lax.ppermute(second, 'grp', swap_pairs(groups, 1))  1.23 us
  transfers between devices with their start and end apart: 5, of which 3 were waited for; matrix products, arithmetic and copies ran while one was open for 0% of the time, Pallas kernels for 3%

profile of v4, /device:TPU:12, one launch (start us, length us, event | category | flops | bytes accessed | tf_op | source)
XLA Modules:
  0.0 26.7 jit_solution(12199928973639607934)
XLA Ops:
  0.0 1.2 %pad_maximum_fusion.src_ref = f32[24,32,256]{2,1,0:T(8,128)S(1)} fusion(f32[1,32,256]{2,1,0:T(8,128)} %bitcast.2, f32[1,32,256]{2,1,0:T(8,128)} %bitcast.3, f32[22,32,256]{2,1,0:T(8,128)} %param.5), kind=kLoop, calls=%fused_computation | loop fusion | flops 393216 | bytes 1572864 | tf_op jit(solution)/shard_map/concatenate | solution.py:450
  1.2 1.0 %shard_map.55 = (f32[2,3,16,2,8,128]{5,4,3,2,1,0:T(8,128)S(1)}, f32[2,2,2,8,128]{4,3,2,1,0:T(8,128)S(1)}, f32[34,8,128]{2,1,0:T(8,128)S(1)}, f32[34,8,128]{2,1,0:T(8,128)S(1)}, f32[96,8,128]{2,1,0:T(8,128)S(1)}) custom-call(f32[24,32,256]{2,1,0:T(8,128)S(1)} %pad_maximum_fusion.src_ref), custom_call_target="tpu_custom_call" | custom-call | tf_op jit(solution)/shard_map/pallas_call | solution.py:437
  2.2 3.5 %collective-permute-start = (f32[34,8,128]{2,1,0:T(8,128)S(1)}, f32[34,8,128]{2,1,0:T(8,128)S(1)}, u32[]{:S(2)}, u32[]{:S(2)}) collective-permute-start(f32[34,8,128]{2,1,0:T(8,128)S(1)} %get-tuple-element.16), channel_id=1, source_target_pairs={{1,2},{2,1},{5,6},{6,5},{9,10},{10,9},{13,14},{14,13},{17,18},{18,... | collective-permute-start | bytes 417800 | tf_op jit(solution)/shard_map/ppermute | solution.py:451
  5.7 0.1 collective-permute-start.1
  5.8 2.5 %collective-permute-start.2 = (f32[96,8,128]{2,1,0:T(8,128)S(1)}, f32[96,8,128]{2,1,0:T(8,128)S(1)}, u32[]{:S(2)}, u32[]{:S(2)}) collective-permute-start(f32[96,8,128]{2,1,0:T(8,128)S(1)} %get-tuple-element.20), channel_id=1, source_target_pairs={{4,0},{8,4},{12,8},{16,12},{20,16},{24,20},{28,24},{5,1},{9,5},{13... | collective-permute-start | bytes 1179656 | tf_op jit(solution)/shard_map/ppermute | solution.py:453
  8.3 1.2 %collective-permute-done.second_ref = f32[34,8,128]{2,1,0:T(8,128)S(1)} collective-permute-done((f32[34,8,128]{2,1,0:T(8,128)S(1)}, f32[34,8,128]{2,1,0:T(8,128)S(1)}, u32[]{:S(2)}, u32[]{:S(2)}) %collective-permute-start) | collective-permute-done | bytes 139296 | tf_op jit(solution)/shard_map/ppermute | solution.py:451
  9.6 1.4 %collective-permute-done.1.first_ref = f32[34,8,128]{2,1,0:T(8,128)S(1)} collective-permute-done((f32[34,8,128]{2,1,0:T(8,128)S(1)}, f32[34,8,128]{2,1,0:T(8,128)S(1)}, u32[]{:S(2)}, u32[]{:S(2)}) %collective-permute-start.1) | collective-permute-done | bytes 139296 | tf_op jit(solution)/shard_map/ppermute | solution.py:452
  10.9 0.0 copy-start
  10.9 0.0 copy-start.1
  10.9 0.7 %shard_map.56 = (f32[2,3,16,8,128]{4,3,2,1,0:T(8,128)S(1)}, f32[2,2,8,128]{3,2,1,0:T(8,128)S(1)}, f32[60,8,128]{2,1,0:T(8,128)S(1)}, f32[60,8,128]{2,1,0:T(8,128)S(1)}) custom-call(f32[2,3,16,2,8,128]{5,4,3,2,1,0:T(8,128)S(1)} %get-tuple-element.14.own_ref, f32[2,2,2,8,128]{4,3,2,1,0:T(8,128)S(1)} %get-tuple-element.15.plane_ref, ...), custom_call_target="tpu_custom_call" | custom-call | flops 5000000000 | tf_op jit(solution)/shard_map/pallas_call | solution.py:454
  11.7 1.9 %collective-permute-start.3 = (f32[60,8,128]{2,1,0:T(8,128)S(1)}, f32[60,8,128]{2,1,0:T(8,128)S(1)}, u32[]{:S(2)}, u32[]{:S(2)}) collective-permute-start(f32[60,8,128]{2,1,0:T(8,128)S(1)} %get-tuple-element.21), channel_id=1, source_target_pairs={{4,8},{12,16},{20,24},{8,4},{16,12},{24,20},{5,9},{13,17},{21,25},... | collective-permute-start | bytes 737288 | tf_op jit(solution)/shard_map/ppermute | solution.py:463
  13.6 1.7 %collective-permute-start.4 = (f32[60,8,128]{2,1,0:T(8,128)S(1)}, f32[60,8,128]{2,1,0:T(8,128)S(1)}, u32[]{:S(2)}, u32[]{:S(2)}) collective-permute-start(f32[60,8,128]{2,1,0:T(8,128)S(1)} %get-tuple-element.22), channel_id=1, source_target_pairs={{0,4},{8,12},{16,20},{24,28},{4,0},{12,8},{20,16},{28,24},{1,5},{9... | collective-permute-start | bytes 737288 | tf_op jit(solution)/shard_map/ppermute | solution.py:462
  15.3 6.6 %collective-permute-done.3.far_ref = f32[60,8,128]{2,1,0:T(8,128)S(1)} collective-permute-done((f32[60,8,128]{2,1,0:T(8,128)S(1)}, f32[60,8,128]{2,1,0:T(8,128)S(1)}, u32[]{:S(2)}, u32[]{:S(2)}) %collective-permute-start.3) | collective-permute-done | bytes 245792 | tf_op jit(solution)/shard_map/ppermute | solution.py:463
  21.8 0.0 collective-permute-done.4.chip_ref
  21.8 0.0 collective-permute-done.2.box_ref
  21.8 0.0 copy-done
  21.9 0.0 copy-done.1
  21.9 4.9 %shard_map.57 = f32[22,48,256]{2,1,0:T(8,128)} custom-call(s32[8]{0:T(128)S(1)} %copy-done, f32[22]{0:T(128)S(1)} %copy-done.1, f32[2,3,16,2,8,128]{5,4,3,2,1,0:T(8,128)S(1)} %get-tuple-element.14.own_ref, f32[2,2,2,8,128]{4,3,2,1,0:T(8,128)S(1)} %get-tuple-element.15.plane_ref, f32[2,3,16,8,128]{4,3,2,1,0:T(8,128)S(1)} %get-tuple-element.18.rim_ref, ...), custom_call_target="tpu_custom_call" | custom-call | tf_op jit(solution)/shard_map/pallas_call | solution.py:465
Async XLA Ops:
  2.2 7.3 %collective-permute-start = (f32[34,8,128]{2,1,0:T(8,128)S(1)}, f32[34,8,128]{2,1,0:T(8,128)S(1)}, u32[]{:S(2)}, u32[]{:S(2)}) collective-permute-start(f32[34,8,128]{2,1,0:T(8,128)S(1)} %get-tuple-element.16), channel_id=1, source_target_pairs={{1,2},{2,1},{5,6},{6,5},{9,10},{10,9},{13,14},{14,13},{17,18},{18,... | collective-permute-start | bytes 417800 | tf_op jit(solution)/shard_map/ppermute | solution.py:451
  5.7 5.2 %collective-permute-start.1 = (f32[34,8,128]{2,1,0:T(8,128)S(1)}, f32[34,8,128]{2,1,0:T(8,128)S(1)}, u32[]{:S(2)}, u32[]{:S(2)}) collective-permute-start(f32[34,8,128]{2,1,0:T(8,128)S(1)} %get-tuple-element.17), channel_id=1, source_target_pairs={{0,1},{2,3},{1,0},{3,2},{4,5},{6,7},{5,4},{7,6},{8,9},{10,11},{9,8... | collective-permute-start | bytes 417800 | tf_op jit(solution)/shard_map/ppermute | solution.py:452
  5.8 16.0 %collective-permute-start.2 = (f32[96,8,128]{2,1,0:T(8,128)S(1)}, f32[96,8,128]{2,1,0:T(8,128)S(1)}, u32[]{:S(2)}, u32[]{:S(2)}) collective-permute-start(f32[96,8,128]{2,1,0:T(8,128)S(1)} %get-tuple-element.20), channel_id=1, source_target_pairs={{4,0},{8,4},{12,8},{16,12},{20,16},{24,20},{28,24},{5,1},{9,5},{13... | collective-permute-start | bytes 1179656 | tf_op jit(solution)/shard_map/ppermute | solution.py:453
  10.9 10.9 %copy-start = (s32[8]{0:T(128)S(1)}, s32[8]{0:T(128)}, u32[]{:S(2)}) copy-start(s32[8]{0:T(128)} %lengths_ref.1) | copy-start | bytes 100
  10.9 10.9 %copy-start.1 = (f32[22]{0:T(128)S(1)}, f32[22]{0:T(128)}, u32[]{:S(2)}) copy-start(f32[22]{0:T(128)} %factor_ref.1) | copy-start | bytes 268
  11.7 10.1 %collective-permute-start.3 = (f32[60,8,128]{2,1,0:T(8,128)S(1)}, f32[60,8,128]{2,1,0:T(8,128)S(1)}, u32[]{:S(2)}, u32[]{:S(2)}) collective-permute-start(f32[60,8,128]{2,1,0:T(8,128)S(1)} %get-tuple-element.21), channel_id=1, source_target_pairs={{4,8},{12,16},{20,24},{8,4},{16,12},{24,20},{5,9},{13,17},{21,25},... | collective-permute-start | bytes 737288 | tf_op jit(solution)/shard_map/ppermute | solution.py:463
  13.6 8.2 %collective-permute-start.4 = (f32[60,8,128]{2,1,0:T(8,128)S(1)}, f32[60,8,128]{2,1,0:T(8,128)S(1)}, u32[]{:S(2)}, u32[]{:S(2)}) collective-permute-start(f32[60,8,128]{2,1,0:T(8,128)S(1)} %get-tuple-element.22), channel_id=1, source_target_pairs={{0,4},{8,12},{16,20},{24,28},{4,0},{12,8},{20,16},{28,24},{1,5},{9... | collective-permute-start | bytes 737288 | tf_op jit(solution)/shard_map/ppermute | solution.py:462

commit v5 on v4

--- a/solution.py
+++ b/solution.py
@@ -210,177 +210,195 @@
     ]
 
 
-def smooth(
-    lengths_ref, factor_ref, own_ref, plane_ref, rim_ref, rim_plane_ref, box_ref, far_ref, chip_ref,
-    out_ref,
-    face_ref, weight_ref, box_rim_ref, edge_ref, inverse_ref, value_ref, placed_ref, shift_ref, sems,
-):
-    channels, rows, _ = out_ref.shape
-    position = lax.axis_index("boxes")
-    group = lax.axis_index("grp")
-    even_box = position % 2 == 0
-    last_box = position == lax.axis_size("boxes") - 1
-    lane, even = lane_places(SUBS)
-    sub = lax.broadcasted_iota(jnp.int32, (SUBS, LANES), 0)
-    tiles = range(3)
-
-    def from_after(i):
-        return jnp.where(even_box, chip_ref[i], far_ref[i])
-
-    def from_before(i):
-        return jnp.where(even_box, far_ref[i], chip_ref[i])
-
-    edges = [[jnp.concatenate([get(58), get(59)], 0) for get in (from_after, from_before)]][0]
-    flat_box = box_ref.reshape(96 * SUBS, LANES)
-    conduct = []
-    for colour in range(2):
-        planes = []
-        for j in tiles:
-            own = [plane_ref[colour, j, q] if j < 2 else rim_plane_ref[colour, q] for q in range(2)]
-            box = flat_box[pl.ds((((3 * colour + 2) * 8) * 2 + j) * SUBS + 7, SUBS, stride=2 * SUBS)] if j < 2 else from_after(56 + colour)
-            edge = jnp.zeros((SUBS, LANES), F32)
-            for place, side, near in ((0, 0, 1), (1, 0, 0), (6, 1, 0), (7, 1, 1)):
-                k = colour * 6 + near * 3 + j
-                edge = jnp.where(sub == place, jnp.broadcast_to(edges[side][k : k + 1], sub.shape), edge)
-            planes.append(jnp.concatenate(own + [box, edge], 0))
-        conduct.append(planes)
-    wide_lane, wide_even = lane_places(RING)
-    for colour in range(2):
-        others = conduct[1 - colour]
-        beside = lane_neighbours(others, wide_lane)
-        for j in tiles:
-            after, before = pltpu.roll(others[j], RING - 1, 0), pltpu.roll(others[j], 1, 0)
-            across = jnp.where(wide_even, *((before, after) if colour == 0 else (after, before)))
-            total = jnp.zeros((RING, LANES), F32)
-            for i, other in enumerate([others[j], across] + beside[j]):
-                face = conduct[colour][j] + other
-                face_ref[colour, i, j] = face
-                total = total + face
-            weight_ref[colour, j] = total
-
-    for p in range(8):
-        reds, blacks = unpack_halo([from_after(4 * p + i) for i in range(4)], lane)
+INNER = [range(1, 15), range(1, 15), range(2, 14), range(2, 14)]
+
+
+class Smoother:
+    def __init__(self, factor_ref, face_ref, weight_ref, inverse_ref, shift_ref, channels, ring):
+        self.face_ref, self.weight_ref, self.inverse_ref = face_ref, weight_ref, inverse_ref
+        self.shift_ref, self.ring = shift_ref, ring
+        self.lane, self.even = lane_places(SUBS)
+        sub = lax.broadcasted_iota(jnp.int32, (SUBS, LANES), 0)
+        group = lax.axis_index("grp")
+        above = jnp.where(group == lax.axis_size("grp") - 1, 0, LANES)
+        below = jnp.where(group == 0, LANES, 0)
+        self.limit = [
+            ((self.lane < jnp.minimum(above, PLANE_Z * rows)))
+            | (self.lane >= jnp.maximum(below, LANES - PLANE_Z * rows))
+            for rows in (3, 2)
+        ]
+        self.factors = []
         for ct in range(3):
-            box_rim_ref[0, ct, p], box_rim_ref[1, ct, p] = reds[ct], blacks[ct]
-    for ct in range(3):
-        for i in range(8):
-            edge_ref[0, ct, i] = from_before(32 + ct * 8 + i)
-            edge_ref[1, ct, i] = from_after(32 + ct * 8 + i)
-
-    def own_source(q):
-        p = q - 2
-        return lambda colour, ct, j: own_ref[colour, ct, p, j] if j < 2 else rim_ref[colour, ct, p]
-
-    def box_source(q):
-        p = q - 18
-        return lambda colour, ct, j: (
-            box_ref[((colour * 3 + ct) * 8 + p) * 2 + j] if j < 2 else box_rim_ref[colour, ct, p]
-        )
-
-    def edge_source(q):
-        near, side = (q in (1, 26)), int(q > 20)
-        return lambda colour, ct, j: edge_ref[side, ct, EDGE.index((colour, int(near), j))]
-
-    lane_limit = [
-        None,
-        None,
-        (lane < jnp.where(group == lax.axis_size("grp") - 1, 0, RIM))
-        | (lane >= jnp.where(group == 0, LANES, RIM)),
-    ]
-    factors = []
-    for ct in range(3):
-        factor = jnp.zeros((SUBS, LANES), F32)
-        for i in range(min(SUBS, channels - ct * SUBS)):
-            factor = jnp.where(sub == i, 0.5 * factor_ref[ct * SUBS + i], factor)
-        factors.append(factor)
-
-    def spread(ref, index, row):
+            factor = jnp.zeros((SUBS, LANES), F32)
+            for i in range(min(SUBS, channels - ct * SUBS)):
+                factor = jnp.where(sub == i, 0.5 * factor_ref[ct * SUBS + i], factor)
+            self.factors.append(factor)
+
+    def find_faces(self, conduct):
+        wide_lane, wide_even = lane_places(self.ring)
+        for colour in range(2):
+            others = conduct[1 - colour]
+            beside = lane_neighbours(others, wide_lane)
+            for j in range(3):
+                after, before = pltpu.roll(others[j], self.ring - 1, 0), pltpu.roll(others[j], 1, 0)
+                across = jnp.where(wide_even, *((before, after) if colour == 0 else (after, before)))
+                total = jnp.zeros((self.ring, LANES), F32)
+                for i, other in enumerate([others[j], across] + beside[j]):
+                    face = conduct[colour][j] + other
+                    self.face_ref[colour, i, j] = face
+                    total = total + face
+                self.weight_ref[colour, j] = total
+
+    def spread(self, ref, index, q):
+        row = (q + RING - 2) % RING
         return jnp.broadcast_to(ref[index + (pl.ds(row, 1),)], (SUBS, LANES))
 
-    def invert(q, colour, source, exists, wanted=(0, 1, 2)):
-        row = (q + RING - 2) % RING
+    def invert(self, q, colour, source, exists, wanted=(0, 1, 2)):
         for j in wanted:
             absorb = jnp.broadcast_to(source(colour, 2, j)[6:7], (SUBS, LANES))
-            weight = spread(weight_ref, (colour, j), row)
+            weight = self.spread(self.weight_ref, (colour, j), q)
+            keep = exists if j < 2 else self.limit[colour]
+            if exists is not None and j == 2:
+                keep = keep & exists
             for ct in range(3):
-                inverse = 1.0 / (absorb + factors[ct] * weight)
-                keep = lane_limit[j]
-                if exists is not None:
-                    keep = exists if keep is None else keep & exists
+                inverse = 1.0 / (absorb + self.factors[ct] * weight)
                 if keep is not None:
                     inverse = jnp.where(keep, inverse, 0.0)
-                inverse_ref[colour, ct, q, j] = inverse
-
-    def start_red(q, source, exists, wanted=(0, 1, 2)):
-        invert(q, 0, source, exists, wanted)
-        for j in wanted:
-            for ct in range(3):
-                value_ref[0, ct, q, j] = source(0, ct, j) * inverse_ref[0, ct, q, j]
-
-    for i, matrix in enumerate(shift_matrices()):
-        shift_ref[i] = matrix
-
-    def shifted(places, colour):
-        index = [(ct, q, j) for q in places for ct in range(3) for j in tiles]
-        x = jnp.concatenate([value_ref[colour, ct, q, j] for ct, q, j in index], 0)
+                self.inverse_ref[colour, ct, q, j] = inverse
+
+    def shifted(self, places, get):
+        index = [(ct, q, j) for q in places for ct in range(3) for j in range(3)]
+        x = jnp.concatenate([get(*key) for key in index], 0)
         high = x.astype(jnp.bfloat16)
         both = jnp.concatenate([high, (x - high.astype(F32)).astype(jnp.bfloat16)], 1)
-        moved = [jnp.dot(both, shift_ref[i], preferred_element_type=F32) for i in range(2)]
+        moved = [jnp.dot(both, self.shift_ref[i], preferred_element_type=F32) for i in range(2)]
         result = {}
         for k, key in enumerate(index):
             rows = slice(k * SUBS, (k + 1) * SUBS)
             result[key] = [m[rows, i * LANES : (i + 1) * LANES] for m in moved for i in range(2)]
         return result
 
-    def update(places, colour, wanted=(0, 1, 2)):
-        moved = shifted(places, 1 - colour)
+    def update(self, places, colour, get, put, source_of, wanted=(0, 1, 2)):
+        lane, even = self.lane, self.even
+        moved = self.shifted(places, get)
         for q in places:
-            row = (q + RING - 2) % RING
             source = source_of(q)
-            faces = [[spread(face_ref, (colour, i, j), row) for i in range(6)] for j in wanted]
+            faces = [
+                [self.spread(self.face_ref, (colour, i, j), q) for i in range(6)] for j in wanted
+            ]
             for ct in range(3):
-                near = [moved[ct, q, j] for j in tiles]
+                near = [moved[ct, q, j] for j in range(3)]
                 for j, face in zip(wanted, faces):
-                    same = value_ref[1 - colour, ct, q, j]
-                    before, after = value_ref[1 - colour, ct, q - 1, j], value_ref[1 - colour, ct, q + 1, j]
+                    before, after = get(ct, q - 1, j), get(ct, q + 1, j)
                     across = jnp.where(even, *((before, after) if colour == 0 else (after, before)))
                     up = jnp.where(lane < LANES - PLANE_Z, near[j][2], near[(j + 1) % 3][2])
                     down = jnp.where(lane < PLANE_Z, near[(j + 2) % 3][3], near[j][3])
-                    inflow = face[0] * same
+                    inflow = face[0] * get(ct, q, j)
                     for one, other in zip(face[1:], [across, near[j][0], near[j][1], up, down]):
                         inflow = inflow + one * other
-                    value = (source(colour, ct, j) + factors[ct] * inflow) * inverse_ref[colour, ct, q, j]
-                    value_ref[colour, ct, q, j] = value
-
-    after_exists = jnp.broadcast_to(jnp.logical_not(last_box), (SUBS, LANES))
-    before_exists = jnp.broadcast_to(position > 0, (SUBS, LANES))
+                    value = source(colour, ct, j) + self.factors[ct] * inflow
+                    put(ct, q, j, value * self.inverse_ref[colour, ct, q, j])
+
+
+def own_run(lengths_ref):
+    position = lax.axis_index("boxes")
+    first_box = lax.fori_loop(0, position, lambda i, total: total + lengths_ref[i], jnp.int32(0))
+    return first_box - position * OLD_DEV, lengths_ref[position]
+
+
+def placer(placed_ref, start, even):
+    rows = placed_ref.shape[2]
+    flat = placed_ref.reshape(2 * 3 * SUBS * rows, LANES)
+
+    def place(ct, q, j, red, black):
+        row = (j * 3 + ct) * SUBS * rows + 2 * (q - 2 - 8 * start)
+        flat[pl.ds(row, SUBS, stride=rows)] = jnp.where(even, red, black)
+        flat[pl.ds(row + 1, SUBS, stride=rows)] = jnp.where(even, black, red)
+
+    return place
+
+
+def smooth_inner(
+    lengths_ref, factor_ref, own_ref, plane_ref, rim_ref, rim_plane_ref,
+    value_ref, placed_ref, shift_ref,
+    face_ref, weight_ref, inverse_ref,
+):
+    pairs = own_ref.shape[2]
+    channels = factor_ref.shape[0]
+    work = Smoother(factor_ref, face_ref, weight_ref, inverse_ref, shift_ref, channels, pairs)
+    for i, matrix in enumerate(shift_matrices()):
+        shift_ref[i] = matrix
+
+    def plane(colour, j):
+        return [plane_ref[colour, j, k] if j < 2 else rim_plane_ref[colour, k] for k in range(2)]
+
+    work.find_faces(
+        [[jnp.concatenate(plane(colour, j), 0) for j in range(3)] for colour in range(2)]
+    )
 
     def source_of(q):
-        return own_source(q) if 2 <= q < 18 else box_source(q) if 18 <= q < 26 else edge_source(q)
-
-    def exists(q):
-        return before_exists if q < 2 else None if q < 18 else after_exists
-
-    for q in range(28):
-        start_red(q, source_of(q), exists(q), (0, 1) if q in (0, 27) else (0, 1, 2))
-    zero = jnp.zeros((SUBS, LANES), F32)
-    for q in (0, 27):
+        p = q - 2
+        return lambda colour, ct, j: own_ref[colour, ct, p, j] if j < 2 else rim_ref[colour, ct, p]
+
+    def getter(stage):
+        return lambda ct, q, j: value_ref[stage, ct, q - 2, j]
+
+    def putter(stage):
+        def put(ct, q, j, value):
+            value_ref[stage, ct, q - 2, j] = value
+
+        return put
+
+    for p in range(pairs):
+        source = source_of(p + 2)
+        work.invert(p + 2, 0, source, None)
+        work.invert(p + 2, 1, source, None)
         for ct in range(3):
-            value_ref[0, ct, q, 2] = zero
-            for j in tiles:
-                value_ref[1, ct, q, j] = zero
-
-    blocks = [range(1, 11), range(11, 19), range(19, 27)]
-    for places in blocks:
-        for q in places:
-            invert(q, 1, source_of(q), exists(q))
-        update(places, 1)
-    for places in blocks:
-        update(places, 0)
-
-    box_count = lengths_ref[position]
-    first_box = lax.fori_loop(0, position, lambda i, total: total + lengths_ref[i], jnp.int32(0))
-    start = first_box - position * OLD_DEV
+            for j in range(3):
+                value_ref[0, ct, p, j] = source(0, ct, j) * inverse_ref[0, ct, p + 2, j]
+    for p in (0, pairs - 1):
+        for ct in range(3):
+            for j in range(3):
+                value_ref[1, ct, p, j] = jnp.zeros((SUBS, LANES), F32)
+    for places in (range(3, 11), range(11, 17)):
+        work.update(places, 1, getter(0), putter(1), source_of)
+    for places in (range(3, 11), range(11, 17)):
+        work.update(places, 0, getter(1), putter(2), source_of)
+    for places in (range(4, 10), range(10, 16)):
+        work.update(places, 1, getter(2), putter(3), source_of, (0, 1))
+
+    start, box_count = own_run(lengths_ref)
+    place = placer(placed_ref, start, work.even)
+    for box, places in enumerate((range(4, 10), range(10, 16))):
+        @pl.when((box >= start) & (box < start + box_count))
+        def _():
+            for q in places:
+                for ct in range(3):
+                    for j in range(2):
+                        place(ct, q, j, getter(2)(ct, q, j), getter(3)(ct, q, j))
+
+    for k in range(1, MOST):
+        @pl.when(k >= box_count)
+        def _():
+            for j in range(2):
+                for c in range(channels):
+                    placed_ref[j, c, k * BOX_X : (k + 1) * BOX_X] = jnp.zeros((BOX_X, LANES), F32)
+
+
+def smooth_outer(
+    lengths_ref, factor_ref, own_ref, plane_ref, rim_ref, rim_plane_ref, box_ref, far_ref, chip_ref,
+    inner_ref, shift_ref, given_ref,
+    out_ref, placed_ref,
+    face_ref, weight_ref, inverse_ref, value_ref, box_rim_ref, edge_ref, sems,
+):
+    channels = out_ref.shape[0]
+    position = lax.axis_index("boxes")
+    even_box = position % 2 == 0
+    last_box = position == lax.axis_size("boxes") - 1
+    work = Smoother(factor_ref, face_ref, weight_ref, inverse_ref, shift_ref, channels, RING)
+    lane = work.lane
+    sub = lax.broadcasted_iota(jnp.int32, (SUBS, LANES), 0)
+    start, box_count = own_run(lengths_ref)
 
     def send(k):
         rows = pl.ds(pl.multiple_of(k * BOX_X, BOX_X), BOX_X)
@@ -393,30 +411,119 @@
             for j in range(2)
         ]
 
-    flat = placed_ref.reshape(2 * 3 * SUBS * rows, LANES)
-    for box in range(MOST):
-        @pl.when((box >= start) & (box < start + box_count))
-        def _():
-            places = range(2 + box * 8, 10 + box * 8)
-            update(places, 1, (0, 1))
-            for q in places:
-                for ct in range(3):
-                    for j in range(2):
-                        red, black = value_ref[0, ct, q, j], value_ref[1, ct, q, j]
-                        row = (j * 3 + ct) * SUBS * rows + 2 * (q - 2 - 8 * start)
-                        flat[pl.ds(row, SUBS, stride=rows)] = jnp.where(even, red, black)
-                        flat[pl.ds(row + 1, SUBS, stride=rows)] = jnp.where(even, black, red)
-            for copy in send(box - start):
-                copy.start()
-
     for k in range(1, MOST):
         @pl.when(k >= box_count)
         def _():
-            for j in range(2):
-                for c in range(channels):
-                    placed_ref[j, c, k * BOX_X : (k + 1) * BOX_X] = jnp.zeros((BOX_X, LANES), F32)
             for copy in send(k):
                 copy.start()
+
+    def from_after(i):
+        return jnp.where(even_box, chip_ref[i], far_ref[i])
+
+    def from_before(i):
+        return jnp.where(even_box, far_ref[i], chip_ref[i])
+
+    edges = [jnp.concatenate([get(58), get(59)], 0) for get in (from_after, from_before)]
+    flat_box = box_ref.reshape(96 * SUBS, LANES)
+    conduct = []
+    for colour in range(2):
+        planes = []
+        for j in range(3):
+            own = [plane_ref[colour, j, k] if j < 2 else rim_plane_ref[colour, k] for k in range(2)]
+            if j < 2:
+                row = (((3 * colour + 2) * 8) * 2 + j) * SUBS + 7
+                box = flat_box[pl.ds(row, SUBS, stride=2 * SUBS)]
+            else:
+                box = from_after(56 + colour)
+            edge = jnp.zeros((SUBS, LANES), F32)
+            for place_at, side, near in ((0, 0, 1), (1, 0, 0), (6, 1, 0), (7, 1, 1)):
+                k = colour * 6 + near * 3 + j
+                row = jnp.broadcast_to(edges[side][k : k + 1], (SUBS, LANES))
+                edge = jnp.where(sub == place_at, row, edge)
+            planes.append(jnp.concatenate(own + [box, edge], 0))
+        conduct.append(planes)
+    work.find_faces(conduct)
+
+    for p in range(8):
+        reds, blacks = unpack_halo([from_after(4 * p + i) for i in range(4)], lane)
+        for ct in range(3):
+            box_rim_ref[0, ct, p], box_rim_ref[1, ct, p] = reds[ct], blacks[ct]
+    for ct in range(3):
+        for i in range(8):
+            edge_ref[0, ct, i] = from_before(32 + ct * 8 + i)
+            edge_ref[1, ct, i] = from_after(32 + ct * 8 + i)
+
+    def source_of(q):
+        if 2 <= q < 18:
+            return lambda colour, ct, j: (
+                own_ref[colour, ct, q - 2, j] if j < 2 else rim_ref[colour, ct, q - 2]
+            )
+        if 18 <= q < 26:
+            return lambda colour, ct, j: (
+                box_ref[((colour * 3 + ct) * 8 + q - 18) * 2 + j]
+                if j < 2
+                else box_rim_ref[colour, ct, q - 18]
+            )
+        near, side = int(q in (1, 26)), int(q > 20)
+        return lambda colour, ct, j: edge_ref[side, ct, EDGE.index((colour, near, j))]
+
+    after_exists = jnp.broadcast_to(jnp.logical_not(last_box), (SUBS, LANES))
+    before_exists = jnp.broadcast_to(position > 0, (SUBS, LANES))
+
+    def exists(q):
+        return before_exists if q < 2 else None if q < 18 else after_exists
+
+    def getter(stage):
+        def get(ct, q, j):
+            if q - 2 in INNER[stage]:
+                return inner_ref[stage, ct, q - 2, j]
+            return value_ref[stage, ct, q, j]
+
+        return get
+
+    def putter(stage):
+        def put(ct, q, j, value):
+            value_ref[stage, ct, q, j] = value
+
+        return put
+
+    def rest(stage, begin, end):
+        return [q for q in range(begin, end) if q - 2 not in INNER[stage]]
+
+    zero = jnp.zeros((SUBS, LANES), F32)
+    for q in sorted(set(rest(0, 0, 28)) | set(rest(2, 1, 27))):
+        wanted = (0, 1) if q in (0, 27) else (0, 1, 2)
+        source = source_of(q)
+        work.invert(q, 0, source, exists(q), wanted)
+        if q - 2 not in INNER[0]:
+            for ct in range(3):
+                for j in wanted:
+                    value_ref[0, ct, q, j] = source(0, ct, j) * inverse_ref[0, ct, q, j]
+    for q in (0, 27):
+        for ct in range(3):
+            value_ref[0, ct, q, 2] = zero
+            for j in range(3):
+                value_ref[1, ct, q, j] = zero
+
+    for q in sorted(set(rest(1, 1, 27)) | set(rest(3, 2, 26))):
+        work.invert(q, 1, source_of(q), exists(q))
+    work.update(rest(1, 1, 27), 1, getter(0), putter(1), source_of)
+    work.update(rest(2, 1, 27), 0, getter(1), putter(2), source_of)
+
+    place = placer(placed_ref, start, work.even)
+    for begin, end, boxes in ((2, 18, (0, 1)), (18, 26, (2,))):
+        places = rest(3, begin, end)
+        work.update(places, 1, getter(2), putter(3), source_of, (0, 1))
+        for box in boxes:
+            @pl.when((box >= start) & (box < start + box_count))
+            def _():
+                for q in places:
+                    if (q - 2) // 8 == box:
+                        for ct in range(3):
+                            for j in range(2):
+                                place(ct, q, j, getter(2)(ct, q, j), value_ref[3, ct, q, j])
+                for copy in send(box - start):
+                    copy.start()
 
     for k in range(MOST):
         for copy in send(k):
@@ -462,24 +569,45 @@
     chip = lax.ppermute(chip, "boxes", swap_pairs(boxes, 0))
     far = lax.ppermute(far, "boxes", swap_pairs(boxes, 1))
     smem = pl.BlockSpec(memory_space=pltpu.SMEM)
-    return pl.pallas_call(
-        smooth,
-        out_shape=jax.ShapeDtypeStruct((channels, MOST * BOX_X, cells), F32),
-        in_specs=[smem, smem] + in_vmem(7),
-        out_specs=pl.BlockSpec(memory_space=pltpu.HBM),
+    placed_shape = (2, 3 * SUBS, MOST * BOX_X, LANES)
+    inner, placed, shift = pl.pallas_call(
+        smooth_inner,
+        out_shape=(
+            real(4, 3, pairs, 3),
+            jax.ShapeDtypeStruct(placed_shape, F32),
+            jax.ShapeDtypeStruct((2, 2 * LANES, 2 * LANES), jnp.bfloat16),
+        ),
+        in_specs=[smem, smem] + in_vmem(4),
+        out_specs=tuple(in_vmem(3)),
+        scratch_shapes=[
+            pltpu.VMEM((2, 6, 3, pairs, LANES), F32),
+            pltpu.VMEM((2, 3, pairs, LANES), F32),
+            vmem(2, 3, pairs + 2, 3),
+        ],
+        compiler_params=params,
+        cost_estimate=pl.CostEstimate(flops=2_000_000_000, bytes_accessed=0, transcendentals=0),
+    )(run_lengths, diffusivity, own, plane, rim, rim_plane)
+    correction, _ = pl.pallas_call(
+        smooth_outer,
+        out_shape=(
+            jax.ShapeDtypeStruct((channels, MOST * BOX_X, cells), F32),
+            jax.ShapeDtypeStruct(placed_shape, F32),
+        ),
+        in_specs=[smem, smem] + in_vmem(10),
+        out_specs=(pl.BlockSpec(memory_space=pltpu.HBM), in_vmem(1)[0]),
+        input_output_aliases={11: 1},
         scratch_shapes=[
             pltpu.VMEM((2, 6, 3, RING, LANES), F32),
             pltpu.VMEM((2, 3, RING, LANES), F32),
+            vmem(2, 3, 28, 3),
+            vmem(4, 3, 28, 3),
             vmem(2, 3, 8),
             vmem(2, 3, 8),
-            vmem(2, 3, 28, 3),
-            vmem(2, 3, 28, 3),
-            pltpu.VMEM((2, 3 * SUBS, MOST * BOX_X, LANES), F32),
-            pltpu.VMEM((2, 2 * LANES, 2 * LANES), jnp.bfloat16),
             pltpu.SemaphoreType.DMA((MOST, 2)),
         ],
         compiler_params=params,
-    )(run_lengths, diffusivity, own, plane, rim, rim_plane, box, far, chip)
+    )(run_lengths, diffusivity, own, plane, rim, rim_plane, box, far, chip, inner, shift, placed)
+    return correction
 
 
 def solution(mesh):

time: 26.7 us -> 25 us (0.936)
  waiting for transfers between devices: 9.17 us -> 6.86 us
  Pallas kernels: 6.63 us -> 7.06 us
    ppermute x1, waiting for transfers between devices: 6.56 us -> 4.24 us  [on_device(): far = lax.ppermute(far, 'boxes', swap_pairs(boxes, 1))]
    pallas_call x1 -> x2, Pallas kernels: 4.87 us -> 5.29 us  [the longest x1 2.99 us: on_device(): pl.pallas_call(smooth_outer, out_shape=(jax.ShapeDtypeStruct((channels, M...]
  transfers between devices with their start and end apart: 5 -> 5, of which waited for: 3 -> 3; matrix products, arithmetic and copies ran while one was open for 0% -> 0% of each run, Pallas kernels for 3% -> 12%
where the time goes in v5:
time: 25 us; the launch traced here: 24.8 us
  starting transfers between devices  9.64 us (39%)
  Pallas kernels  7.06 us (28%)
  waiting for transfers between devices  6.86 us (27%)
  other arithmetic  1.21 us (5%)
    ppermute x1, waiting for transfers between devices, on_device(): far = lax.ppermute(far, 'boxes', swap_pairs(boxes, 1))  4.24 us
    ppermute x1, starting transfers between devices, on_device(): second = lax.ppermute(second, 'grp', swap_pairs(groups, 1))  3.48 us
    pallas_call x1, Pallas kernels, on_device(): pl.pallas_call(smooth_outer, out_shape=(jax.ShapeDtypeStruct((channels, M...  2.99 us
    ppermute x1, starting transfers between devices, on_device(): box = lax.ppermute(box, 'boxes', [(i + 1, i) for i in range(boxes - 1)])  2.5 us
    pallas_call x1, Pallas kernels, on_device(): pl.pallas_call(smooth_inner, out_shape=(real(4, 3, pairs, 3), jax.ShapeDt...  2.3 us
    ppermute x1, starting transfers between devices, on_device(): far = lax.ppermute(far, 'boxes', swap_pairs(boxes, 1))  1.92 us
    ppermute x1, starting transfers between devices, on_device(): chip = lax.ppermute(chip, 'boxes', swap_pairs(boxes, 0))  1.66 us
    ppermute x1, waiting for transfers between devices, on_device(): first = lax.ppermute(first, 'grp', swap_pairs(groups, 0))  1.38 us
  transfers between devices with their start and end apart: 5, of which 3 were waited for; matrix products, arithmetic and copies ran while one was open for 0% of the time, Pallas kernels for 12%

profile of v5, /device:TPU:12, one launch (start us, length us, event | category | flops | bytes accessed | tf_op | source)
XLA Modules:
  0.0 24.8 jit_solution(4079074696026649500)
XLA Ops:
  0.0 1.2 %pad_maximum_fusion.src_ref = f32[24,32,256]{2,1,0:T(8,128)S(1)} fusion(f32[1,32,256]{2,1,0:T(8,128)} %bitcast.2, f32[1,32,256]{2,1,0:T(8,128)} %bitcast.3, f32[22,32,256]{2,1,0:T(8,128)} %param.5), kind=kLoop, calls=%fused_computation | loop fusion | flops 393216 | bytes 1572864 | tf_op jit(solution)/shard_map/concatenate | solution.py:557
  1.2 1.0 %shard_map.55 = (f32[2,3,16,2,8,128]{5,4,3,2,1,0:T(8,128)S(1)}, f32[2,2,2,8,128]{4,3,2,1,0:T(8,128)S(1)}, f32[34,8,128]{2,1,0:T(8,128)S(1)}, f32[34,8,128]{2,1,0:T(8,128)S(1)}, f32[96,8,128]{2,1,0:T(8,128)S(1)}) custom-call(f32[24,32,256]{2,1,0:T(8,128)S(1)} %pad_maximum_fusion.src_ref), custom_call_target="tpu_custom_call" | custom-call | tf_op jit(solution)/shard_map/pallas_call | solution.py:544
  2.3 3.5 %collective-permute-start = (f32[34,8,128]{2,1,0:T(8,128)S(1)}, f32[34,8,128]{2,1,0:T(8,128)S(1)}, u32[]{:S(2)}, u32[]{:S(2)}) collective-permute-start(f32[34,8,128]{2,1,0:T(8,128)S(1)} %get-tuple-element.20), channel_id=1, source_target_pairs={{1,2},{2,1},{5,6},{6,5},{9,10},{10,9},{13,14},{14,13},{17,18},{18,... | collective-permute-start | bytes 417800 | tf_op jit(solution)/shard_map/ppermute | solution.py:558
  5.7 0.1 collective-permute-start.1
  5.8 2.5 %collective-permute-start.2 = (f32[96,8,128]{2,1,0:T(8,128)S(1)}, f32[96,8,128]{2,1,0:T(8,128)S(1)}, u32[]{:S(2)}, u32[]{:S(2)}) collective-permute-start(f32[96,8,128]{2,1,0:T(8,128)S(1)} %get-tuple-element.24), channel_id=1, source_target_pairs={{4,0},{8,4},{12,8},{16,12},{20,16},{24,20},{28,24},{5,1},{9,5},{13... | collective-permute-start | bytes 1179656 | tf_op jit(solution)/shard_map/ppermute | solution.py:560
  8.3 1.2 %collective-permute-done.second_ref = f32[34,8,128]{2,1,0:T(8,128)S(1)} collective-permute-done((f32[34,8,128]{2,1,0:T(8,128)S(1)}, f32[34,8,128]{2,1,0:T(8,128)S(1)}, u32[]{:S(2)}, u32[]{:S(2)}) %collective-permute-start) | collective-permute-done | bytes 139296 | tf_op jit(solution)/shard_map/ppermute | solution.py:558
  9.6 1.4 %collective-permute-done.1.first_ref = f32[34,8,128]{2,1,0:T(8,128)S(1)} collective-permute-done((f32[34,8,128]{2,1,0:T(8,128)S(1)}, f32[34,8,128]{2,1,0:T(8,128)S(1)}, u32[]{:S(2)}, u32[]{:S(2)}) %collective-permute-start.1) | collective-permute-done | bytes 139296 | tf_op jit(solution)/shard_map/ppermute | solution.py:559
  10.9 0.0 copy-start
  10.9 0.0 copy-start.1
  10.9 0.7 %shard_map.56 = (f32[2,3,16,8,128]{4,3,2,1,0:T(8,128)S(1)}, f32[2,2,8,128]{3,2,1,0:T(8,128)S(1)}, f32[60,8,128]{2,1,0:T(8,128)S(1)}, f32[60,8,128]{2,1,0:T(8,128)S(1)}) custom-call(f32[2,3,16,2,8,128]{5,4,3,2,1,0:T(8,128)S(1)} %get-tuple-element.18.own_ref, f32[2,2,2,8,128]{4,3,2,1,0:T(8,128)S(1)} %get-tuple-element.19.plane_ref, ...), custom_call_target="tpu_custom_call" | custom-call | flops 5000000000 | tf_op jit(solution)/shard_map/pallas_call | solution.py:561
  11.7 1.9 %collective-permute-start.3 = (f32[60,8,128]{2,1,0:T(8,128)S(1)}, f32[60,8,128]{2,1,0:T(8,128)S(1)}, u32[]{:S(2)}, u32[]{:S(2)}) collective-permute-start(f32[60,8,128]{2,1,0:T(8,128)S(1)} %get-tuple-element.25), channel_id=1, source_target_pairs={{4,8},{12,16},{20,24},{8,4},{16,12},{24,20},{5,9},{13,17},{21,25},... | collective-permute-start | bytes 737288 | tf_op jit(solution)/shard_map/ppermute | solution.py:570
  13.6 1.7 %collective-permute-start.4 = (f32[60,8,128]{2,1,0:T(8,128)S(1)}, f32[60,8,128]{2,1,0:T(8,128)S(1)}, u32[]{:S(2)}, u32[]{:S(2)}) collective-permute-start(f32[60,8,128]{2,1,0:T(8,128)S(1)} %get-tuple-element.26), channel_id=1, source_target_pairs={{0,4},{8,12},{16,20},{24,28},{4,0},{12,8},{20,16},{28,24},{1,5},{9... | collective-permute-start | bytes 737288 | tf_op jit(solution)/shard_map/ppermute | solution.py:569
  15.3 0.0 copy-done
  15.3 0.0 copy-done.1
  15.3 2.3 %shard_map.57 = (f32[4,3,16,3,8,128]{5,4,3,2,1,0:T(8,128)S(1)}, f32[2,24,48,128]{3,2,1,0:T(8,128)S(1)}, bf16[2,256,256]{2,1,0:T(8,128)(2,1)S(1)}) custom-call(s32[8]{0:T(128)S(1)} %copy-done, f32[22]{0:T(128)S(1)} %copy-done.1, f32[2,3,16,2,8,128]{5,4,3,2,1,0:T(8,128)S(1)} %get-tuple-element.18.own_ref, ...), custom_call_target="tpu_custom_call" | custom-call | flops 2000000000 | tf_op jit(solution)/shard_map/pallas_call | solution.py:573
  17.6 4.2 %collective-permute-done.3.far_ref = f32[60,8,128]{2,1,0:T(8,128)S(1)} collective-permute-done((f32[60,8,128]{2,1,0:T(8,128)S(1)}, f32[60,8,128]{2,1,0:T(8,128)S(1)}, u32[]{:S(2)}, u32[]{:S(2)}) %collective-permute-start.3) | collective-permute-done | bytes 245792 | tf_op jit(solution)/shard_map/ppermute | solution.py:570
  21.8 0.0 collective-permute-done.4.chip_ref
  21.8 0.0 collective-permute-done.2.box_ref
  21.9 3.0 %shard_map.58 = (f32[22,48,256]{2,1,0:T(8,128)}, f32[2,24,48,128]{3,2,1,0:T(8,128)S(1)}) custom-call(s32[8]{0:T(128)S(1)} %copy-done, f32[22]{0:T(128)S(1)} %copy-done.1, f32[2,3,16,2,8,128]{5,4,3,2,1,0:T(8,128)S(1)} %get-tuple-element.18.own_ref, f32[2,2,2,8,128]{4,3,2,1,0:T(8,128)S(1)} %get-tuple-element.19.plane_ref, ...), custom_call_target="tpu_custom_call", output_to_operand_aliasing={{1}: (11, {})} | custom-call | tf_op jit(solution)/shard_map/pallas_call | solution.py:590
Async XLA Ops:
  2.3 7.3 %collective-permute-start = (f32[34,8,128]{2,1,0:T(8,128)S(1)}, f32[34,8,128]{2,1,0:T(8,128)S(1)}, u32[]{:S(2)}, u32[]{:S(2)}) collective-permute-start(f32[34,8,128]{2,1,0:T(8,128)S(1)} %get-tuple-element.20), channel_id=1, source_target_pairs={{1,2},{2,1},{5,6},{6,5},{9,10},{10,9},{13,14},{14,13},{17,18},{18,... | collective-permute-start | bytes 417800 | tf_op jit(solution)/shard_map/ppermute | solution.py:558
  5.7 5.2 %collective-permute-start.1 = (f32[34,8,128]{2,1,0:T(8,128)S(1)}, f32[34,8,128]{2,1,0:T(8,128)S(1)}, u32[]{:S(2)}, u32[]{:S(2)}) collective-permute-start(f32[34,8,128]{2,1,0:T(8,128)S(1)} %get-tuple-element.21), channel_id=1, source_target_pairs={{0,1},{2,3},{1,0},{3,2},{4,5},{6,7},{5,4},{7,6},{8,9},{10,11},{9,8... | collective-permute-start | bytes 417800 | tf_op jit(solution)/shard_map/ppermute | solution.py:559
  5.8 16.0 %collective-permute-start.2 = (f32[96,8,128]{2,1,0:T(8,128)S(1)}, f32[96,8,128]{2,1,0:T(8,128)S(1)}, u32[]{:S(2)}, u32[]{:S(2)}) collective-permute-start(f32[96,8,128]{2,1,0:T(8,128)S(1)} %get-tuple-element.24), channel_id=1, source_target_pairs={{4,0},{8,4},{12,8},{16,12},{20,16},{24,20},{28,24},{5,1},{9,5},{13... | collective-permute-start | bytes 1179656 | tf_op jit(solution)/shard_map/ppermute | solution.py:560
  10.9 4.3 %copy-start = (s32[8]{0:T(128)S(1)}, s32[8]{0:T(128)}, u32[]{:S(2)}) copy-start(s32[8]{0:T(128)} %lengths_ref.3) | copy-start | bytes 100
  10.9 4.3 %copy-start.1 = (f32[22]{0:T(128)S(1)}, f32[22]{0:T(128)}, u32[]{:S(2)}) copy-start(f32[22]{0:T(128)} %factor_ref.3) | copy-start | bytes 268
  11.7 10.1 %collective-permute-start.3 = (f32[60,8,128]{2,1,0:T(8,128)S(1)}, f32[60,8,128]{2,1,0:T(8,128)S(1)}, u32[]{:S(2)}, u32[]{:S(2)}) collective-permute-start(f32[60,8,128]{2,1,0:T(8,128)S(1)} %get-tuple-element.25), channel_id=1, source_target_pairs={{4,8},{12,16},{20,24},{8,4},{16,12},{24,20},{5,9},{13,17},{21,25},... | collective-permute-start | bytes 737288 | tf_op jit(solution)/shard_map/ppermute | solution.py:570
  13.6 8.2 %collective-permute-start.4 = (f32[60,8,128]{2,1,0:T(8,128)S(1)}, f32[60,8,128]{2,1,0:T(8,128)S(1)}, u32[]{:S(2)}, u32[]{:S(2)}) collective-permute-start(f32[60,8,128]{2,1,0:T(8,128)S(1)} %get-tuple-element.26), channel_id=1, source_target_pairs={{0,4},{8,12},{16,20},{24,28},{4,0},{12,8},{20,16},{28,24},{1,5},{9... | collective-permute-start | bytes 737288 | tf_op jit(solution)/shard_map/ppermute | solution.py:569

commit v6 on v5

--- a/solution.py
+++ b/solution.py
@@ -29,20 +29,26 @@
 
 
 def roll(x, shift):
-    return pltpu.roll(x, shift % LANES, 1)
-
-
-def pack_rim(red, black, lane):
-    first = jnp.where(lane < 64, red[0], roll(red[1], 64))
-    first = jnp.where((lane >= 48) & (lane < 64), roll(black[2], 48), first)
-    first = jnp.where(lane >= 112, roll(black[2], 96), first)
-    second = jnp.where(lane < 32, black[0], jnp.where(lane < 64, roll(black[1], 32), roll(red[2], 64)))
+    return pltpu.roll(x, shift % LANES, 1) if shift % LANES else x
+
+
+def pack_rim(red, black, lane, high):
+    red_from, black_from = (LANES - 48, LANES - 32) if high else (0, 0)
+    reds = [roll(x, to - red_from) for x, to in zip(red, (0, 64, 64))]
+    first = jnp.where(lane < 64, reds[0], reds[1])
+    first = jnp.where((lane >= 48) & (lane < 64), roll(black[2], 48 - black_from), first)
+    first = jnp.where(lane >= 112, roll(black[2], 96 - black_from), first)
+    second = jnp.where(lane < 64, roll(black[1], 32 - black_from), reds[2])
+    second = jnp.where(lane < 32, roll(black[0], -black_from), second)
     return first, second
 
 
-def unpack_rim(first, second, lane):
-    black = jnp.where(lane < 16, roll(first, -48), roll(first, -96))
-    return [first, roll(first, -64), roll(second, -64)], [second, roll(second, -32), black]
+def unpack_rim(first, second, lane, high):
+    red_to, black_to = (LANES - 48, LANES - 32) if high else (0, 0)
+    red = [roll(first, red_to), roll(first, red_to - 64), roll(second, red_to - 64)]
+    black = [roll(second, black_to), roll(second, black_to - 32)]
+    black.append(jnp.where(lane < black_to + 16, roll(first, black_to - 48), roll(first, black_to - 96)))
+    return red, black
 
 
 def pack_halo(red, black, lane):
@@ -93,10 +99,15 @@
                 if p < 8:
                     box_ref[(ct * 8 + p) * 2 + j] = red[ct]
                     box_ref[((3 + ct) * 8 + p) * 2 + j] = black[ct]
+                if p in (8, 9):
+                    near = int(p == 8)
+                    box_ref[96 + ct * 6 + EDGE.index((0, near, j))] = red[ct]
+                    if near:
+                        box_ref[96 + ct * 6 + EDGE.index((1, near, j))] = black[ct]
             reds.append(red)
             blacks.append(black)
-        low_rim = pack_rim(reds[0], blacks[0], lane)
-        high_rim = pack_rim([roll(x, 48) for x in reds[1]], [roll(x, 32) for x in blacks[1]], lane)
+        low_rim = pack_rim(reds[0], blacks[0], lane, False)
+        high_rim = pack_rim(reds[1], blacks[1], lane, True)
         for i in range(2):
             first_ref[2 * p + i] = jnp.where(even_group, high_rim[i], low_rim[i])
             second_ref[2 * p + i] = jnp.where(even_group, low_rim[i], high_rim[i])
@@ -116,7 +127,7 @@
         second_ref[2 * half + q] = jnp.where(even_group, low_rim, high_rim)
 
 
-def pack_faces(own_ref, plane_ref, second_ref, first_ref, rim_ref, rim_plane_ref, chip_ref, far_ref):
+def pack_faces(own_ref, plane_ref, first_ref, second_ref, rim_ref, rim_plane_ref, chip_ref, far_ref):
     pairs = own_ref.shape[2]
     lane, _ = lane_places(SUBS)
     low_half = lane < RIM
@@ -127,38 +138,36 @@
         first, second = first_ref[i], second_ref[i]
         return jnp.where(even_group, first, second), jnp.where(even_group, second, first)
 
+    def put(i, to_before, to_after):
+        chip_ref[i] = jnp.where(even_box, to_after, to_before)
+        far_ref[i] = jnp.where(even_box, to_before, to_after)
+
     for p in range(pairs):
         above, below = zip(*[sides(2 * p + i) for i in range(2)])
-        above, below = unpack_rim(*above, lane), unpack_rim(*below, lane)
+        above, below = unpack_rim(*above, lane, False), unpack_rim(*below, lane, True)
         reds, blacks = [], []
         for ct in range(3):
-            reds.append(jnp.where(low_half, above[0][ct], roll(below[0][ct], -48)))
-            blacks.append(jnp.where(low_half, above[1][ct], roll(below[1][ct], -32)))
+            reds.append(jnp.where(low_half, above[0][ct], below[0][ct]))
+            blacks.append(jnp.where(low_half, above[1][ct], below[1][ct]))
             rim_ref[0, ct, p] = reds[ct]
             rim_ref[1, ct, p] = blacks[ct]
         if p < 8:
             for i, part in enumerate(pack_halo(reds, blacks, lane)):
-                chip_ref[4 * p + i] = part
-                far_ref[4 * p + i] = part
+                k = 4 * p + i
+                if k < 18:
+                    colour, near, j = EDGE[k % 6]
+                    put(k, part, own_ref[colour, k // 6, 15 if near else 14, j])
+                else:
+                    put(k, part, part)
     for q in range(2):
         above, below = sides(2 * pairs + q)
         rim_plane_ref[0, q] = jnp.where(low_half, above, roll(below, RIM))
         rim_plane_ref[1, q] = jnp.where(low_half, roll(above, RIM), below)
 
-    def put(i, to_before, to_after):
-        chip_ref[i] = jnp.where(even_box, to_after, to_before)
-        far_ref[i] = jnp.where(even_box, to_before, to_after)
-
-    def piece(colour, ct, p, j):
-        return own_ref[colour, ct, p, j] if j < 2 else rim_ref[colour, ct, p]
-
-    for ct in range(3):
-        for i, (colour, near, j) in enumerate(EDGE):
-            down, up = (8, 15) if near else (9, 14)
-            put(32 + ct * 8 + i, piece(colour, ct, down, j), piece(colour, ct, up, j))
     for colour in range(2):
-        chip_ref[56 + colour] = rim_plane_ref[colour, 0]
-        far_ref[56 + colour] = rim_plane_ref[colour, 0]
+        for ct in range(3):
+            put(32 + ct * 2 + colour, rim_ref[colour, ct, 8], rim_ref[colour, ct, 15])
+        put(38 + colour, rim_plane_ref[colour, 0], rim_plane_ref[colour, 0])
     for colour in range(2):
         for near in range(2):
             for j in range(3):
@@ -168,13 +177,13 @@
                     for k in (down, up)
                 ]
                 k = colour * 6 + near * 3 + j
-                chip_ref[58 + k // 8, k % 8 : k % 8 + 1] = jnp.where(even_box, rows[1], rows[0])
-                far_ref[58 + k // 8, k % 8 : k % 8 + 1] = jnp.where(even_box, rows[0], rows[1])
-    chip_ref[59, 4:8] = jnp.zeros((4, LANES), F32)
-    far_ref[59, 4:8] = jnp.zeros((4, LANES), F32)
-
-
-EDGE = [(0, 1, 0), (0, 1, 1), (0, 1, 2), (0, 0, 0), (0, 0, 1), (1, 1, 0), (1, 1, 1), (1, 1, 2)]
+                chip_ref[40 + k // 8, k % 8 : k % 8 + 1] = jnp.where(even_box, rows[1], rows[0])
+                far_ref[40 + k // 8, k % 8 : k % 8 + 1] = jnp.where(even_box, rows[0], rows[1])
+    chip_ref[41, 4:8] = jnp.zeros((4, LANES), F32)
+    far_ref[41, 4:8] = jnp.zeros((4, LANES), F32)
+
+
+EDGE = [(0, 1, 0), (0, 1, 1), (0, 0, 0), (0, 0, 1), (1, 1, 0), (1, 1, 1), (0, 1, 2), (1, 1, 2)]
 
 
 def shift_matrices():
@@ -423,8 +432,8 @@
     def from_before(i):
         return jnp.where(even_box, far_ref[i], chip_ref[i])
 
-    edges = [jnp.concatenate([get(58), get(59)], 0) for get in (from_after, from_before)]
-    flat_box = box_ref.reshape(96 * SUBS, LANES)
+    edges = [jnp.concatenate([get(40), get(41)], 0) for get in (from_after, from_before)]
+    flat_box = box_ref.reshape(114 * SUBS, LANES)
     conduct = []
     for colour in range(2):
         planes = []
@@ -434,7 +443,7 @@
                 row = (((3 * colour + 2) * 8) * 2 + j) * SUBS + 7
                 box = flat_box[pl.ds(row, SUBS, stride=2 * SUBS)]
             else:
-                box = from_after(56 + colour)
+                box = from_after(38 + colour)
             edge = jnp.zeros((SUBS, LANES), F32)
             for place_at, side, near in ((0, 0, 1), (1, 0, 0), (6, 1, 0), (7, 1, 1)):
                 k = colour * 6 + near * 3 + j
@@ -449,9 +458,12 @@
         for ct in range(3):
             box_rim_ref[0, ct, p], box_rim_ref[1, ct, p] = reds[ct], blacks[ct]
     for ct in range(3):
-        for i in range(8):
-            edge_ref[0, ct, i] = from_before(32 + ct * 8 + i)
-            edge_ref[1, ct, i] = from_after(32 + ct * 8 + i)
+        for i in range(6):
+            edge_ref[0, ct, i] = from_before(ct * 6 + i)
+            edge_ref[1, ct, i] = box_ref[96 + ct * 6 + i]
+        for colour in range(2):
+            edge_ref[0, ct, 6 + colour] = from_before(32 + ct * 2 + colour)
+            edge_ref[1, ct, 6 + colour] = from_after(32 + ct * 2 + colour)
 
     def source_of(q):
         if 2 <= q < 18:
@@ -548,7 +560,7 @@
             real(2, 2, 2),
             real(2 * pairs + 2),
             real(2 * pairs + 2),
-            real(96),
+            real(114),
         ),
         in_specs=in_vmem(1),
         out_specs=tuple(in_vmem(5)),
@@ -560,12 +572,12 @@
     box = lax.ppermute(box, "boxes", [(i + 1, i) for i in range(boxes - 1)])
     rim, rim_plane, chip, far = pl.pallas_call(
         pack_faces,
-        out_shape=(real(2, 3, pairs), real(2, 2), real(60), real(60)),
+        out_shape=(real(2, 3, pairs), real(2, 2), real(42), real(42)),
         in_specs=in_vmem(4),
         out_specs=tuple(in_vmem(4)),
         cost_estimate=pl.CostEstimate(flops=5_000_000_000, bytes_accessed=0, transcendentals=0),
         compiler_params=params,
-    )(own, plane, second, first)
+    )(own, plane, first, second)
     chip = lax.ppermute(chip, "boxes", swap_pairs(boxes, 0))
     far = lax.ppermute(far, "boxes", swap_pairs(boxes, 1))
     smem = pl.BlockSpec(memory_space=pltpu.SMEM)

time: 25 us -> 24.2 us (0.968)
  the two profiles are of different devices: /device:TPU:12 before, /device:TPU:11 now
where the time goes in v6:
time: 24.2 us; the launch traced here: 23.8 us
  starting transfers between devices  12.2 us (50%)
  Pallas kernels  6.39 us (26%)
  waiting for transfers between devices  3.93 us (16%)
  other arithmetic  1.21 us (5%)
    ppermute x1, starting transfers between devices, on_device(): far = lax.ppermute(far, 'boxes', swap_pairs(boxes, 1))  4.42 us
    ppermute x1, starting transfers between devices, on_device(): second = lax.ppermute(second, 'grp', swap_pairs(groups, 1))  4.32 us
    ppermute x1, waiting for transfers between devices, on_device(): far = lax.ppermute(far, 'boxes', swap_pairs(boxes, 1))  3.92 us
    ppermute x1, starting transfers between devices, on_device(): box = lax.ppermute(box, 'boxes', [(i + 1, i) for i in range(boxes - 1)])  3.14 us
    pallas_call x1, Pallas kernels, on_device(): pl.pallas_call(smooth_outer, out_shape=(jax.ShapeDtypeStruct((channels, M...  2.97 us
    pallas_call x1, Pallas kernels, on_device(): pl.pallas_call(smooth_inner, out_shape=(real(4, 3, pairs, 3), jax.ShapeDt...  2.34 us
    concatenate x1, other arithmetic, on_device(): jnp.concatenate([sources, absorption[None], conductance[None]])  1.21 us
    pallas_call x1, Pallas kernels, on_device(): pl.pallas_call(pack_rims, out_shape=(real(2, 3, pairs, 2), real(2, 2, 2),...  0.59 us
  transfers between devices with their start and end apart: 5, of which 1 were waited for; matrix products, arithmetic and copies ran while one was open for 0% of the time, Pallas kernels for 12%

profile of v6, /device:TPU:11, one launch (start us, length us, event | category | flops | bytes accessed | tf_op | source)
XLA Modules:
  0.0 23.8 jit_solution(17557128810070619783)
XLA Ops:
  0.0 1.2 %pad_maximum_fusion.src_ref = f32[24,32,256]{2,1,0:T(8,128)S(1)} fusion(f32[1,32,256]{2,1,0:T(8,128)} %bitcast.2, f32[1,32,256]{2,1,0:T(8,128)} %bitcast.3, f32[22,32,256]{2,1,0:T(8,128)} %param.5), kind=kLoop, calls=%fused_computation | loop fusion | flops 393216 | bytes 1572864 | tf_op jit(solution)/shard_map/concatenate | solution.py:569
  1.2 0.6 %shard_map.55 = (f32[2,3,16,2,8,128]{5,4,3,2,1,0:T(8,128)S(1)}, f32[2,2,2,8,128]{4,3,2,1,0:T(8,128)S(1)}, f32[34,8,128]{2,1,0:T(8,128)S(1)}, f32[34,8,128]{2,1,0:T(8,128)S(1)}, f32[114,8,128]{2,1,0:T(8,128)S(1)}) custom-call(f32[24,32,256]{2,1,0:T(8,128)S(1)} %pad_maximum_fusion.src_ref), custom_call_target="tpu_custom_call" | custom-call | tf_op jit(solution)/shard_map/pallas_call | solution.py:556
  1.8 0.2 collective-permute-start
  2.1 4.3 %collective-permute-start.1 = (f32[34,8,128]{2,1,0:T(8,128)S(1)}, f32[34,8,128]{2,1,0:T(8,128)S(1)}, u32[]{:S(2)}, u32[]{:S(2)}) collective-permute-start(f32[34,8,128]{2,1,0:T(8,128)S(1)} %get-tuple-element.21), channel_id=1, source_target_pairs={{1,2},{2,1},{5,6},{6,5},{9,10},{10,9},{13,14},{14,13},{17,18},{18,... | collective-permute-start | bytes 417800 | tf_op jit(solution)/shard_map/ppermute | solution.py:570
  6.4 3.1 %collective-permute-start.2 = (f32[114,8,128]{2,1,0:T(8,128)S(1)}, f32[114,8,128]{2,1,0:T(8,128)S(1)}, u32[]{:S(2)}, u32[]{:S(2)}) collective-permute-start(f32[114,8,128]{2,1,0:T(8,128)S(1)} %get-tuple-element.24), channel_id=1, source_target_pairs={{4,0},{8,4},{12,8},{16,12},{20,16},{24,20},{28,24},{5,1},{9,5},{13... | collective-permute-start | bytes 1400840 | tf_op jit(solution)/shard_map/ppermute | solution.py:572
  9.5 0.0 collective-permute-done.first_ref
  9.5 0.0 collective-permute-done.1.second_ref
  9.6 0.0 copy-start
  9.6 0.0 copy-start.1
  9.6 0.5 %shard_map.56 = (f32[2,3,16,8,128]{4,3,2,1,0:T(8,128)S(1)}, f32[2,2,8,128]{3,2,1,0:T(8,128)S(1)}, f32[42,8,128]{2,1,0:T(8,128)S(1)}, f32[42,8,128]{2,1,0:T(8,128)S(1)}) custom-call(f32[2,3,16,2,8,128]{5,4,3,2,1,0:T(8,128)S(1)} %get-tuple-element.18.own_ref, f32[2,2,2,8,128]{4,3,2,1,0:T(8,128)S(1)} %get-tuple-element.19.plane_ref, ...), custom_call_target="tpu_custom_call" | custom-call | flops 5000000000 | tf_op jit(solution)/shard_map/pallas_call | solution.py:573
  10.1 4.4 %collective-permute-start.3 = (f32[42,8,128]{2,1,0:T(8,128)S(1)}, f32[42,8,128]{2,1,0:T(8,128)S(1)}, u32[]{:S(2)}, u32[]{:S(2)}) collective-permute-start(f32[42,8,128]{2,1,0:T(8,128)S(1)} %get-tuple-element.25), channel_id=1, source_target_pairs={{4,8},{12,16},{20,24},{8,4},{16,12},{24,20},{5,9},{13,17},{21,25},... | collective-permute-start | bytes 516104 | tf_op jit(solution)/shard_map/ppermute | solution.py:582
  14.5 0.1 collective-permute-start.4
  14.6 0.0 copy-done
  14.6 0.0 copy-done.1
  14.6 2.3 %shard_map.57 = (f32[4,3,16,3,8,128]{5,4,3,2,1,0:T(8,128)S(1)}, f32[2,24,48,128]{3,2,1,0:T(8,128)S(1)}, bf16[2,256,256]{2,1,0:T(8,128)(2,1)S(1)}) custom-call(s32[8]{0:T(128)S(1)} %copy-done, f32[22]{0:T(128)S(1)} %copy-done.1, f32[2,3,16,2,8,128]{5,4,3,2,1,0:T(8,128)S(1)} %get-tuple-element.18.own_ref, ...), custom_call_target="tpu_custom_call" | custom-call | flops 2000000000 | tf_op jit(solution)/shard_map/pallas_call | solution.py:585
  16.9 3.9 %collective-permute-done.3.far_ref = f32[42,8,128]{2,1,0:T(8,128)S(1)} collective-permute-done((f32[42,8,128]{2,1,0:T(8,128)S(1)}, f32[42,8,128]{2,1,0:T(8,128)S(1)}, u32[]{:S(2)}, u32[]{:S(2)}) %collective-permute-start.3) | collective-permute-done | bytes 172064 | tf_op jit(solution)/shard_map/ppermute | solution.py:582
  20.9 0.0 collective-permute-done.4.chip_ref
  20.9 0.0 collective-permute-done.2.box_ref
  20.9 3.0 %shard_map.58 = (f32[22,48,256]{2,1,0:T(8,128)}, f32[2,24,48,128]{3,2,1,0:T(8,128)S(1)}) custom-call(s32[8]{0:T(128)S(1)} %copy-done, f32[22]{0:T(128)S(1)} %copy-done.1, f32[2,3,16,2,8,128]{5,4,3,2,1,0:T(8,128)S(1)} %get-tuple-element.18.own_ref, f32[2,2,2,8,128]{4,3,2,1,0:T(8,128)S(1)} %get-tuple-element.19.plane_ref, ...), custom_call_target="tpu_custom_call", output_to_operand_aliasing={{1}: (11, {})} | custom-call | tf_op jit(solution)/shard_map/pallas_call | solution.py:602
Async XLA Ops:
  1.8 7.7 %collective-permute-start = (f32[34,8,128]{2,1,0:T(8,128)S(1)}, f32[34,8,128]{2,1,0:T(8,128)S(1)}, u32[]{:S(2)}, u32[]{:S(2)}) collective-permute-start(f32[34,8,128]{2,1,0:T(8,128)S(1)} %get-tuple-element.20), channel_id=1, source_target_pairs={{0,1},{2,3},{1,0},{3,2},{4,5},{6,7},{5,4},{7,6},{8,9},{10,11},{9,8... | collective-permute-start | bytes 417800 | tf_op jit(solution)/shard_map/ppermute | solution.py:571
  2.1 7.5 %collective-permute-start.1 = (f32[34,8,128]{2,1,0:T(8,128)S(1)}, f32[34,8,128]{2,1,0:T(8,128)S(1)}, u32[]{:S(2)}, u32[]{:S(2)}) collective-permute-start(f32[34,8,128]{2,1,0:T(8,128)S(1)} %get-tuple-element.21), channel_id=1, source_target_pairs={{1,2},{2,1},{5,6},{6,5},{9,10},{10,9},{13,14},{14,13},{17,18},{18,... | collective-permute-start | bytes 417800 | tf_op jit(solution)/shard_map/ppermute | solution.py:570
  6.4 14.5 %collective-permute-start.2 = (f32[114,8,128]{2,1,0:T(8,128)S(1)}, f32[114,8,128]{2,1,0:T(8,128)S(1)}, u32[]{:S(2)}, u32[]{:S(2)}) collective-permute-start(f32[114,8,128]{2,1,0:T(8,128)S(1)} %get-tuple-element.24), channel_id=1, source_target_pairs={{4,0},{8,4},{12,8},{16,12},{20,16},{24,20},{28,24},{5,1},{9,5},{13... | collective-permute-start | bytes 1400840 | tf_op jit(solution)/shard_map/ppermute | solution.py:572
  9.6 5.0 %copy-start = (s32[8]{0:T(128)S(1)}, s32[8]{0:T(128)}, u32[]{:S(2)}) copy-start(s32[8]{0:T(128)} %lengths_ref.3) | copy-start | bytes 100
  9.6 5.0 %copy-start.1 = (f32[22]{0:T(128)S(1)}, f32[22]{0:T(128)}, u32[]{:S(2)}) copy-start(f32[22]{0:T(128)} %factor_ref.3) | copy-start | bytes 268
  10.1 10.8 %collective-permute-start.3 = (f32[42,8,128]{2,1,0:T(8,128)S(1)}, f32[42,8,128]{2,1,0:T(8,128)S(1)}, u32[]{:S(2)}, u32[]{:S(2)}) collective-permute-start(f32[42,8,128]{2,1,0:T(8,128)S(1)} %get-tuple-element.25), channel_id=1, source_target_pairs={{4,8},{12,16},{20,24},{8,4},{16,12},{24,20},{5,9},{13,17},{21,25},... | collective-permute-start | bytes 516104 | tf_op jit(solution)/shard_map/ppermute | solution.py:582
  14.5 6.4 %collective-permute-start.4 = (f32[42,8,128]{2,1,0:T(8,128)S(1)}, f32[42,8,128]{2,1,0:T(8,128)S(1)}, u32[]{:S(2)}, u32[]{:S(2)}) collective-permute-start(f32[42,8,128]{2,1,0:T(8,128)S(1)} %get-tuple-element.26), channel_id=1, source_target_pairs={{0,4},{8,12},{16,20},{24,28},{4,0},{12,8},{20,16},{28,24},{1,5},{9... | collective-permute-start | bytes 516104 | tf_op jit(solution)/shard_map/ppermute | solution.py:581

commit v7 on v6

--- a/solution.py
+++ b/solution.py
@@ -17,9 +17,21 @@
 F32 = jnp.float32
 
 
-def swap_pairs(count, first):
-    lower = range(first, count - 1, 2)
-    return [(i, i + 1) for i in lower] + [(i + 1, i) for i in lower]
+def swap_pairs(boxes, groups, along_boxes, first):
+    count, other = (boxes, groups) if along_boxes else (groups, boxes)
+    pairs = []
+    for i in range(count):
+        k = i + 1 if (i - first) % 2 == 0 else i - 1
+        for m in range(other):
+            here, there = (i, m), (k, m)
+            if not 0 <= k < count:
+                there = (i, m ^ 1)
+                if (m ^ 1) >= other:
+                    continue
+            if not along_boxes:
+                here, there = here[::-1], there[::-1]
+            pairs.append(tuple(b * groups + g for b, g in (here, there)))
+    return pairs
 
 
 def lane_places(rows):
@@ -131,7 +143,8 @@
     pairs = own_ref.shape[2]
     lane, _ = lane_places(SUBS)
     low_half = lane < RIM
-    even_group = lax.axis_index("grp") % 2 == 0
+    group = lax.axis_index("grp")
+    even_group = group % 2 == 0
     even_box = lax.axis_index("boxes") % 2 == 0
 
     def sides(i):
@@ -161,6 +174,8 @@
                     put(k, part, part)
     for q in range(2):
         above, below = sides(2 * pairs + q)
+        above = jnp.where(group == lax.axis_size("grp") - 1, 0.0, above)
+        below = jnp.where(group == 0, 0.0, below)
         rim_plane_ref[0, q] = jnp.where(low_half, above, roll(below, RIM))
         rim_plane_ref[1, q] = jnp.where(low_half, roll(above, RIM), below)
 
@@ -432,7 +447,10 @@
     def from_before(i):
         return jnp.where(even_box, far_ref[i], chip_ref[i])
 
-    edges = [jnp.concatenate([get(40), get(41)], 0) for get in (from_after, from_before)]
+    edges = [
+        jnp.where(missing, 0.0, jnp.concatenate([get(40), get(41)], 0))
+        for get, missing in ((from_after, last_box), (from_before, position == 0))
+    ]
     flat_box = box_ref.reshape(114 * SUBS, LANES)
     conduct = []
     for colour in range(2):
@@ -444,6 +462,7 @@
                 box = flat_box[pl.ds(row, SUBS, stride=2 * SUBS)]
             else:
                 box = from_after(38 + colour)
+            box = jnp.where(last_box, 0.0, box)
             edge = jnp.zeros((SUBS, LANES), F32)
             for place_at, side, near in ((0, 0, 1), (1, 0, 0), (6, 1, 0), (7, 1, 1)):
                 k = colour * 6 + near * 3 + j
@@ -567,19 +586,18 @@
         scratch_shapes=[pltpu.VMEM((2, channels + 2, planes, LANES), F32)],
         compiler_params=params,
     )(jnp.concatenate([sources, absorption[None], conductance[None]]))
-    second = lax.ppermute(second, "grp", swap_pairs(groups, 1))
-    first = lax.ppermute(first, "grp", swap_pairs(groups, 0))
-    box = lax.ppermute(box, "boxes", [(i + 1, i) for i in range(boxes - 1)])
+    second = lax.ppermute(second, ("boxes", "grp"), swap_pairs(boxes, groups, False, 1))
+    first = lax.ppermute(first, ("boxes", "grp"), swap_pairs(boxes, groups, False, 0))
+    box = lax.ppermute(box, "boxes", [((i + 1) % boxes, i) for i in range(boxes)])
     rim, rim_plane, chip, far = pl.pallas_call(
         pack_faces,
         out_shape=(real(2, 3, pairs), real(2, 2), real(42), real(42)),
         in_specs=in_vmem(4),
         out_specs=tuple(in_vmem(4)),
-        cost_estimate=pl.CostEstimate(flops=5_000_000_000, bytes_accessed=0, transcendentals=0),
         compiler_params=params,
     )(own, plane, first, second)
-    chip = lax.ppermute(chip, "boxes", swap_pairs(boxes, 0))
-    far = lax.ppermute(far, "boxes", swap_pairs(boxes, 1))
+    chip = lax.ppermute(chip, ("boxes", "grp"), swap_pairs(boxes, groups, True, 0))
+    far = lax.ppermute(far, ("boxes", "grp"), swap_pairs(boxes, groups, True, 1))
     smem = pl.BlockSpec(memory_space=pltpu.SMEM)
     placed_shape = (2, 3 * SUBS, MOST * BOX_X, LANES)
     inner, placed, shift = pl.pallas_call(

time: 24.2 us -> 20.4 us (0.84)
  the two profiles are of different devices: /device:TPU:11 before, /device:TPU:0 now
where the time goes in v7:
time: 20.4 us; the launch traced here: 20.3 us
  starting transfers between devices  7.73 us (38%)
  Pallas kernels  6.72 us (33%)
  waiting for transfers between devices  4.55 us (22%)
  other arithmetic  1.21 us (6%)
    ppermute x1, waiting for transfers between devices, on_device(): lax.ppermute(first, ('boxes', 'grp'), swap_pairs(boxes, groups, False, 0))  3.48 us
    ppermute x1, starting transfers between devices, on_device(): lax.ppermute(box, 'boxes', [((i + 1) % boxes, i) for i in range(boxes)])  3.39 us
    pallas_call x1, Pallas kernels, on_device(): pl.pallas_call(smooth_outer, out_shape=(jax.ShapeDtypeStruct((channels, M...  3.35 us
    ppermute x1, starting transfers between devices, on_device(): lax.ppermute(far, ('boxes', 'grp'), swap_pairs(boxes, groups, True, 1))  2.76 us
    pallas_call x1, Pallas kernels, on_device(): pl.pallas_call(smooth_inner, out_shape=(real(4, 3, pairs, 3), jax.ShapeDt...  2.3 us
    ppermute x1, starting transfers between devices, on_device(): lax.ppermute(first, ('boxes', 'grp'), swap_pairs(boxes, groups, False, 0))  1.58 us
    concatenate x1, other arithmetic, on_device(): jnp.concatenate([sources, absorption[None], conductance[None]])  1.21 us
    ppermute x1, waiting for transfers between devices, on_device(): lax.ppermute(far, ('boxes', 'grp'), swap_pairs(boxes, groups, True, 1))  1.07 us
  transfers between devices with their start and end apart: 5, of which 2 were waited for; matrix products, arithmetic and copies ran while one was open for 0% of the time, Pallas kernels for 14%

profile of v7, /device:TPU:0, one launch (start us, length us, event | category | flops | bytes accessed | tf_op | source)
XLA Modules:
  0.0 20.3 jit_solution(9784507673014170004)
XLA Ops:
  0.0 1.2 %pad_maximum_fusion.src_ref = f32[24,32,256]{2,1,0:T(8,128)S(1)} fusion(f32[1,32,256]{2,1,0:T(8,128)} %bitcast.2, f32[1,32,256]{2,1,0:T(8,128)} %bitcast.3, f32[22,32,256]{2,1,0:T(8,128)} %param.5), kind=kLoop, calls=%fused_computation | loop fusion | flops 393216 | bytes 1572864 | tf_op jit(solution)/shard_map/concatenate | solution.py:588
  1.2 0.0 copy-start
  1.2 0.0 copy-start.1
  1.2 0.6 %shard_map.55 = (f32[2,3,16,2,8,128]{5,4,3,2,1,0:T(8,128)S(1)}, f32[2,2,2,8,128]{4,3,2,1,0:T(8,128)S(1)}, f32[34,8,128]{2,1,0:T(8,128)S(1)}, f32[34,8,128]{2,1,0:T(8,128)S(1)}, f32[114,8,128]{2,1,0:T(8,128)S(1)}) custom-call(f32[24,32,256]{2,1,0:T(8,128)S(1)} %pad_maximum_fusion.src_ref), custom_call_target="tpu_custom_call" | custom-call | tf_op jit(solution)/shard_map/pallas_call | solution.py:575
  1.8 3.4 %collective-permute-start.2 = (f32[114,8,128]{2,1,0:T(8,128)S(1)}, f32[114,8,128]{2,1,0:T(8,128)S(1)}, u32[]{:S(2)}, u32[]{:S(2)}) collective-permute-start(f32[114,8,128]{2,1,0:T(8,128)S(1)} %get-tuple-element.24), channel_id=1, source_target_pairs={{4,0},{8,4},{12,8},{16,12},{20,16},{24,20},{28,24},{0,28},{5,1},{9... | collective-permute-start | bytes 1400840 | tf_op jit(solution)/shard_map/ppermute | solution.py:591
  5.2 1.6 %collective-permute-start = (f32[34,8,128]{2,1,0:T(8,128)S(1)}, f32[34,8,128]{2,1,0:T(8,128)S(1)}, u32[]{:S(2)}, u32[]{:S(2)}) collective-permute-start(f32[34,8,128]{2,1,0:T(8,128)S(1)} %get-tuple-element.20), channel_id=1, source_target_pairs={{0,1},{4,5},{8,9},{12,13},{16,17},{20,21},{24,25},{28,29},{1,0},{5... | collective-permute-start | bytes 417800 | tf_op jit(solution)/shard_map/ppermute | solution.py:590
  6.8 0.0 collective-permute-start.1
  6.8 3.5 %collective-permute-done.first_ref = f32[34,8,128]{2,1,0:T(8,128)S(1)} collective-permute-done((f32[34,8,128]{2,1,0:T(8,128)S(1)}, f32[34,8,128]{2,1,0:T(8,128)S(1)}, u32[]{:S(2)}, u32[]{:S(2)}) %collective-permute-start) | collective-permute-done | bytes 139296 | tf_op jit(solution)/shard_map/ppermute | solution.py:590
  10.3 0.0 collective-permute-done.1.second_ref
  10.3 0.5 %shard_map.56 = (f32[2,3,16,8,128]{4,3,2,1,0:T(8,128)S(1)}, f32[2,2,8,128]{3,2,1,0:T(8,128)S(1)}, f32[42,8,128]{2,1,0:T(8,128)S(1)}, f32[42,8,128]{2,1,0:T(8,128)S(1)}) custom-call(f32[2,3,16,2,8,128]{5,4,3,2,1,0:T(8,128)S(1)} %get-tuple-element.18.own_ref, f32[2,2,2,8,128]{4,3,2,1,0:T(8,128)S(1)} %get-tuple-element.19.plane_ref, ...), custom_call_target="tpu_custom_call" | custom-call | tf_op jit(solution)/shard_map/pallas_call | solution.py:592
  10.8 2.8 %collective-permute-start.3 = (f32[42,8,128]{2,1,0:T(8,128)S(1)}, f32[42,8,128]{2,1,0:T(8,128)S(1)}, u32[]{:S(2)}, u32[]{:S(2)}) collective-permute-start(f32[42,8,128]{2,1,0:T(8,128)S(1)} %get-tuple-element.25), channel_id=1, source_target_pairs={{0,1},{1,0},{2,3},{3,2},{4,8},{5,9},{6,10},{7,11},{8,4},{9,5},{10,... | collective-permute-start | bytes 516104 | tf_op jit(solution)/shard_map/ppermute | solution.py:600
  13.5 0.0 collective-permute-start.4
  13.5 0.0 copy-done
  13.5 0.0 copy-done.1
  13.6 2.3 %shard_map.57 = (f32[4,3,16,3,8,128]{5,4,3,2,1,0:T(8,128)S(1)}, f32[2,24,48,128]{3,2,1,0:T(8,128)S(1)}, bf16[2,256,256]{2,1,0:T(8,128)(2,1)S(1)}) custom-call(s32[8]{0:T(128)S(1)} %copy-done, f32[22]{0:T(128)S(1)} %copy-done.1, f32[2,3,16,2,8,128]{5,4,3,2,1,0:T(8,128)S(1)} %get-tuple-element.18.own_ref, ...), custom_call_target="tpu_custom_call" | custom-call | flops 2000000000 | tf_op jit(solution)/shard_map/pallas_call | solution.py:603
  15.9 1.1 %collective-permute-done.3.far_ref = f32[42,8,128]{2,1,0:T(8,128)S(1)} collective-permute-done((f32[42,8,128]{2,1,0:T(8,128)S(1)}, f32[42,8,128]{2,1,0:T(8,128)S(1)}, u32[]{:S(2)}, u32[]{:S(2)}) %collective-permute-start.3) | collective-permute-done | bytes 172064 | tf_op jit(solution)/shard_map/ppermute | solution.py:600
  16.9 0.0 collective-permute-done.4.chip_ref
  16.9 0.0 collective-permute-done.2.box_ref
  16.9 3.3 %shard_map.58 = (f32[22,48,256]{2,1,0:T(8,128)}, f32[2,24,48,128]{3,2,1,0:T(8,128)S(1)}) custom-call(s32[8]{0:T(128)S(1)} %copy-done, f32[22]{0:T(128)S(1)} %copy-done.1, f32[2,3,16,2,8,128]{5,4,3,2,1,0:T(8,128)S(1)} %get-tuple-element.18.own_ref, f32[2,2,2,8,128]{4,3,2,1,0:T(8,128)S(1)} %get-tuple-element.19.plane_ref, ...), custom_call_target="tpu_custom_call", output_to_operand_aliasing={{1}: (11, {})} | custom-call | tf_op jit(solution)/shard_map/pallas_call | solution.py:620
Async XLA Ops:
  1.2 12.3 %copy-start = (s32[8]{0:T(128)S(1)}, s32[8]{0:T(128)}, u32[]{:S(2)}) copy-start(s32[8]{0:T(128)} %lengths_ref.3) | copy-start | bytes 100
  1.2 12.3 %copy-start.1 = (f32[22]{0:T(128)S(1)}, f32[22]{0:T(128)}, u32[]{:S(2)}) copy-start(f32[22]{0:T(128)} %factor_ref.3) | copy-start | bytes 268
  1.8 15.1 %collective-permute-start.2 = (f32[114,8,128]{2,1,0:T(8,128)S(1)}, f32[114,8,128]{2,1,0:T(8,128)S(1)}, u32[]{:S(2)}, u32[]{:S(2)}) collective-permute-start(f32[114,8,128]{2,1,0:T(8,128)S(1)} %get-tuple-element.24), channel_id=1, source_target_pairs={{4,0},{8,4},{12,8},{16,12},{20,16},{24,20},{28,24},{0,28},{5,1},{9... | collective-permute-start | bytes 1400840 | tf_op jit(solution)/shard_map/ppermute | solution.py:591
  5.2 5.1 %collective-permute-start = (f32[34,8,128]{2,1,0:T(8,128)S(1)}, f32[34,8,128]{2,1,0:T(8,128)S(1)}, u32[]{:S(2)}, u32[]{:S(2)}) collective-permute-start(f32[34,8,128]{2,1,0:T(8,128)S(1)} %get-tuple-element.20), channel_id=1, source_target_pairs={{0,1},{4,5},{8,9},{12,13},{16,17},{20,21},{24,25},{28,29},{1,0},{5... | collective-permute-start | bytes 417800 | tf_op jit(solution)/shard_map/ppermute | solution.py:590
  6.8 3.5 %collective-permute-start.1 = (f32[34,8,128]{2,1,0:T(8,128)S(1)}, f32[34,8,128]{2,1,0:T(8,128)S(1)}, u32[]{:S(2)}, u32[]{:S(2)}) collective-permute-start(f32[34,8,128]{2,1,0:T(8,128)S(1)} %get-tuple-element.21), channel_id=1, source_target_pairs={{0,4},{4,0},{8,12},{12,8},{16,20},{20,16},{24,28},{28,24},{1,2},{5... | collective-permute-start | bytes 417800 | tf_op jit(solution)/shard_map/ppermute | solution.py:589
  10.8 6.2 %collective-permute-start.3 = (f32[42,8,128]{2,1,0:T(8,128)S(1)}, f32[42,8,128]{2,1,0:T(8,128)S(1)}, u32[]{:S(2)}, u32[]{:S(2)}) collective-permute-start(f32[42,8,128]{2,1,0:T(8,128)S(1)} %get-tuple-element.25), channel_id=1, source_target_pairs={{0,1},{1,0},{2,3},{3,2},{4,8},{5,9},{6,10},{7,11},{8,4},{9,5},{10,... | collective-permute-start | bytes 516104 | tf_op jit(solution)/shard_map/ppermute | solution.py:600
  13.5 3.4 %collective-permute-start.4 = (f32[42,8,128]{2,1,0:T(8,128)S(1)}, f32[42,8,128]{2,1,0:T(8,128)S(1)}, u32[]{:S(2)}, u32[]{:S(2)}) collective-permute-start(f32[42,8,128]{2,1,0:T(8,128)S(1)} %get-tuple-element.26), channel_id=1, source_target_pairs={{0,4},{1,5},{2,6},{3,7},{4,0},{5,1},{6,2},{7,3},{8,12},{9,13},{10,... | collective-permute-start | bytes 516104 | tf_op jit(solution)/shard_map/ppermute | solution.py:599

commit v8 on v7

--- a/solution.py
+++ b/solution.py
@@ -81,7 +81,7 @@
 
 def pack_rims(
     src_ref,
-    own_ref, plane_ref, first_ref, second_ref, box_ref,
+    own_ref, plane_ref, first_ref, second_ref, third_ref, box_ref,
     tiles_ref,
 ):
     layers, planes, _ = src_ref.shape
@@ -122,6 +122,7 @@
         high_rim = pack_rim(reds[1], blacks[1], lane, True)
         for i in range(2):
             first_ref[2 * p + i] = jnp.where(even_group, high_rim[i], low_rim[i])
+            third_ref[2 * p + i] = jnp.where(even_group, high_rim[i], low_rim[i])
             second_ref[2 * p + i] = jnp.where(even_group, low_rim[i], high_rim[i])
 
     for q in range(2):
@@ -136,24 +137,21 @@
         low_rim = jnp.where(lane < RIM, compact[0][0], roll(compact[0][1], RIM))
         high_rim = jnp.where(lane < RIM, roll(compact[1][0], RIM), compact[1][1])
         first_ref[2 * half + q] = jnp.where(even_group, high_rim, low_rim)
+        third_ref[2 * half + q] = jnp.where(even_group, high_rim, low_rim)
         second_ref[2 * half + q] = jnp.where(even_group, low_rim, high_rim)
 
 
-def pack_faces(own_ref, plane_ref, first_ref, second_ref, rim_ref, rim_plane_ref, chip_ref, far_ref):
+def pack_faces(own_ref, plane_ref, first_ref, second_ref, third_ref, rim_ref, rim_plane_ref, down_ref, up_ref):
     pairs = own_ref.shape[2]
     lane, _ = lane_places(SUBS)
     low_half = lane < RIM
     group = lax.axis_index("grp")
     even_group = group % 2 == 0
-    even_box = lax.axis_index("boxes") % 2 == 0
+    early = group // 2 % 2 == 0
 
     def sides(i):
-        first, second = first_ref[i], second_ref[i]
+        first, second = jnp.where(early, first_ref[i], third_ref[i]), second_ref[i]
         return jnp.where(even_group, first, second), jnp.where(even_group, second, first)
-
-    def put(i, to_before, to_after):
-        chip_ref[i] = jnp.where(even_box, to_after, to_before)
-        far_ref[i] = jnp.where(even_box, to_before, to_after)
 
     for p in range(pairs):
         above, below = zip(*[sides(2 * p + i) for i in range(2)])
@@ -166,12 +164,7 @@
             rim_ref[1, ct, p] = blacks[ct]
         if p < 8:
             for i, part in enumerate(pack_halo(reds, blacks, lane)):
-                k = 4 * p + i
-                if k < 18:
-                    colour, near, j = EDGE[k % 6]
-                    put(k, part, own_ref[colour, k // 6, 15 if near else 14, j])
-                else:
-                    put(k, part, part)
+                down_ref[4 * p + i] = part
     for q in range(2):
         above, below = sides(2 * pairs + q)
         above = jnp.where(group == lax.axis_size("grp") - 1, 0.0, above)
@@ -181,8 +174,12 @@
 
     for colour in range(2):
         for ct in range(3):
-            put(32 + ct * 2 + colour, rim_ref[colour, ct, 8], rim_ref[colour, ct, 15])
-        put(38 + colour, rim_plane_ref[colour, 0], rim_plane_ref[colour, 0])
+            down_ref[32 + ct * 2 + colour] = rim_ref[colour, ct, 8]
+            up_ref[18 + ct * 2 + colour] = rim_ref[colour, ct, 15]
+        down_ref[38 + colour] = rim_plane_ref[colour, 0]
+    for ct in range(3):
+        for i, (colour, near, j) in enumerate(EDGE[:6]):
+            up_ref[ct * 6 + i] = own_ref[colour, ct, 15 if near else 14, j]
     for colour in range(2):
         for near in range(2):
             for j in range(3):
@@ -192,10 +189,10 @@
                     for k in (down, up)
                 ]
                 k = colour * 6 + near * 3 + j
-                chip_ref[40 + k // 8, k % 8 : k % 8 + 1] = jnp.where(even_box, rows[1], rows[0])
-                far_ref[40 + k // 8, k % 8 : k % 8 + 1] = jnp.where(even_box, rows[0], rows[1])
-    chip_ref[41, 4:8] = jnp.zeros((4, LANES), F32)
-    far_ref[41, 4:8] = jnp.zeros((4, LANES), F32)
+                down_ref[40 + k // 8, k % 8 : k % 8 + 1] = rows[0]
+                up_ref[24 + k // 8, k % 8 : k % 8 + 1] = rows[1]
+    down_ref[41, 4:8] = jnp.zeros((4, LANES), F32)
+    up_ref[25, 4:8] = jnp.zeros((4, LANES), F32)
 
 
 EDGE = [(0, 1, 0), (0, 1, 1), (0, 0, 0), (0, 0, 1), (1, 1, 0), (1, 1, 1), (0, 1, 2), (1, 1, 2)]
@@ -410,14 +407,13 @@
 
 
 def smooth_outer(
-    lengths_ref, factor_ref, own_ref, plane_ref, rim_ref, rim_plane_ref, box_ref, far_ref, chip_ref,
+    lengths_ref, factor_ref, own_ref, plane_ref, rim_ref, rim_plane_ref, box_ref, down_ref, up_ref,
     inner_ref, shift_ref, given_ref,
     out_ref, placed_ref,
     face_ref, weight_ref, inverse_ref, value_ref, box_rim_ref, edge_ref, sems,
 ):
     channels = out_ref.shape[0]
     position = lax.axis_index("boxes")
-    even_box = position % 2 == 0
     last_box = position == lax.axis_size("boxes") - 1
     work = Smoother(factor_ref, face_ref, weight_ref, inverse_ref, shift_ref, channels, RING)
     lane = work.lane
@@ -441,15 +437,9 @@
             for copy in send(k):
                 copy.start()
 
-    def from_after(i):
-        return jnp.where(even_box, chip_ref[i], far_ref[i])
-
-    def from_before(i):
-        return jnp.where(even_box, far_ref[i], chip_ref[i])
-
     edges = [
-        jnp.where(missing, 0.0, jnp.concatenate([get(40), get(41)], 0))
-        for get, missing in ((from_after, last_box), (from_before, position == 0))
+        jnp.where(missing, 0.0, jnp.concatenate([ref[i], ref[i + 1]], 0))
+        for ref, i, missing in ((down_ref, 40, last_box), (up_ref, 24, position == 0))
     ]
     flat_box = box_ref.reshape(114 * SUBS, LANES)
     conduct = []
@@ -461,7 +451,7 @@
                 row = (((3 * colour + 2) * 8) * 2 + j) * SUBS + 7
                 box = flat_box[pl.ds(row, SUBS, stride=2 * SUBS)]
             else:
-                box = from_after(38 + colour)
+                box = down_ref[38 + colour]
             box = jnp.where(last_box, 0.0, box)
             edge = jnp.zeros((SUBS, LANES), F32)
             for place_at, side, near in ((0, 0, 1), (1, 0, 0), (6, 1, 0), (7, 1, 1)):
@@ -473,16 +463,16 @@
     work.find_faces(conduct)
 
     for p in range(8):
-        reds, blacks = unpack_halo([from_after(4 * p + i) for i in range(4)], lane)
+        reds, blacks = unpack_halo([down_ref[4 * p + i] for i in range(4)], lane)
         for ct in range(3):
             box_rim_ref[0, ct, p], box_rim_ref[1, ct, p] = reds[ct], blacks[ct]
     for ct in range(3):
         for i in range(6):
-            edge_ref[0, ct, i] = from_before(ct * 6 + i)
+            edge_ref[0, ct, i] = up_ref[ct * 6 + i]
             edge_ref[1, ct, i] = box_ref[96 + ct * 6 + i]
         for colour in range(2):
-            edge_ref[0, ct, 6 + colour] = from_before(32 + ct * 2 + colour)
-            edge_ref[1, ct, 6 + colour] = from_after(32 + ct * 2 + colour)
+            edge_ref[0, ct, 6 + colour] = up_ref[18 + ct * 2 + colour]
+            edge_ref[1, ct, 6 + colour] = down_ref[32 + ct * 2 + colour]
 
     def source_of(q):
         if 2 <= q < 18:
@@ -572,32 +562,42 @@
     real = lambda *shape: jax.ShapeDtypeStruct(shape + (SUBS, LANES), F32)
     vmem = lambda *shape: pltpu.VMEM(shape + (SUBS, LANES), F32)
     params = pltpu.CompilerParams(vmem_limit_bytes=VMEM_LIMIT)
-    own, plane, first, second, box = pl.pallas_call(
+    own, plane, first, second, third, box = pl.pallas_call(
         pack_rims,
         out_shape=(
             real(2, 3, pairs, 2),
             real(2, 2, 2),
             real(2 * pairs + 2),
             real(2 * pairs + 2),
+            real(2 * pairs + 2),
             real(114),
         ),
         in_specs=in_vmem(1),
-        out_specs=tuple(in_vmem(5)),
+        out_specs=tuple(in_vmem(6)),
         scratch_shapes=[pltpu.VMEM((2, channels + 2, planes, LANES), F32)],
         compiler_params=params,
     )(jnp.concatenate([sources, absorption[None], conductance[None]]))
+    near = swap_pairs(boxes, groups, False, 0)
+    beside = [(i, (i // groups ^ 1) * groups + i % groups) for i in range(boxes * groups)]
+
+    def turn(which):
+        return [
+            pair if pair[0] % groups // 2 % 2 == which else beside[pair[0]] for pair in near
+        ]
+
+    third = lax.ppermute(third, ("boxes", "grp"), turn(1))
     second = lax.ppermute(second, ("boxes", "grp"), swap_pairs(boxes, groups, False, 1))
-    first = lax.ppermute(first, ("boxes", "grp"), swap_pairs(boxes, groups, False, 0))
+    first = lax.ppermute(first, ("boxes", "grp"), turn(0))
     box = lax.ppermute(box, "boxes", [((i + 1) % boxes, i) for i in range(boxes)])
-    rim, rim_plane, chip, far = pl.pallas_call(
+    rim, rim_plane, down, up = pl.pallas_call(
         pack_faces,
-        out_shape=(real(2, 3, pairs), real(2, 2), real(42), real(42)),
-        in_specs=in_vmem(4),
+        out_shape=(real(2, 3, pairs), real(2, 2), real(42), real(26)),
+        in_specs=in_vmem(5),
         out_specs=tuple(in_vmem(4)),
         compiler_params=params,
-    )(own, plane, first, second)
-    chip = lax.ppermute(chip, ("boxes", "grp"), swap_pairs(boxes, groups, True, 0))
-    far = lax.ppermute(far, ("boxes", "grp"), swap_pairs(boxes, groups, True, 1))
+    )(own, plane, first, second, third)
+    down = lax.ppermute(down, "boxes", [((i + 1) % boxes, i) for i in range(boxes)])
+    up = lax.ppermute(up, "boxes", [(i, (i + 1) % boxes) for i in range(boxes)])
     smem = pl.BlockSpec(memory_space=pltpu.SMEM)
     placed_shape = (2, 3 * SUBS, MOST * BOX_X, LANES)
     inner, placed, shift = pl.pallas_call(
@@ -615,7 +615,7 @@
             vmem(2, 3, pairs + 2, 3),
         ],
         compiler_params=params,
-        cost_estimate=pl.CostEstimate(flops=2_000_000_000, bytes_accessed=0, transcendentals=0),
+        cost_estimate=pl.CostEstimate(flops=4_000_000_000, bytes_accessed=0, transcendentals=0),
     )(run_lengths, diffusivity, own, plane, rim, rim_plane)
     correction, _ = pl.pallas_call(
         smooth_outer,
@@ -636,7 +636,7 @@
             pltpu.SemaphoreType.DMA((MOST, 2)),
         ],
         compiler_params=params,
-    )(run_lengths, diffusivity, own, plane, rim, rim_plane, box, far, chip, inner, shift, placed)
+    )(run_lengths, diffusivity, own, plane, rim, rim_plane, box, down, up, inner, shift, placed)
     return correction
 
 

time: 20.4 us -> 20 us (0.980)
  waiting for transfers between devices: 4.55 us -> 3.57 us
  starting transfers between devices: 7.73 us -> 8.34 us
    ppermute x3 -> x4, starting transfers between devices: 4.34 us -> 6.29 us  [the longest x1 3.09 us: on_device(): first = lax.ppermute(first, ('boxes', 'grp'), turn(0))]
    ppermute x1, starting transfers between devices: 3.39 us -> 2.05 us  [on_device(): lax.ppermute(box, 'boxes', [((i + 1) % boxes, i) for i in range(boxes)])]
    ppermute x3 -> x4, waiting for transfers between devices: 4.55 us -> 3.57 us  [the longest x1 1.28 us: on_device(): up = lax.ppermute(up, 'boxes', [(i, (i + 1) % boxes) for i in range(boxes)])]
  transfers between devices with their start and end apart: 5 -> 6, of which waited for: 2 -> 3; matrix products, arithmetic and copies ran while one was open for 0% -> 0% of each run, Pallas kernels for 14% -> 14%
where the time goes in v8:
time: 20 us; the launch traced here: 19.9 us
  starting transfers between devices  8.34 us (42%)
  Pallas kernels  6.7 us (34%)
  waiting for transfers between devices  3.57 us (18%)
  other arithmetic  1.21 us (6%)
    pallas_call x1, Pallas kernels, on_device(): pl.pallas_call(smooth_outer, out_shape=(jax.ShapeDtypeStruct((channels, M...  3.32 us
    ppermute x1, starting transfers between devices, on_device(): first = lax.ppermute(first, ('boxes', 'grp'), turn(0))  3.09 us
    ppermute x1, starting transfers between devices, on_device(): lax.ppermute(down, 'boxes', [((i + 1) % boxes, i) for i in range(boxes)])  2.63 us
    pallas_call x1, Pallas kernels, on_device(): pl.pallas_call(smooth_inner, out_shape=(real(4, 3, pairs, 3), jax.ShapeDt...  2.29 us
    ppermute x1, starting transfers between devices, on_device(): lax.ppermute(box, 'boxes', [((i + 1) % boxes, i) for i in range(boxes)])  2.05 us
    ppermute x1, waiting for transfers between devices, on_device(): up = lax.ppermute(up, 'boxes', [(i, (i + 1) % boxes) for i in range(boxes)])  1.28 us
    concatenate x1, other arithmetic, on_device(): jnp.concatenate([sources, absorption[None], conductance[None]])  1.21 us
    ppermute x1, waiting for transfers between devices, on_device(): lax.ppermute(down, 'boxes', [((i + 1) % boxes, i) for i in range(boxes)])  1.18 us
  transfers between devices with their start and end apart: 6, of which 3 were waited for; matrix products, arithmetic and copies ran while one was open for 0% of the time, Pallas kernels for 14%

profile of v8, /device:TPU:0, one launch (start us, length us, event | category | flops | bytes accessed | tf_op | source)
XLA Modules:
  0.0 19.9 jit_solution(2205586554246193767)
XLA Ops:
  0.0 1.2 %pad_maximum_fusion.src_ref = f32[24,32,256]{2,1,0:T(8,128)S(1)} fusion(f32[1,32,256]{2,1,0:T(8,128)} %bitcast.2, f32[1,32,256]{2,1,0:T(8,128)} %bitcast.3, f32[22,32,256]{2,1,0:T(8,128)} %param.5), kind=kLoop, calls=%fused_computation | loop fusion | flops 393216 | bytes 1572864 | tf_op jit(solution)/shard_map/concatenate | solution.py:579
  1.2 0.0 copy-start
  1.2 0.0 copy-start.1
  1.2 0.6 %shard_map.55 = (f32[2,3,16,2,8,128]{5,4,3,2,1,0:T(8,128)S(1)}, f32[2,2,2,8,128]{4,3,2,1,0:T(8,128)S(1)}, f32[34,8,128]{2,1,0:T(8,128)S(1)}, f32[34,8,128]{2,1,0...) custom-call(f32[24,32,256]{2,1,0:T(8,128)S(1)} %pad_maximum_fusion.src_ref), custom_call_target="tpu_custom_call" | custom-call | tf_op jit(solution)/shard_map/pallas_call | solution.py:565
  1.9 3.1 %collective-permute-start = (f32[34,8,128]{2,1,0:T(8,128)S(1)}, f32[34,8,128]{2,1,0:T(8,128)S(1)}, u32[]{:S(2)}, u32[]{:S(2)}) collective-permute-start(f32[34,8,128]{2,1,0:T(8,128)S(1)} %get-tuple-element.21), channel_id=1, source_target_pairs={{0,1},{4,5},{8,9},{12,13},{16,17},{20,21},{24,25},{28,29},{1,0},{5... | collective-permute-start | bytes 417800 | tf_op jit(solution)/shard_map/ppermute | solution.py:590
  4.9 0.0 collective-permute-start.1
  4.9 0.5 %collective-permute-start.2 = (f32[34,8,128]{2,1,0:T(8,128)S(1)}, f32[34,8,128]{2,1,0:T(8,128)S(1)}, u32[]{:S(2)}, u32[]{:S(2)}) collective-permute-start(f32[34,8,128]{2,1,0:T(8,128)S(1)} %get-tuple-element.23), channel_id=1, source_target_pairs={{0,4},{4,0},{8,12},{12,8},{16,20},{20,16},{24,28},{28,24},{1,5},{5... | collective-permute-start | bytes 417800 | tf_op jit(solution)/shard_map/ppermute | solution.py:588
  5.5 2.1 %collective-permute-start.3 = (f32[114,8,128]{2,1,0:T(8,128)S(1)}, f32[114,8,128]{2,1,0:T(8,128)S(1)}, u32[]{:S(2)}, u32[]{:S(2)}) collective-permute-start(f32[114,8,128]{2,1,0:T(8,128)S(1)} %get-tuple-element.26), channel_id=1, source_target_pairs={{4,0},{8,4},{12,8},{16,12},{20,16},{24,20},{28,24},{0,28},{5,1},{9... | collective-permute-start | bytes 1400840 | tf_op jit(solution)/shard_map/ppermute | solution.py:591
  7.5 1.1 %collective-permute-done.first_ref = f32[34,8,128]{2,1,0:T(8,128)S(1)} collective-permute-done((f32[34,8,128]{2,1,0:T(8,128)S(1)}, f32[34,8,128]{2,1,0:T(8,128)S(1)}, u32[]{:S(2)}, u32[]{:S(2)}) %collective-permute-start) | collective-permute-done | bytes 139296 | tf_op jit(solution)/shard_map/ppermute | solution.py:590
  8.6 0.0 collective-permute-done.1.second_ref
  8.6 0.0 collective-permute-done.2.third_ref
  8.6 0.5 %shard_map.56 = (f32[2,3,16,8,128]{4,3,2,1,0:T(8,128)S(1)}, f32[2,2,8,128]{3,2,1,0:T(8,128)S(1)}, f32[42,8,128]{2,1,0:T(8,128)S(1)}, f32[26,8,128]{2,1,0:T(8,128)S(1)}) custom-call(f32[2,3,16,2,8,128]{5,4,3,2,1,0:T(8,128)S(1)} %get-tuple-element.19.own_ref, f32[2,2,2,8,128]{4,3,2,1,0:T(8,128)S(1)} %get-tuple-element.20.plane_ref, ...), custom_call_target="tpu_custom_call" | custom-call | tf_op jit(solution)/shard_map/pallas_call | solution.py:592
  9.1 0.1 collective-permute-start.5
  9.2 2.6 %collective-permute-start.4 = (f32[42,8,128]{2,1,0:T(8,128)S(1)}, f32[42,8,128]{2,1,0:T(8,128)S(1)}, u32[]{:S(2)}, u32[]{:S(2)}) collective-permute-start(f32[42,8,128]{2,1,0:T(8,128)S(1)} %get-tuple-element.27), channel_id=1, source_target_pairs={{4,0},{8,4},{12,8},{16,12},{20,16},{24,20},{28,24},{0,28},{5,1},{9... | collective-permute-start | bytes 516104 | tf_op jit(solution)/shard_map/ppermute | solution.py:599
  11.8 0.0 copy-done
  11.8 0.0 copy-done.1
  11.8 2.3 %shard_map.57 = (f32[4,3,16,3,8,128]{5,4,3,2,1,0:T(8,128)S(1)}, f32[2,24,48,128]{3,2,1,0:T(8,128)S(1)}, bf16[2,256,256]{2,1,0:T(8,128)(2,1)S(1)}) custom-call(s32[8]{0:T(128)S(1)} %copy-done, f32[22]{0:T(128)S(1)} %copy-done.1, f32[2,3,16,2,8,128]{5,4,3,2,1,0:T(8,128)S(1)} %get-tuple-element.19.own_ref, ...), custom_call_target="tpu_custom_call" | custom-call | flops 4000000000 | tf_op jit(solution)/shard_map/pallas_call | solution.py:603
  14.1 1.3 %collective-permute-done.5.up_ref = f32[26,8,128]{2,1,0:T(8,128)S(1)} collective-permute-done((f32[26,8,128]{2,1,0:T(8,128)S(1)}, f32[26,8,128]{2,1,0:T(8,128)S(1)}, u32[]{:S(2)}, u32[]{:S(2)}) %collective-permute-start.5) | collective-permute-done | bytes 106528 | tf_op jit(solution)/shard_map/ppermute | solution.py:600
  15.4 1.2 %collective-permute-done.4.down_ref = f32[42,8,128]{2,1,0:T(8,128)S(1)} collective-permute-done((f32[42,8,128]{2,1,0:T(8,128)S(1)}, f32[42,8,128]{2,1,0:T(8,128)S(1)}, u32[]{:S(2)}, u32[]{:S(2)}) %collective-permute-start.4) | collective-permute-done | bytes 172064 | tf_op jit(solution)/shard_map/ppermute | solution.py:599
  16.6 0.0 collective-permute-done.3.box_ref
  16.6 3.3 %shard_map.58 = (f32[22,48,256]{2,1,0:T(8,128)}, f32[2,24,48,128]{3,2,1,0:T(8,128)S(1)}) custom-call(s32[8]{0:T(128)S(1)} %copy-done, f32[22]{0:T(128)S(1)} %copy-done.1, f32[2,3,16,2,8,128]{5,4,3,2,1,0:T(8,128)S(1)} %get-tuple-element.19.own_ref, f32[2,2,2,8,128]{4,3,2,1,0:T(8,128)S(1)} %get-tuple-element.20.plane_ref, ...), custom_call_target="tpu_custom_call", output_to_operand_aliasing={{1}: (11, {})} | custom-call | tf_op jit(solution)/shard_map/pallas_call | solution.py:620
Async XLA Ops:
  1.2 10.6 %copy-start = (s32[8]{0:T(128)S(1)}, s32[8]{0:T(128)}, u32[]{:S(2)}) copy-start(s32[8]{0:T(128)} %lengths_ref.3) | copy-start | bytes 100
  1.2 10.6 %copy-start.1 = (f32[22]{0:T(128)S(1)}, f32[22]{0:T(128)}, u32[]{:S(2)}) copy-start(f32[22]{0:T(128)} %factor_ref.3) | copy-start | bytes 268
  1.9 6.8 %collective-permute-start = (f32[34,8,128]{2,1,0:T(8,128)S(1)}, f32[34,8,128]{2,1,0:T(8,128)S(1)}, u32[]{:S(2)}, u32[]{:S(2)}) collective-permute-start(f32[34,8,128]{2,1,0:T(8,128)S(1)} %get-tuple-element.21), channel_id=1, source_target_pairs={{0,1},{4,5},{8,9},{12,13},{16,17},{20,21},{24,25},{28,29},{1,0},{5... | collective-permute-start | bytes 417800 | tf_op jit(solution)/shard_map/ppermute | solution.py:590
  4.9 3.7 %collective-permute-start.1 = (f32[34,8,128]{2,1,0:T(8,128)S(1)}, f32[34,8,128]{2,1,0:T(8,128)S(1)}, u32[]{:S(2)}, u32[]{:S(2)}) collective-permute-start(f32[34,8,128]{2,1,0:T(8,128)S(1)} %get-tuple-element.22), channel_id=1, source_target_pairs={{0,4},{4,0},{8,12},{12,8},{16,20},{20,16},{24,28},{28,24},{1,2},{5... | collective-permute-start | bytes 417800 | tf_op jit(solution)/shard_map/ppermute | solution.py:589
  4.9 3.7 %collective-permute-start.2 = (f32[34,8,128]{2,1,0:T(8,128)S(1)}, f32[34,8,128]{2,1,0:T(8,128)S(1)}, u32[]{:S(2)}, u32[]{:S(2)}) collective-permute-start(f32[34,8,128]{2,1,0:T(8,128)S(1)} %get-tuple-element.23), channel_id=1, source_target_pairs={{0,4},{4,0},{8,12},{12,8},{16,20},{20,16},{24,28},{28,24},{1,5},{5... | collective-permute-start | bytes 417800 | tf_op jit(solution)/shard_map/ppermute | solution.py:588
  5.5 11.1 %collective-permute-start.3 = (f32[114,8,128]{2,1,0:T(8,128)S(1)}, f32[114,8,128]{2,1,0:T(8,128)S(1)}, u32[]{:S(2)}, u32[]{:S(2)}) collective-permute-start(f32[114,8,128]{2,1,0:T(8,128)S(1)} %get-tuple-element.26), channel_id=1, source_target_pairs={{4,0},{8,4},{12,8},{16,12},{20,16},{24,20},{28,24},{0,28},{5,1},{9... | collective-permute-start | bytes 1400840 | tf_op jit(solution)/shard_map/ppermute | solution.py:591
  9.1 6.3 %collective-permute-start.5 = (f32[26,8,128]{2,1,0:T(8,128)S(1)}, f32[26,8,128]{2,1,0:T(8,128)S(1)}, u32[]{:S(2)}, u32[]{:S(2)}) collective-permute-start(f32[26,8,128]{2,1,0:T(8,128)S(1)} %get-tuple-element.28), channel_id=1, source_target_pairs={{0,4},{4,8},{8,12},{12,16},{16,20},{20,24},{24,28},{28,0},{1,5},{5... | collective-permute-start | bytes 319496 | tf_op jit(solution)/shard_map/ppermute | solution.py:600
  9.2 7.4 %collective-permute-start.4 = (f32[42,8,128]{2,1,0:T(8,128)S(1)}, f32[42,8,128]{2,1,0:T(8,128)S(1)}, u32[]{:S(2)}, u32[]{:S(2)}) collective-permute-start(f32[42,8,128]{2,1,0:T(8,128)S(1)} %get-tuple-element.27), channel_id=1, source_target_pairs={{4,0},{8,4},{12,8},{16,12},{20,16},{24,20},{28,24},{0,28},{5,1},{9... | collective-permute-start | bytes 516104 | tf_op jit(solution)/shard_map/ppermute | solution.py:599
